TPU v7x, 32 devices: a whole 2x2x4 slice. The times are simulated.
32 devices in a mesh: exa: 4 (over z), exb: 8 (over y, x, core).
Axes of the slice: x: 2, y: 2, z: 4, core: 2. Of those that a mesh axis runs over, the one named last changes fastest.
Arguments:
- features: float32 [262144, 128], P(('exa', 'exb')), may hold values from -6 to 6
- sign_bits: int32 [262144], P(('exa', 'exb')), may hold values from 0 to 1
- sample_device: int32 [16384, 1], replicated, may hold values from 0 to 31; in each aligned block of 512 rows (0 to 511, 512 to 1023, ...) at most 32 rows name the same one
- sample_offset: int32 [16384], replicated, may hold values from 0 to 8191, as said below
Outputs:
- q_rows: float32 [16384, 128], P(('exa', 'exb'))
- upper_factor: float32 [128, 128], replicated
Inputs may be any that keep to these rules, and one draw needn't show every extreme that they name: `sample_device`: within each aligned block of 512 rows no value appears more than 32 times. `sample_offset`: within each aligned block of 512 rows, at most 32 values fall into any one range of 256 consecutive offsets that starts at a multiple of 256, and in every block some range holds exactly 32.
All inputs are finite; a program needn't handle non-finite values.
Results may differ from a plain program's by a relative error of at most 0.000071.
Values sent between devices are 32-bit elements; how exact they have to be, the bound alone decides.
No kernel may reach another device: no remote copies, remote signals or barrier semaphores. Data moves between devices by JAX's collectives and lax.ppermute only.
A program may use at most 64 MiB of HBM per device.

v0:
```python
import math

import jax
import jax.numpy as jnp
from jax import lax
from jax.sharding import PartitionSpec as P


def hadamard_table(order_size):
    index = jnp.arange(order_size, dtype=jnp.int32)
    common = index[:, None] & index[None, :]
    parity = jnp.zeros((order_size, order_size), jnp.int32)
    for bit_pos in range(max(order_size.bit_length(), 1)):
        parity = parity + (common >> bit_pos & 1)
    return (1 - 2 * (parity % 2)).astype(jnp.float32)


def cholesky_upper(gram):
    width = gram.shape[0]
    columns = jnp.arange(width, dtype=jnp.int32)

    def cholesky_one_row(step, upper):
        column = lax.dynamic_slice_in_dim(upper, step, 1, 1)[:, 0]
        target = lax.dynamic_slice_in_dim(gram, step, 1, 0)[0]
        remain = target - jnp.dot(column, upper, precision=lax.Precision.HIGHEST)
        pivot = jnp.sqrt(lax.dynamic_slice_in_dim(remain, step, 1, 0)[0])
        new_row = jnp.where(columns >= step, remain / pivot, 0.0)
        return lax.dynamic_update_slice_in_dim(upper, new_row[None, :], step, 0)

    return lax.fori_loop(0, width, cholesky_one_row, jnp.zeros((width, width), jnp.float32))


def upper_inverse(upper):
    width = upper.shape[0]
    columns = jnp.arange(width, dtype=jnp.int32)

    def upper_one_row(count, inverse):
        step = width - 1 - count
        row_u = lax.dynamic_slice_in_dim(upper, step, 1, 0)[0]
        pivot = lax.dynamic_slice_in_dim(row_u, step, 1, 0)[0]
        unit_row = (columns == step).astype(jnp.float32)
        new_row = (unit_row - jnp.dot(row_u, inverse, precision=lax.Precision.HIGHEST)) / pivot
        return lax.dynamic_update_slice_in_dim(inverse, new_row[None, :], step, 0)

    return lax.fori_loop(0, width, upper_one_row, jnp.zeros((width, width), jnp.float32))


def slot_select(from_here, values, slot_count):
    own_count = from_here.shape[1]
    positions = jnp.arange(own_count, dtype=jnp.int32)
    before_mask = (positions[:, None] < positions[None, :]).astype(jnp.float32)
    slot_rank = jnp.dot(
        from_here.astype(jnp.float32), before_mask, precision=lax.Precision.HIGHEST
    ).astype(jnp.int32)
    slot_ids = jnp.arange(slot_count, dtype=jnp.int32)
    slot_hit = from_here[:, :, None] & (slot_rank[:, :, None] == slot_ids[None, None, :])
    picked = jnp.sum(jnp.where(slot_hit, values[:, :, None], 0), axis=1)
    slot_valid = jnp.any(slot_hit, axis=1).astype(jnp.float32)
    return (picked, slot_valid)


def rank_within(keys_mine):
    own_count = keys_mine.shape[0]
    positions = jnp.arange(own_count, dtype=jnp.int32)
    same_key = keys_mine[:, None] == keys_mine[None, :]
    earlier_rows = positions[None, :] < positions[:, None]
    return jnp.sum((same_key & earlier_rows).astype(jnp.int32), axis=1)


def per_device(features, sign_bits, sample_device, sample_offset):
    highest = lax.Precision.HIGHEST
    rows_dev, feat_width = features.shape
    n_outer = lax.axis_size("exa")
    n_inner = lax.axis_size("exb")
    n_all = n_outer * n_inner
    myself = lax.axis_index("exa") * n_inner + lax.axis_index("exb")
    sign_values = (2 * sign_bits - 1).astype(jnp.float32)
    signed = features * sign_values[:, None]
    blocks = rows_dev // 128
    local_grid = signed.reshape(blocks, 128, feat_width)
    local_grid = jnp.einsum("kj,bjf->bkf", hadamard_table(128), local_grid, precision=highest)
    local_grid = jnp.einsum("kb,bjf->kjf", hadamard_table(blocks), local_grid, precision=highest)
    signed_local = local_grid.reshape(rows_dev, feat_width)
    piece_rows = rows_dev // n_inner
    sub_rows = piece_rows // n_outer
    inner_table = hadamard_table(n_inner)
    outer_table = hadamard_table(n_outer)
    inner_mixed = jnp.einsum(
        "ks,spf->kpf",
        inner_table,
        lax.all_to_all(
            signed_local.reshape(n_inner, piece_rows, feat_width),
            "exb",
            split_axis=0,
            concat_axis=0,
            tiled=True,
        ),
        precision=highest,
    )
    inner_mixed = inner_mixed.reshape(n_inner, n_outer, sub_rows, feat_width)
    mixed = jnp.einsum(
        "ks,bsqf->bkqf",
        outer_table,
        lax.all_to_all(inner_mixed, "exa", split_axis=1, concat_axis=1, tiled=True),
        precision=highest,
    )
    scale = 1.0 / math.sqrt(rows_dev * n_all)
    total_samples = sample_device.shape[0]
    own_count = total_samples // n_all
    source_all = sample_device[:, 0].reshape(n_all, own_count)
    offset_all = sample_offset.reshape(n_all, own_count)
    offset_mine = lax.dynamic_slice_in_dim(sample_offset, myself * own_count, own_count)
    group_rows = rows_dev // n_all
    group_slots = max(4, 2 * own_count // n_all)
    group_all = offset_all // group_rows
    within_all = offset_all % group_rows
    group_mine = offset_mine // group_rows
    my_group = lax.axis_index("exb") * n_outer + lax.axis_index("exa")
    flat_all = (
        source_all % n_inner * (n_outer * group_rows)
        + source_all // n_inner * group_rows
        + within_all
    )
    holder_mine = group_mine % n_outer * n_inner + group_mine // n_outer
    held_flat = mixed.reshape(n_all * group_rows, feat_width)
    from_here = group_all == my_group
    picked_rows, slot_valid = slot_select(from_here, flat_all, group_slots)
    outgoing = jnp.take(held_flat, picked_rows.reshape(-1), axis=0) * (
        slot_valid.reshape(-1)[:, None] * scale
    )
    outgoing = outgoing.reshape(n_all, group_slots, feat_width)
    received = lax.all_to_all(outgoing, ("exa", "exb"), split_axis=0, concat_axis=0, tiled=True)
    rank_mine = rank_within(group_mine)
    sketch = jnp.take(
        received.reshape(n_all * group_slots, feat_width),
        holder_mine * group_slots + rank_mine,
        axis=0,
    )
    gram_local = jnp.dot(sketch.T, sketch, precision=highest) / total_samples
    gram = lax.psum(gram_local, ("exa", "exb"))
    upper_factor = cholesky_upper(gram)
    inverse = upper_inverse(upper_factor)
    q_rows = jnp.dot(sketch, inverse, precision=highest)
    return (q_rows, upper_factor)


def solution(mesh):
    placed = (P(("exa", "exb"), None), P(("exa", "exb")), P(), P())
    return jax.shard_map(
        per_device,
        mesh=mesh,
        in_specs=placed,
        out_specs=(P(("exa", "exb"), None), P()),
        check_vma=False,
    )
```

profile of v0, /device:TPU:0, one launch (start us, length us, event | category | flops | bytes accessed | tf_op | source)
XLA Modules:
  0.0 890.2 jit_solution(15307705369202869935)
XLA Ops:
  7.9 5.0 broadcast_multiply_fusion
  12.9 8.3 convolution_bitcast_fusion.2
  21.2 5.4 copy.32
  26.6 5.5 fusion.56
  32.1 2.4 copy.33
  34.6 54.0 %all_to_all.15 = f32[8,1024,128]{2,1,0:T(8,128)S(1)} all-to-all(f32[8,1024,128]{2,1,0:T(8,128)S(1)} %bitcast.79), channel_id=1, replica_groups=mesh['exa'=4,'exb'=8] {'exb'}, dimensions={0} | all-to-all | bytes 8388608 | tf_op jit(solution)/shard_map/all_to_all | solution.py:91
  88.6 5.8 fusion.16
  94.4 2.7 copy.35
  97.1 5.2 all-to-all-start.1
  105.5 89.6 %all-to-all-done.1 = f32[8,4,256,128]{3,2,0,1:T(8,128)} async-done(((f32[8,4,256,128]{3,2,0,1:T(8,128)}), f32[8,4,256,128]{3,2,0,1:T(8,128)}, u32[]{:S(2)}, u32[]{:S(2)}) %all-to-all-start.1) | async-done | bytes 4194336 | tf_op jit(solution)/shard_map/all_to_all | solution.py:104
  195.1 12.1 %fusion.18 = f32[8,4,256,128]{3,1,2,0:T(4,128)S(1)} fusion(f32[8,4,256,128]{3,2,0,1:T(8,128)} %all-to-all-done.1), kind=kOutput, calls=%fused_computation.22 | convolution fusion | flops 50332016 | bytes 8388608 | tf_op jit(solution)/shard_map/ks,bsqf->bkqf/dot_general | solution.py:101
  207.2 2.5 copy.37
  209.7 5.0 gather_fusion
  214.7 1.1 select_multiply_fusion
  215.8 2.6 all-to-all-start.2
  218.9 15.0 %all-to-all-done.2 = f32[32,32,128]{2,1,0:T(8,128)S(1)} async-done(((f32[32,32,128]{2,1,0:T(8,128)}), f32[32,32,128]{2,1,0:T(8,128)S(1)}, u32[]{:S(2)}, u32[]{:S(2)}) %all-to-all-start.2) | async-done | bytes 524320 | tf_op jit(solution)/shard_map/all_to_all | solution.py:132
  234.0 1.0 gather_fusion.1
  235.0 1.4 convolution_multiply_fusion
  236.4 116.0 %all-reduce.2.cloned.1.call-done = f32[128,128]{1,0:T(8,128)} async-done(((f32[128,128]{1,0:T(8,128)}), f32[128,128]{1,0:T(8,128)}) %all-reduce.2.cloned.1.call-update) | async-done | bytes 65552 | tf_op jit(solution)/shard_map/psum | solution.py:140
  352.5 344.3 %while.31 = (s32[]{:T(128)}, f32[128,128]{0,1:T(8,128)S(1)}, f32[128,128]{1,0:T(8,128)}, s32[]{:T(128)}, s32[]{:T(128)}) while((s32[]{:T(128)}, f32[128,128]{0,1:T(8,128)S(1)}, f32[128,128]{1,0:T(8,128)}, s32[]{:T(128)}, s32[]{:T(128)}) %tuple.85), condition=%wide.region_5.6_spmd.clone, body=%wide.region_4.5_spmd.clone.sunk | while | flops 197122 | bytes 71261 | solution.py:30
  486.9 0.9 fusion.148
  489.6 0.9 fusion.148
  696.9 185.3 %while.32 = (s32[]{:T(128)}, f32[128,128]{1,0:T(8,128)S(1)}, f32[128,128]{1,0:T(8,128)S(1)}, s32[]{:T(128)}, s32[]{:T(128)}, /*index=5*/s32[]{:T(128)}, s32[]{:T(128)}) while((s32[]{:T(128)}, f32[128,128]{1,0:T(8,128)S(1)}, f32[128,128]{1,0:T(8,128)S(1)}, s32[]{:T(128)}, s32[]{:T(128)}, /*index=5*/s32[]{:T(128)}, s32[]{:T(128)}) %tuple.88), condition=%wide.region_7.8_spmd.clone, body=%wide.region_6.7_spmd.clone.sunk | while | flops 197127 | bytes 67751 | solution.py:45
  882.2 1.1 fusion.24
  (1052 shorter events, 435.7 us)
Async XLA Ops:
  97.1 5.2 copy-start.1
  97.1 5.8 copy-start.2
  97.1 98.0 %all-to-all-start.1 = ((f32[8,4,256,128]{3,2,0,1:T(8,128)}), f32[8,4,256,128]{3,2,0,1:T(8,128)}, u32[]{:S(2)}, u32[]{:S(2)}) async-start(f32[8,4,256,128]{3,2,0,1:T(8,128)} %copy.35), calls=%async_computation.1 | async-start | bytes 8388608 | tf_op jit(solution)/shard_map/all_to_all | solution.py:104
  215.8 18.2 %all-to-all-start.2 = ((f32[32,32,128]{2,1,0:T(8,128)}), f32[32,32,128]{2,1,0:T(8,128)S(1)}, u32[]{:S(2)}, u32[]{:S(2)}) async-start(f32[32,32,128]{2,1,0:T(8,128)} %select_multiply_fusion), calls=%async_computation.2 | async-start | bytes 1048576 | tf_op jit(solution)/shard_map/all_to_all | solution.py:132
  218.4 134.1 %all-reduce.2.cloned.1.call-start = ((), (), s32[]{:S(2)}) async-start(), calls=%async_computation.3 | async-start | bytes 131072 | tf_op jit(solution)/shard_map/psum | solution.py:140
  882.2 1.1 copy-start
Sparse Core Ops, SparseCore 0:
  236.6 115.8 all-reduce.1
where the time goes:
time: 899 us; the launch traced here: 890 us
  matrix products  245 us (27%)
  local copies, waits for them, and re-layouts  241 us (27%)
  waiting for transfers between devices  221 us (25%)
  loops' own time  96.7 us (11%)
  blocking collectives  54 us (6%)
  between operations  14.3 us (2%)
  other arithmetic  10.3 us (1%)
    psum x1, waiting for transfers between devices, per_device(): gram = lax.psum(gram_local, ('exa', 'exb'))  116 us
    dot_general x128, matrix products, cholesky_one_row(): remain = target - jnp.dot(column, upper, precision=lax.Precision.HIGHEST)  109 us
    dot_general x128, matrix products, upper_one_row(): jnp.dot(row_u, inverse, precision=lax.Precision.HIGHEST)  102 us
    another operation x1, loops' own time, cholesky_upper(): lax.fori_loop(0, width, cholesky_one_row, jnp.zeros((width, width), jnp.f...  92.7 us
    all_to_all x1, waiting for transfers between devices, per_device(): lax.all_to_all(inner_mixed, 'exa', split_axis=1, concat_axis=1, tiled=True)  89.6 us
    dynamic_slice x128, local copies, waits for them, and re-layouts, cholesky_one_row(): pivot = jnp.sqrt(lax.dynamic_slice_in_dim(remain, step, 1, 0)[0])  81.4 us
    dynamic_slice x128, local copies, waits for them, and re-layouts, upper_one_row(): pivot = lax.dynamic_slice_in_dim(row_u, step, 1, 0)[0]  75.3 us
    all_to_all x1, blocking collectives, per_device(): lax.all_to_all(signed_local.reshape(n_inner, piece_rows, feat_width), 'ex...  54 us
  transfers between devices with their start and end apart: 3, of which 3 were waited for; matrix products, arithmetic and copies ran while one was open for 0% of the time, Pallas kernels for 0%

commit v1 on v0

v1 whole, which is shorter than its diff:
```python
import functools
import math

import jax
import jax.numpy as jnp
from jax import lax
from jax.experimental import pallas as pl
from jax.experimental.pallas import tpu as pltpu
from jax.sharding import PartitionSpec as P

F32 = jnp.float32
BF16 = jnp.bfloat16
I32 = jnp.int32
SUB = 8
MIB = 1 << 20


def parity(bits, width):
    total = jnp.zeros_like(bits)
    for place in range(width):
        total = total ^ (bits >> place)
    return total & 1


def split3(x):
    high = x.astype(BF16).astype(F32)
    rest = x - high
    mid = rest.astype(BF16).astype(F32)
    return high, mid, rest - mid


def bit_perm(size, bit):
    return [(i, i ^ bit) for i in range(size)]


def mix_low(x_ref, sign_ref, mid_ref, table):
    low = table.shape[0]
    blocks = x_ref.shape[0] // low

    def one(b, carry):
        rows = pl.ds(pl.multiple_of(b * low, low), low)
        sign = (2 * sign_ref[pl.ds(b, 1), :] - 1).astype(F32)
        left = (table * sign).astype(BF16)
        x = x_ref[rows, :]
        high = x.astype(BF16)
        rest = x - high.astype(F32)
        mid = rest.astype(BF16)
        last = (rest - mid.astype(F32)).astype(BF16)
        wide = jnp.dot(left, jnp.concatenate([high, mid], 1), preferred_element_type=F32)
        width = x.shape[1]
        tail = jnp.dot(left, last, preferred_element_type=F32)
        mid_ref[rows, :] = wide[:, :width] + (wide[:, width:] + tail)
        return carry

    lax.fori_loop(0, blocks, one, 0)


def low_table(low):
    width = max(low.bit_length() - 1, 1)
    r = lax.broadcasted_iota(I32, (low, low), 0)
    c = lax.broadcasted_iota(I32, (low, low), 1)
    return (1 - 2 * parity(r & c, width)).astype(F32)


def mix_high(mid_ref, low, emit):
    blocks = mid_ref.shape[0] // low

    def one(g, carry):
        start = pl.multiple_of(g * SUB, SUB)
        parts = [mid_ref[pl.ds(b * low + start, SUB), :] for b in range(blocks)]
        step = 1
        while step < blocks:
            mixed = list(parts)
            for b in range(blocks):
                if not b & step:
                    mixed[b] = parts[b] + parts[b | step]
                    mixed[b | step] = parts[b] - parts[b | step]
            parts = mixed
            step *= 2
        for b in range(blocks):
            emit(b * low + start, parts[b])
        return carry

    lax.fori_loop(0, low // SUB, one, 0)


def own_kernel(low, x_ref, sign_ref, out_ref, mid_ref):
    mix_low(x_ref, sign_ref, mid_ref, low_table(low))

    def emit(row, value):
        out_ref[pl.ds(row, SUB), :] = value

    mix_high(mid_ref, low, emit)


def pair_kernel(low, x_ref, sign_ref, own_ref, out_ref, mid_ref):
    mix_low(x_ref, sign_ref, mid_ref, low_table(low))
    count = x_ref.shape[0]

    def emit(row, value):
        own = own_ref[pl.ds(row, SUB), :]
        out_ref[pl.ds(row, SUB), :] = own + value
        out_ref[pl.ds(count + row, SUB), :] = own - value

    mix_high(mid_ref, low, emit)


def pick_kernel(unroll, row_ref, sign_ref, table_ref, out_ref):
    def some(i, carry):
        for u in range(unroll):
            r = i * unroll + u
            out_ref[pl.ds(r, 1), :] = table_ref[pl.ds(row_ref[r], 1), :] * sign_ref[r]
        return carry

    lax.fori_loop(0, out_ref.shape[0] // unroll, some, 0)


def pick(rows, signs, table):
    count = rows.shape[0]
    vmem = pl.BlockSpec(memory_space=pltpu.VMEM)
    smem = pl.BlockSpec(memory_space=pltpu.SMEM)
    return pl.pallas_call(
        functools.partial(pick_kernel, math.gcd(count, 32)),
        out_shape=jax.ShapeDtypeStruct((count, table.shape[1]), F32),
        in_specs=[smem, smem, vmem],
        out_specs=vmem,
        compiler_params=pltpu.CompilerParams(vmem_limit_bytes=24 * MIB),
        cost_estimate=pl.CostEstimate(
            flops=count * 128, bytes_accessed=4 * 4 * MIB, transcendentals=0
        ),
        name="pick",
    )(rows, signs, table)


def factor_panel(left, right, at):
    shape = left.shape
    rows = lax.broadcasted_iota(I32, shape, 0)
    column = [jnp.broadcast_to(left[:, at + i : at + i + 1], shape) for i in range(SUB)]
    pivots = jnp.ones_like(left)
    for i in range(SUB):
        pivot = jnp.broadcast_to(column[i][i : i + 1, :], shape)
        pivots = jnp.where(rows == i, pivot, pivots)
        if i < SUB - 1:
            ratio = jnp.where(rows > i, column[i] * (1.0 / pivot), 0.0)
            for j in range(i + 1, SUB):
                column[j] = column[j] - ratio * jnp.broadcast_to(column[j][i : i + 1, :], shape)
            left = left - ratio * jnp.broadcast_to(left[i : i + 1, :], shape)
            right = right - ratio * jnp.broadcast_to(right[i : i + 1, :], shape)
    scale = lax.rsqrt(pivots)
    return left * scale, right * scale


def factor(gram):
    n = gram.shape[0]
    rest = gram
    unit = (
        lax.broadcasted_iota(I32, (n, n), 0) == lax.broadcasted_iota(I32, (n, n), 1)
    ).astype(F32)
    lanes = lax.broadcasted_iota(I32, (SUB, n), 1)
    panel_rows = lax.broadcasted_iota(I32, (SUB, n), 0)
    uppers, inverses = [], []
    for at in range(0, n, SUB):
        left, right = factor_panel(rest[:SUB], unit[:SUB], at)
        left = jnp.where(lanes >= panel_rows + at, left, 0.0)
        uppers.append(left)
        inverses.append(right)
        if at + SUB < n:
            h, m, l = split3(left)
            uh, um, ul = split3(right)
            terms = jnp.concatenate([h, h, m, h, l, m], 0)
            others = jnp.concatenate(
                [
                    jnp.concatenate([h, m, h, l, h, m], 0),
                    jnp.concatenate([uh, um, uh, ul, uh, um], 0),
                ],
                1,
            )
            change = jnp.dot(terms.T[at + SUB :], others, preferred_element_type=F32)
            rest = rest[SUB:] - change[:, :n]
            unit = unit[SUB:] - change[:, n:]
    return jnp.concatenate(uppers, 0), jnp.concatenate(inverses, 0)


def finish_kernel(gram_ref, sketch_ref, q_ref, upper_ref):
    upper, inverse = factor(gram_ref[...])
    upper_ref[...] = upper
    q_ref[...] = lax.dot_general(
        sketch_ref[...],
        inverse,
        (((1,), (1,)), ((), ())),
        precision=lax.Precision.HIGHEST,
        preferred_element_type=F32,
    )


def per_device(features, sign_bits, sample_device, sample_offset):
    rows_dev, width = features.shape
    n_outer = lax.axis_size("exa")
    n_inner = lax.axis_size("exb")
    n_all = n_outer * n_inner
    bits = n_all.bit_length() - 1
    inner_bits = n_inner.bit_length() - 1
    myself = lax.axis_index("exa") * n_inner + lax.axis_index("exb")
    total = sample_offset.shape[0]
    own_count = total // n_all
    low = min(256, rows_dev)
    vmem = pl.BlockSpec(memory_space=pltpu.VMEM)

    def swap(value, bit):
        if bit < inner_bits:
            return lax.ppermute(value, "exb", bit_perm(n_inner, 1 << bit))
        return lax.ppermute(value, "exa", bit_perm(n_outer, 1 << (bit - inner_bits)))

    source = sample_device[:, 0]
    scale = 1.0 / math.sqrt(rows_dev * n_all)
    row_all = sample_offset + (source & 1) * rows_dev
    sign_all = (1 - 2 * parity(source & myself, bits)).astype(F32) * scale
    row_blocks = row_all.reshape(n_all, own_count)
    sign_blocks = sign_all.reshape(n_all, own_count)

    far_features = swap(features, 0)
    far_signs = swap(sign_bits, 0)
    table_shape = (rows_dev // low, low)
    half = jax.ShapeDtypeStruct((rows_dev, width), F32)
    params = pltpu.CompilerParams(vmem_limit_bytes=32 * MIB)
    scratch = [pltpu.VMEM((rows_dev, width), F32)]
    own = pl.pallas_call(
        functools.partial(own_kernel, low),
        out_shape=half,
        in_specs=[vmem, vmem],
        out_specs=vmem,
        scratch_shapes=scratch,
        compiler_params=params,
        cost_estimate=pl.CostEstimate(flops=4 * 10**9, bytes_accessed=8 * MIB, transcendentals=0),
        name="own",
    )(features, sign_bits.reshape(table_shape))
    table = pl.pallas_call(
        functools.partial(pair_kernel, low),
        out_shape=jax.ShapeDtypeStruct((2 * rows_dev, width), F32),
        in_specs=[vmem, vmem, vmem],
        out_specs=vmem,
        scratch_shapes=scratch,
        compiler_params=params,
        cost_estimate=pl.CostEstimate(flops=4 * 10**9, bytes_accessed=16 * MIB, transcendentals=0),
        name="pair",
    )(far_features, far_signs.reshape(table_shape), own)

    outer_order = list(range(inner_bits, bits))
    inner_order = list(range(1, inner_bits))
    chunk_rows = own_count // 2
    chunks = [
        (0, chunk_rows, inner_order + outer_order),
        (chunk_rows, chunk_rows, inner_order[::-1] + outer_order),
    ]

    def targets(order):
        listed = [0]
        for bit in order[::-1]:
            listed = [e | 1 << bit for e in listed] + listed
        return listed

    def take(start, count, which):
        blocks = myself ^ jnp.array(which, I32)
        rows = jnp.take(row_blocks[:, start : start + count], blocks, axis=0).reshape(-1)
        signs = jnp.take(sign_blocks[:, start : start + count], blocks, axis=0).reshape(-1)
        return pick(rows, signs, table)

    lists = [targets(order) for _, _, order in chunks]
    sent = []
    for (start, count, order), listed in zip(chunks, lists):
        send = take(start, count, listed[: len(listed) // 2])
        sent.append(swap(send, order[0]))
    kept = [take(s, c, listed[len(listed) // 2 :]) for (s, c, _), listed in zip(chunks, lists)]
    for stage in range(1, len(chunks[0][2]) + 1):
        for n, (_, _, order) in enumerate(chunks):
            sums = kept[n] + sent[n]
            if stage < len(order):
                halfway = sums.shape[0] // 2
                sent[n] = swap(sums[:halfway], order[stage])
                kept[n] = sums[halfway:]
            else:
                kept[n] = sums
    sketch = jnp.concatenate(kept, 0)

    gram = lax.dot_general(
        sketch,
        sketch,
        (((0,), (0,)), ((), ())),
        precision=lax.Precision.HIGHEST,
        preferred_element_type=F32,
    ) / total
    for bit in range(bits):
        gram = gram + swap(gram, bit)

    return pl.pallas_call(
        finish_kernel,
        out_shape=(
            jax.ShapeDtypeStruct((own_count, width), F32),
            jax.ShapeDtypeStruct((width, width), F32),
        ),
        in_specs=[vmem, vmem],
        out_specs=(vmem, vmem),
        name="finish",
    )(gram, sketch)


def solution(mesh):
    placed = (P(("exa", "exb"), None), P(("exa", "exb")), P(), P())
    return jax.shard_map(
        per_device,
        mesh=mesh,
        in_specs=placed,
        out_specs=(P(("exa", "exb"), None), P()),
        check_vma=False,
    )
```

time: 899 us -> 141 us (0.16)
  matrix products: 245 us -> 0.6 us
  local copies, waits for them, and re-layouts: 241 us -> 22.9 us
  waiting for transfers between devices: 221 us -> 44.9 us
  loops' own time: 96.7 us -> 0 us
  blocking collectives: 54 us -> 0 us
  Pallas kernels: 0 us -> 42.4 us
  between operations: 14.3 us -> 0.96 us
  starting transfers between devices: 7.85 us -> 19.1 us
    dot_general x263 -> x1, matrix products: 245 us -> 0.6 us  [per_device(): lax.dot_general(sketch, sketch, (((0,), (0,)), ((), ())), precision=lax.P...]
    dynamic_slice x256 -> x0, local copies, waits for them, and re-layouts: 157 us -> none  [the longest x128 81.4 us: cholesky_one_row(): pivot = jnp.sqrt(lax.dynamic_slice_in_dim(remain, step, 1, 0)[0])]
    psum x1 -> x0, waiting for transfers between devices: 116 us -> none  [per_device(): gram = lax.psum(gram_local, ('exa', 'exb'))]
    all_to_all x2 -> x0, waiting for transfers between devices: 105 us -> none  [the longest x1 89.6 us: per_device(): lax.all_to_all(inner_mixed, 'exa', split_axis=1, concat_axis=1, tiled=True)]
    another operation x2 -> x0, loops' own time: 96.7 us -> none  [the longest x1 92.7 us: cholesky_upper(): lax.fori_loop(0, width, cholesky_one_row, jnp.zeros((width, width), jnp.f...]
    all_to_all x1 -> x0, blocking collectives: 54 us -> none  [per_device(): lax.all_to_all(signed_local.reshape(n_inner, piece_rows, feat_width), 'ex...]
    dynamic_update_slice x256 -> x0, local copies, waits for them, and re-layouts: 49.9 us -> none  [the longest x128 45.9 us: cholesky_one_row(): return lax.dynamic_update_slice_in_dim(upper, new_row[None, :], step, 0)]
    ppermute x0 -> x15, waiting for transfers between devices: none -> 44.9 us  [the longest x9 22.7 us: swap(): return lax.ppermute(value, 'exb', bit_perm(n_inner, 1 << bit))]
  transfers between devices with their start and end apart: 3 -> 15, of which waited for: 3 -> 12; matrix products, arithmetic and copies ran while one was open for 0% -> 11% of each run, Pallas kernels for 0% -> 14%
where the time goes in v1:
time: 141 us; the launch traced here: 140 us
  waiting for transfers between devices  44.9 us (32%)
  Pallas kernels  42.4 us (30%)
  local copies, waits for them, and re-layouts  22.9 us (16%)
  starting transfers between devices  19.1 us (14%)
  other arithmetic  9.06 us (6%)
    ppermute x9, waiting for transfers between devices, swap(): return lax.ppermute(value, 'exb', bit_perm(n_inner, 1 << bit))  22.7 us
    ppermute x6, waiting for transfers between devices, swap(): return lax.ppermute(value, 'exa', bit_perm(n_outer, 1 << bit - inner_bits))  22.2 us
    unnamed x22, local copies, waits for them, and re-layouts  16.6 us
    pallas_call x4, Pallas kernels, pick(): pl.pallas_call(functools.partial(pick_kernel, math.gcd(count, 32)), out_s...  13.2 us
    pallas_call x1, Pallas kernels, per_device(): pl.pallas_call(functools.partial(pair_kernel, low), out_shape=jax.ShapeDt...  12.1 us
    ppermute x9, starting transfers between devices, swap(): return lax.ppermute(value, 'exb', bit_perm(n_inner, 1 << bit))  10.2 us
    pallas_call x1, Pallas kernels, per_device(): pl.pallas_call(functools.partial(own_kernel, low), out_shape=half, in_spe...  9.12 us
    ppermute x6, starting transfers between devices, swap(): return lax.ppermute(value, 'exa', bit_perm(n_outer, 1 << bit - inner_bits))  8.9 us
  transfers between devices with their start and end apart: 15, of which 12 were waited for; matrix products, arithmetic and copies ran while one was open for 11% of the time, Pallas kernels for 14%

profile of v1, /device:TPU:0, one launch (start us, length us, event | category | flops | bytes accessed | tf_op | source)
XLA Modules:
  0.0 139.9 jit_solution(14371241369907875936)
XLA Ops:
  7.7 2.2 %copy-done.6 = f32[8192,128]{1,0:T(8,128)S(1)} copy-done((f32[8192,128]{1,0:T(8,128)S(1)}, f32[8192,128]{1,0:T(8,128)}, u32[]{:S(2)}) %copy-start.6) | copy-done | bytes 4194328
  9.9 9.1 %own.1.own_ref = f32[8192,128]{1,0:T(8,128)S(1)} custom-call(f32[8192,128]{1,0:T(8,128)S(1)} %copy-done.6, s32[32,256]{1,0:T(8,128)S(1)} %reshape.71.sign_ref), custom_call_target="tpu_custom_call" | custom-call | flops 4000000000 | bytes 8388608 | tf_op jit(solution)/shard_map/own/pallas_call | solution.py:227
  19.0 2.0 %copy-done.4 = f32[8192,128]{1,0:T(8,128)} copy-done((f32[8192,128]{1,0:T(8,128)}, f32[8192,128]{1,0:T(8,128)S(1)}, u32[]{:S(2)}) %copy-start.4) | copy-done | bytes 4194328
  21.7 2.2 %copy-done.5 = f32[8192,128]{1,0:T(8,128)S(1)} copy-done((f32[8192,128]{1,0:T(8,128)S(1)}, f32[8192,128]{1,0:T(8,128)}, u32[]{:S(2)}) %copy-start.5) | copy-done | bytes 4194328
  23.9 12.1 %pair.1.table_ref = f32[16384,128]{1,0:T(8,128)S(1)} custom-call(f32[8192,128]{1,0:T(8,128)} %collective-permute-done.x_ref, s32[32,256]{1,0:T(8,128)S(1)} %reshape.70.sign_ref, f32[8192,128]{1,0:T(8,128)S(1)} %copy-done.5), custom_call_target="tpu_custom_call" | custom-call | flops 4000000000 | bytes 16777216 | tf_op jit(solution)/shard_map/pair/pallas_call | solution.py:237
  36.0 3.3 %pick.5 = f32[2048,128]{1,0:T(8,128)S(1)} custom-call(s32[2048]{0:T(1024)S(1)} %bitcast.26, f32[2048]{0:T(1024)S(1)} %bitcast.25, f32[16384,128]{1,0:T(8,128)S(1)} %pair.1.table_ref), custom_call_target="tpu_custom_call" | custom-call | flops 262144 | bytes 16777216 | tf_op jit(solution)/shard_map/pick/pallas_call | solution.py:122
  39.3 3.0 %collective-permute-start.2 = (f32[2048,128]{1,0:T(8,128)S(1)}, f32[2048,128]{1,0:T(8,128)}, u32[]{:S(2)}, u32[]{:S(2)}) collective-permute-start(f32[2048,128]{1,0:T(8,128)S(1)} %pick.5), channel_id=1, source_target_pairs={{0,2},{1,3},{2,0},{3,1},{4,6},{5,7},{6,4},{7,5},{8,10},{9,11},{10,... | collective-permute-start | bytes 3145736 | tf_op jit(solution)/shard_map/ppermute | solution.py:211
  43.0 3.4 %copy-done.1 = f32[16384,128]{1,0:T(8,128)S(1)} copy-done((f32[16384,128]{1,0:T(8,128)S(1)}, f32[16384,128]{1,0:T(8,128)}, u32[]{:S(2)}) %copy-start.1) | copy-done | bytes 8388632
  46.4 3.3 %pick.7 = f32[2048,128]{1,0:T(8,128)S(1)} custom-call(s32[2048]{0:T(1024)S(1)} %bitcast.31, f32[2048]{0:T(1024)S(1)} %bitcast.28, f32[16384,128]{1,0:T(8,128)S(1)} %copy-done.1), custom_call_target="tpu_custom_call" | custom-call | flops 262144 | bytes 16777216 | tf_op jit(solution)/shard_map/pick/pallas_call | solution.py:122
  53.2 3.4 %copy-done.2 = f32[16384,128]{1,0:T(8,128)S(1)} copy-done((f32[16384,128]{1,0:T(8,128)S(1)}, f32[16384,128]{1,0:T(8,128)}, u32[]{:S(2)}) %copy-start.2) | copy-done | bytes 8388632
  56.5 3.3 %pick.4 = f32[2048,128]{1,0:T(8,128)S(1)} custom-call(s32[2048]{0:T(1024)S(1)} %bitcast.32, f32[2048]{0:T(1024)S(1)} %bitcast.27, f32[16384,128]{1,0:T(8,128)S(1)} %copy-done.2), custom_call_target="tpu_custom_call" | custom-call | flops 262144 | bytes 16777216 | tf_op jit(solution)/shard_map/pick/pallas_call | solution.py:122
  59.8 6.0 %collective-permute-done.2 = f32[2048,128]{1,0:T(8,128)} collective-permute-done((f32[2048,128]{1,0:T(8,128)S(1)}, f32[2048,128]{1,0:T(8,128)}, u32[]{:S(2)}, u32[]{:S(2)}) %collective-permute-start.2) | collective-permute-done | bytes 1048608 | tf_op jit(solution)/shard_map/ppermute | solution.py:211
  70.5 3.4 %copy-done.3 = f32[16384,128]{1,0:T(8,128)S(1)} copy-done((f32[16384,128]{1,0:T(8,128)S(1)}, f32[16384,128]{1,0:T(8,128)}, u32[]{:S(2)}) %copy-start.3) | copy-done | bytes 8388632
  73.9 3.3 %pick.6 = f32[2048,128]{1,0:T(8,128)S(1)} custom-call(s32[2048]{0:T(1024)S(1)} %bitcast.30, f32[2048]{0:T(1024)S(1)} %bitcast.29, f32[16384,128]{1,0:T(8,128)S(1)} %copy-done.3), custom_call_target="tpu_custom_call" | custom-call | flops 262144 | bytes 16777216 | tf_op jit(solution)/shard_map/pick/pallas_call | solution.py:122
  79.0 7.0 %collective-permute-done.3 = f32[1024,128]{1,0:T(8,128)} collective-permute-done((f32[1024,128]{1,0:T(8,128)}, f32[1024,128]{1,0:T(8,128)}, u32[]{:S(2)}, u32[]{:S(2)}) %collective-permute-start.3) | collective-permute-done | bytes 524320 | tf_op jit(solution)/shard_map/ppermute | solution.py:211
  92.0 5.8 %collective-permute-done.4 = f32[512,128]{1,0:T(8,128)S(1)} collective-permute-done((f32[512,128]{1,0:T(8,128)S(1)}, f32[512,128]{1,0:T(8,128)S(1)}, u32[]{:S(2)}, u32[]{:S(2)}) %collective-permute-start.4) | collective-permute-done | bytes 262176 | tf_op jit(solution)/shard_map/ppermute | solution.py:212
  99.5 1.9 %collective-permute-done.8 = f32[512,128]{1,0:T(8,128)S(1)} collective-permute-done((f32[512,128]{1,0:T(8,128)S(1)}, f32[512,128]{1,0:T(8,128)S(1)}, u32[]{:S(2)}, u32[]{:S(2)}) %collective-permute-start.8) | collective-permute-done | bytes 262176 | tf_op jit(solution)/shard_map/ppermute | solution.py:212
  101.4 2.6 %collective-permute-start.9 = (f32[256,128]{1,0:T(8,128)S(1)}, f32[256,128]{1,0:T(8,128)S(1)}, u32[]{:S(2)}, u32[]{:S(2)}) collective-permute-start(f32[256,128]{1,0:T(8,128)S(1)} %slice.99), channel_id=1, source_target_pairs={{0,16},{8,24},{16,0},{24,8},{1,17},{9,25},{17,1},{25,9},{2,18},{10... | collective-permute-start | bytes 393224 | tf_op jit(solution)/shard_map/ppermute | solution.py:212
  104.0 5.2 %collective-permute-done.5 = f32[256,128]{1,0:T(8,128)S(1)} collective-permute-done((f32[256,128]{1,0:T(8,128)S(1)}, f32[256,128]{1,0:T(8,128)S(1)}, u32[]{:S(2)}, u32[]{:S(2)}) %collective-permute-start.5) | collective-permute-done | bytes 131104 | tf_op jit(solution)/shard_map/ppermute | solution.py:212
  113.0 4.3 %collective-permute-done.11 = f32[128,128]{1,0:T(8,128)S(1)} collective-permute-done((f32[128,128]{1,0:T(8,128)S(1)}, f32[128,128]{1,0:T(8,128)S(1)}, u32[]{:S(2)}, u32[]{:S(2)}) %collective-permute-start.11) | collective-permute-done | bytes 65568 | tf_op jit(solution)/shard_map/ppermute | solution.py:211
  118.8 2.7 %collective-permute-done.12 = f32[128,128]{1,0:T(8,128)S(1)} collective-permute-done((f32[128,128]{1,0:T(8,128)S(1)}, f32[128,128]{1,0:T(8,128)S(1)}, u32[]{:S(2)}, u32[]{:S(2)}) %collective-permute-start.12) | collective-permute-done | bytes 65568 | tf_op jit(solution)/shard_map/ppermute | solution.py:211
  121.6 4.3 %collective-permute-done.13 = f32[128,128]{1,0:T(8,128)S(1)} collective-permute-done((f32[128,128]{1,0:T(8,128)S(1)}, f32[128,128]{1,0:T(8,128)S(1)}, u32[]{:S(2)}, u32[]{:S(2)}) %collective-permute-start.13) | collective-permute-done | bytes 65568 | tf_op jit(solution)/shard_map/ppermute | solution.py:212
  127.9 3.3 %collective-permute-done.14 = f32[128,128]{1,0:T(8,128)S(1)} collective-permute-done((f32[128,128]{1,0:T(8,128)S(1)}, f32[128,128]{1,0:T(8,128)S(1)}, u32[]{:S(2)}, u32[]{:S(2)}) %collective-permute-start.14) | collective-permute-done | bytes 65568 | tf_op jit(solution)/shard_map/ppermute | solution.py:212
  131.9 8.0 %finish.1 = (f32[512,128]{1,0:T(8,128)}, f32[128,128]{1,0:T(8,128)}) custom-call(f32[128,128]{1,0:T(8,128)} %add.65.gram_ref, f32[512,128]{1,0:T(8,128)} %pad_maximum_fusion.sketch_ref), custom_call_target="tpu_custom_call" | custom-call | tf_op jit(solution)/shard_map/finish/pallas_call | solution.py:295
  (87 shorter events, 34.0 us)
Async XLA Ops:
  0.6 21.0 %collective-permute-start.1 = (s32[8192]{0:T(1024)}, s32[8192]{0:T(1024)S(1)}, u32[]{:S(2)}, u32[]{:S(2)}) collective-permute-start(s32[8192]{0:T(1024)} %param.13), channel_id=1, source_target_pairs={{0,1},{1,0},{2,3},{3,2},{4,5},{5,4},{6,7},{7,6},{8,9},{9,8},{10,11... | collective-permute-start | bytes 98312 | tf_op jit(solution)/shard_map/ppermute | solution.py:211
  1.1 20.5 %collective-permute-start = (f32[8192,128]{1,0:T(8,128)}, f32[8192,128]{1,0:T(8,128)}, u32[]{:S(2)}, u32[]{:S(2)}) collective-permute-start(f32[8192,128]{1,0:T(8,128)} %x_ref.1), channel_id=1, source_target_pairs={{0,1},{1,0},{2,3},{3,2},{4,5},{5,4},{6,7},{7,6},{8,9},{9,8},{10,11... | collective-permute-start | bytes 12582920 | tf_op jit(solution)/shard_map/ppermute | solution.py:211
  7.7 2.2 %copy-start.6 = (f32[8192,128]{1,0:T(8,128)S(1)}, f32[8192,128]{1,0:T(8,128)}, u32[]{:S(2)}) copy-start(f32[8192,128]{1,0:T(8,128)} %x_ref.1) | copy-start | bytes 12582916
  19.0 2.0 %copy-start.4 = (f32[8192,128]{1,0:T(8,128)}, f32[8192,128]{1,0:T(8,128)S(1)}, u32[]{:S(2)}) copy-start(f32[8192,128]{1,0:T(8,128)S(1)} %own.1.own_ref) | copy-start | bytes 12582916
  21.7 2.2 %copy-start.5 = (f32[8192,128]{1,0:T(8,128)S(1)}, f32[8192,128]{1,0:T(8,128)}, u32[]{:S(2)}) copy-start(f32[8192,128]{1,0:T(8,128)} %copy-done.4) | copy-start | bytes 12582916
  36.0 3.3 %copy-start = (f32[16384,128]{1,0:T(8,128)}, f32[16384,128]{1,0:T(8,128)S(1)}, u32[]{:S(2)}) copy-start(f32[16384,128]{1,0:T(8,128)S(1)} %pair.1.table_ref) | copy-start | bytes 25165828
  39.3 26.5 %collective-permute-start.2 = (f32[2048,128]{1,0:T(8,128)S(1)}, f32[2048,128]{1,0:T(8,128)}, u32[]{:S(2)}, u32[]{:S(2)}) collective-permute-start(f32[2048,128]{1,0:T(8,128)S(1)} %pick.5), channel_id=1, source_target_pairs={{0,2},{1,3},{2,0},{3,1},{4,6},{5,7},{6,4},{7,5},{8,10},{9,11},{10,... | collective-permute-start | bytes 3145736 | tf_op jit(solution)/shard_map/ppermute | solution.py:211
  43.0 3.4 %copy-start.1 = (f32[16384,128]{1,0:T(8,128)S(1)}, f32[16384,128]{1,0:T(8,128)}, u32[]{:S(2)}) copy-start(f32[16384,128]{1,0:T(8,128)} %copy-done) | copy-start | bytes 25165828
  49.7 27.5 %collective-permute-start.6 = (f32[2048,128]{1,0:T(8,128)S(1)}, f32[2048,128]{1,0:T(8,128)S(1)}, u32[]{:S(2)}, u32[]{:S(2)}) collective-permute-start(f32[2048,128]{1,0:T(8,128)S(1)} %pick.7), channel_id=1, source_target_pairs={{0,4},{1,5},{2,6},{3,7},{4,0},{5,1},{6,2},{7,3},{8,12},{9,13},{10,... | collective-permute-start | bytes 3145736 | tf_op jit(solution)/shard_map/ppermute | solution.py:211
  53.2 3.4 %copy-start.2 = (f32[16384,128]{1,0:T(8,128)S(1)}, f32[16384,128]{1,0:T(8,128)}, u32[]{:S(2)}) copy-start(f32[16384,128]{1,0:T(8,128)} %copy-done) | copy-start | bytes 25165828
  68.0 17.9 %collective-permute-start.3 = (f32[1024,128]{1,0:T(8,128)}, f32[1024,128]{1,0:T(8,128)}, u32[]{:S(2)}, u32[]{:S(2)}) collective-permute-start(f32[1024,128]{1,0:T(8,128)} %slice.87), channel_id=1, source_target_pairs={{0,4},{1,5},{2,6},{3,7},{4,0},{5,1},{6,2},{7,3},{8,12},{9,13},{10,... | collective-permute-start | bytes 1572872 | tf_op jit(solution)/shard_map/ppermute | solution.py:211
  70.5 3.4 %copy-start.3 = (f32[16384,128]{1,0:T(8,128)S(1)}, f32[16384,128]{1,0:T(8,128)}, u32[]{:S(2)}) copy-start(f32[16384,128]{1,0:T(8,128)} %copy-done) | copy-start | bytes 25165828
  77.4 12.9 %collective-permute-start.7 = (f32[1024,128]{1,0:T(8,128)S(1)}, f32[1024,128]{1,0:T(8,128)S(1)}, u32[]{:S(2)}, u32[]{:S(2)}) collective-permute-start(f32[1024,128]{1,0:T(8,128)S(1)} %slice.95), channel_id=1, source_target_pairs={{0,2},{1,3},{2,0},{3,1},{4,6},{5,7},{6,4},{7,5},{8,10},{9,11},{10,... | collective-permute-start | bytes 1572872 | tf_op jit(solution)/shard_map/ppermute | solution.py:211
  87.1 10.7 %collective-permute-start.4 = (f32[512,128]{1,0:T(8,128)S(1)}, f32[512,128]{1,0:T(8,128)S(1)}, u32[]{:S(2)}, u32[]{:S(2)}) collective-permute-start(f32[512,128]{1,0:T(8,128)S(1)} %slice.89), channel_id=1, source_target_pairs={{0,8},{8,0},{16,24},{24,16},{1,9},{9,1},{17,25},{25,17},{2,10},{10... | collective-permute-start | bytes 786440 | tf_op jit(solution)/shard_map/ppermute | solution.py:212
  90.4 11.0 %collective-permute-start.8 = (f32[512,128]{1,0:T(8,128)S(1)}, f32[512,128]{1,0:T(8,128)S(1)}, u32[]{:S(2)}, u32[]{:S(2)}) collective-permute-start(f32[512,128]{1,0:T(8,128)S(1)} %slice.97), channel_id=1, source_target_pairs={{0,8},{8,0},{16,24},{24,16},{1,9},{9,1},{17,25},{25,17},{2,10},{10... | collective-permute-start | bytes 786440 | tf_op jit(solution)/shard_map/ppermute | solution.py:212
  97.9 11.3 %collective-permute-start.5 = (f32[256,128]{1,0:T(8,128)S(1)}, f32[256,128]{1,0:T(8,128)S(1)}, u32[]{:S(2)}, u32[]{:S(2)}) collective-permute-start(f32[256,128]{1,0:T(8,128)S(1)} %slice.91), channel_id=1, source_target_pairs={{0,16},{8,24},{16,0},{24,8},{1,17},{9,25},{17,1},{25,9},{2,18},{10... | collective-permute-start | bytes 393224 | tf_op jit(solution)/shard_map/ppermute | solution.py:212
  101.4 9.6 %collective-permute-start.9 = (f32[256,128]{1,0:T(8,128)S(1)}, f32[256,128]{1,0:T(8,128)S(1)}, u32[]{:S(2)}, u32[]{:S(2)}) collective-permute-start(f32[256,128]{1,0:T(8,128)S(1)} %slice.99), channel_id=1, source_target_pairs={{0,16},{8,24},{16,0},{24,8},{1,17},{9,25},{17,1},{25,9},{2,18},{10... | collective-permute-start | bytes 393224 | tf_op jit(solution)/shard_map/ppermute | solution.py:212
  111.5 1.3 collective-permute-start.10
  112.9 4.3 %collective-permute-start.11 = (f32[128,128]{1,0:T(8,128)S(1)}, f32[128,128]{1,0:T(8,128)S(1)}, u32[]{:S(2)}, u32[]{:S(2)}) collective-permute-start(f32[128,128]{1,0:T(8,128)S(1)} %add.61), channel_id=1, source_target_pairs={{0,2},{1,3},{2,0},{3,1},{4,6},{5,7},{6,4},{7,5},{8,10},{9,11},{10,... | collective-permute-start | bytes 196616 | tf_op jit(solution)/shard_map/ppermute | solution.py:211
  117.2 4.3 %collective-permute-start.12 = (f32[128,128]{1,0:T(8,128)S(1)}, f32[128,128]{1,0:T(8,128)S(1)}, u32[]{:S(2)}, u32[]{:S(2)}) collective-permute-start(f32[128,128]{1,0:T(8,128)S(1)} %add.62), channel_id=1, source_target_pairs={{0,4},{1,5},{2,6},{3,7},{4,0},{5,1},{6,2},{7,3},{8,12},{9,13},{10,... | collective-permute-start | bytes 196616 | tf_op jit(solution)/shard_map/ppermute | solution.py:211
  121.6 4.3 %collective-permute-start.13 = (f32[128,128]{1,0:T(8,128)S(1)}, f32[128,128]{1,0:T(8,128)S(1)}, u32[]{:S(2)}, u32[]{:S(2)}) collective-permute-start(f32[128,128]{1,0:T(8,128)S(1)} %add.63), channel_id=1, source_target_pairs={{0,8},{8,0},{16,24},{24,16},{1,9},{9,1},{17,25},{25,17},{2,10},{10... | collective-permute-start | bytes 196616 | tf_op jit(solution)/shard_map/ppermute | solution.py:212
  125.9 5.4 %collective-permute-start.14 = (f32[128,128]{1,0:T(8,128)S(1)}, f32[128,128]{1,0:T(8,128)S(1)}, u32[]{:S(2)}, u32[]{:S(2)}) collective-permute-start(f32[128,128]{1,0:T(8,128)S(1)} %add.64), channel_id=1, source_target_pairs={{0,16},{8,24},{16,0},{24,8},{1,17},{9,25},{17,1},{25,9},{2,18},{10... | collective-permute-start | bytes 196616 | tf_op jit(solution)/shard_map/ppermute | solution.py:212

commit v2 on v1

v2 whole, which is shorter than its diff:
```python
import functools
import math

import jax
import jax.numpy as jnp
from jax import lax
from jax.experimental import pallas as pl
from jax.experimental.pallas import tpu as pltpu
from jax.sharding import PartitionSpec as P

F32 = jnp.float32
BF16 = jnp.bfloat16
I32 = jnp.int32
SUB = 8
PER_WORD = 32
GROUP = SUB * PER_WORD
BLOCK = 4 * GROUP
MIB = 1 << 20


def parity(bits, width):
    total = jnp.zeros_like(bits)
    for place in range(width):
        total = total ^ (bits >> place)
    return total & 1


def split3(x):
    high = x.astype(BF16).astype(F32)
    rest = x - high
    mid = rest.astype(BF16).astype(F32)
    return high, mid, rest - mid


def bit_perm(size, bit):
    return [(i, i ^ bit) for i in range(size)]


def butterfly(parts, steps):
    for step in steps:
        mixed = list(parts)
        for i in range(len(parts)):
            if not i & step:
                mixed[i] = parts[i] + parts[i | step]
                mixed[i | step] = parts[i] - parts[i | step]
        parts = mixed
    return parts


def powers(count):
    return [1 << i for i in range(count.bit_length() - 1)]


def word_bit(v):
    return 1 << v if v < 31 else -(1 << 31)


def mix_block(x_ref, word_ref, out_ref, at):
    def signed_group(g, carry):
        base = pl.multiple_of(at + g * GROUP, GROUP)
        words = word_ref[pl.ds(pl.multiple_of(base // PER_WORD, SUB), SUB), :]
        parts = []
        for v in range(PER_WORD):
            part = x_ref[pl.ds(base + SUB * v, SUB), :]
            parts.append(jnp.where((words & word_bit(v)) != 0, part, -part))
        for v, part in enumerate(butterfly(parts, powers(PER_WORD))):
            out_ref[pl.ds(base + SUB * v, SUB), :] = part
        return carry

    lax.fori_loop(0, BLOCK // GROUP, signed_group, 0)

    def within_group(m, carry):
        base = pl.multiple_of(at + m * SUB * SUB, SUB * SUB)
        spots = [GROUP * k for k in range(BLOCK // GROUP)]
        parts = [
            out_ref[pl.ds(base + spot + t, SUB, stride=SUB), :] for spot in spots for t in range(SUB)
        ]
        parts = butterfly(parts, powers(len(parts)))
        for k, spot in enumerate(spots):
            for t in range(SUB):
                out_ref[pl.ds(base + spot + SUB * t, SUB), :] = parts[SUB * k + t]
        return carry

    lax.fori_loop(0, GROUP // (SUB * SUB), within_group, 0)


def spread_signs(bits_ref, word_ref):
    lanes = bits_ref.shape[1]
    at = lax.broadcasted_iota(I32, (SUB, lanes), 1)
    row = lax.broadcasted_iota(I32, (SUB, lanes), 0)
    weights = jnp.where(at % SUB == row, 1 << (at // SUB), 0).astype(F32)
    halves = lax.dot_general(
        weights, bits_ref[...].astype(F32), (((1,), (1,)), ((), ())), preferred_element_type=F32
    ).astype(I32)
    for g in range(word_ref.shape[0] // SUB):
        word = halves[:, 2 * g : 2 * g + 1] | halves[:, 2 * g + 1 : 2 * g + 2] << (lanes // SUB)
        word_ref[SUB * g : SUB * g + SUB, :] = jnp.broadcast_to(word, (SUB, word_ref.shape[1]))


def table_row(row):
    return (row & ~63) | ((row & 7) << 3) | ((row >> 3) & 7)


def mix_blocks(x_ref, bits_ref, x, mid, word_ref, sems, emit):
    blocks = mid.shape[0] // BLOCK

    def fetch(h):
        rows = pl.ds(pl.multiple_of(h * BLOCK, BLOCK), BLOCK)
        return pltpu.make_async_copy(x_ref.at[rows], x.at[rows], sems.at[h])

    for h in range(blocks):
        fetch(h).start()
    spread_signs(bits_ref, word_ref)

    def one(h, carry):
        fetch(h).wait()
        mix_block(x, word_ref, mid, h * BLOCK)
        return carry

    lax.fori_loop(0, blocks, one, 0)

    def across(g, carry):
        row = pl.multiple_of(g * SUB, SUB)
        parts = [mid[pl.ds(BLOCK * h + row, SUB), :] for h in range(blocks)]
        for h, part in enumerate(butterfly(parts, powers(blocks))):
            emit(BLOCK * h + row, part)
        return carry

    lax.fori_loop(0, BLOCK // SUB, across, 0, unroll=4)


def own_kernel(
    scale, spans, x_ref, bits_ref, me_ref, source_ref, offset_ref, out_ref, *refs
):
    x, mid, words, sems = refs[-4:]
    rows_dev = x.shape[0]
    me = me_ref[0]
    for n, span in enumerate(spans):
        row_ref, sign_ref = refs[2 * n], refs[2 * n + 1]
        to = 0
        for target, block, start, count in span:
            at = pl.multiple_of((me ^ target) * block + start, math.gcd(128, start, count))
            source = source_ref[:, pl.ds(at, count)]
            offset = offset_ref[:, pl.ds(at, count)]
            row_ref[:, to : to + count] = table_row(offset) + (source & 1) * rows_dev
            odd = parity(source & me, 16) != 0
            sign_ref[:, to : to + count] = jnp.where(odd, -scale, scale)
            to += count

    def emit(row, value):
        out_ref[pl.ds(row, SUB), :] = value

    mix_blocks(x_ref, bits_ref, x, mid, words, sems, emit)


def pair_kernel(x_ref, bits_ref, own_ref, out_ref, x, mid, words, sems):
    count = x.shape[0]

    def emit(row, value):
        own = own_ref[pl.ds(row, SUB), :]
        out_ref[pl.ds(row, SUB), :] = own + value
        out_ref[pl.ds(count + row, SUB), :] = own - value

    mix_blocks(x_ref, bits_ref, x, mid, words, sems, emit)


def pick_kernel(row_ref, sign_ref, table_ref, out_ref):
    count = out_ref.shape[0]
    unroll = math.gcd(count, 32)

    def some(i, carry):
        for u in range(unroll):
            r = i * unroll + u
            out_ref[pl.ds(r, 1), :] = table_ref[pl.ds(row_ref[0, r], 1), :] * sign_ref[0, r]
        return carry

    lax.fori_loop(0, count // unroll, some, 0)


def pick(places, table):
    rows, signs = places
    count = rows.shape[1]
    vmem = pl.BlockSpec(memory_space=pltpu.VMEM)
    smem = pl.BlockSpec(memory_space=pltpu.SMEM)
    return pl.pallas_call(
        pick_kernel,
        out_shape=jax.ShapeDtypeStruct((count, table.shape[1]), F32),
        in_specs=[smem, smem, vmem],
        out_specs=vmem,
        compiler_params=pltpu.CompilerParams(vmem_limit_bytes=14 * MIB),
        cost_estimate=pl.CostEstimate(
            flops=count * 128, bytes_accessed=count * 6 * 1024, transcendentals=0
        ),
        name="pick",
    )(rows, signs, pltpu.with_memory_space_constraint(table, pltpu.VMEM))


def factor_panel(left, right, at):
    shape = left.shape
    rows = lax.broadcasted_iota(I32, shape, 0)
    column = [jnp.broadcast_to(left[:, at + i : at + i + 1], shape) for i in range(SUB)]
    pivots = jnp.ones_like(left)
    for i in range(SUB):
        pivot = jnp.broadcast_to(column[i][i : i + 1, :], shape)
        pivots = jnp.where(rows == i, pivot, pivots)
        if i < SUB - 1:
            ratio = jnp.where(rows > i, column[i] * (1.0 / pivot), 0.0)
            for j in range(i + 1, SUB):
                column[j] = column[j] - ratio * jnp.broadcast_to(column[j][i : i + 1, :], shape)
            left = left - ratio * jnp.broadcast_to(left[i : i + 1, :], shape)
            right = right - ratio * jnp.broadcast_to(right[i : i + 1, :], shape)
    scale = lax.rsqrt(pivots)
    return left * scale, right * scale


def factor(gram):
    n = gram.shape[0]
    rest = gram
    unit = (
        lax.broadcasted_iota(I32, (n, n), 0) == lax.broadcasted_iota(I32, (n, n), 1)
    ).astype(F32)
    lanes = lax.broadcasted_iota(I32, (SUB, n), 1)
    panel_rows = lax.broadcasted_iota(I32, (SUB, n), 0)
    uppers, inverses = [], []
    for at in range(0, n, SUB):
        left, right = factor_panel(rest[:SUB], unit[:SUB], at)
        left = jnp.where(lanes >= panel_rows + at, left, 0.0)
        uppers.append(left)
        inverses.append(right)
        if at + SUB < n:
            h, m, l = split3(left)
            uh, um, ul = split3(right)
            terms = jnp.concatenate([h, h, m, h, l, m], 0)
            others = jnp.concatenate(
                [
                    jnp.concatenate([h, m, h, l, h, m], 0),
                    jnp.concatenate([uh, um, uh, ul, uh, um], 0),
                ],
                1,
            )
            change = jnp.dot(terms.T[at + SUB :], others, preferred_element_type=F32)
            rest = rest[SUB:] - change[:, :n]
            unit = unit[SUB:] - change[:, n:]
    return jnp.concatenate(uppers, 0), jnp.concatenate(inverses, 0)


def finish_kernel(gram_ref, sketch_ref, q_ref, upper_ref):
    upper, inverse = factor(gram_ref[...])
    upper_ref[...] = upper
    q_ref[...] = lax.dot_general(
        sketch_ref[...],
        inverse,
        (((1,), (1,)), ((), ())),
        precision=lax.Precision.HIGHEST,
        preferred_element_type=F32,
    )


def per_device(features, sign_bits, sample_device, sample_offset):
    rows_dev, width = features.shape
    n_outer = lax.axis_size("exa")
    n_inner = lax.axis_size("exb")
    n_all = n_outer * n_inner
    bits = n_all.bit_length() - 1
    inner_bits = n_inner.bit_length() - 1
    myself = lax.axis_index("exa") * n_inner + lax.axis_index("exb")
    total = sample_offset.shape[0]
    own_count = total // n_all
    vmem = pl.BlockSpec(memory_space=pltpu.VMEM)

    def swap(value, mask):
        if mask < n_inner:
            return lax.ppermute(value, "exb", bit_perm(n_inner, mask))
        return lax.ppermute(value, "exa", bit_perm(n_outer, mask // n_inner))

    outer = tuple(range(inner_bits, bits))
    inner = [(bit,) for bit in range(1, inner_bits)]
    chunk_rows = own_count // 2
    chunks = [
        (0, chunk_rows, inner + [outer]),
        (chunk_rows, chunk_rows, inner[::-1] + [outer]),
    ]

    def masks(step):
        listed = [0]
        for bit in step:
            listed = [e | 1 << bit for e in listed] + listed
        return listed

    def targets(steps):
        listed = [0]
        for step in steps[::-1]:
            listed = [m | e for m in masks(step) for e in listed]
        return listed

    firsts = []
    for start, count, steps in chunks:
        listed = targets(steps)
        moves = masks(steps[0])
        per = len(listed) // len(moves)
        firsts.append(
            [
                [(e, own_count, start, count) for e in listed[i * per : i * per + per]]
                for i in range(len(moves))
            ]
        )
    flat = [piece for pieces in firsts for piece in pieces]

    far_features = swap(features, 1)
    far_signs = swap(sign_bits, 1)
    params = pltpu.CompilerParams(vmem_limit_bytes=22 * MIB)
    scratch = [
        pltpu.VMEM((rows_dev, width), F32),
        pltpu.VMEM((rows_dev, width), F32),
        pltpu.VMEM((rows_dev // PER_WORD, width), I32),
        pltpu.SemaphoreType.DMA((rows_dev // BLOCK,)),
    ]
    bits_shape = (rows_dev // 128, 128)
    place_shapes = [
        jax.ShapeDtypeStruct((1, sum(count for _, _, _, count in piece)), kind)
        for piece in flat
        for kind in (I32, F32)
    ]
    own, *places = pl.pallas_call(
        functools.partial(own_kernel, 1.0 / math.sqrt(rows_dev * n_all), flat),
        out_shape=[jax.ShapeDtypeStruct((rows_dev, width), F32)] + place_shapes,
        in_specs=[
            pl.BlockSpec(memory_space=pl.ANY),
            vmem,
            pl.BlockSpec(memory_space=pltpu.SMEM),
            vmem,
            vmem,
        ],
        out_specs=[vmem] * (1 + len(place_shapes)),
        scratch_shapes=scratch,
        compiler_params=params,
        cost_estimate=pl.CostEstimate(flops=10**7, bytes_accessed=12 * MIB, transcendentals=0),
        name="own",
    )(
        pltpu.with_memory_space_constraint(features, pltpu.HBM),
        sign_bits.reshape(bits_shape),
        myself.reshape(1),
        sample_device.reshape(1, total),
        sample_offset.reshape(1, total),
    )
    table = pl.pallas_call(
        pair_kernel,
        out_shape=jax.ShapeDtypeStruct((2 * rows_dev, width), F32),
        in_specs=[pl.BlockSpec(memory_space=pl.ANY), vmem, vmem],
        out_specs=vmem,
        scratch_shapes=scratch,
        compiler_params=params,
        cost_estimate=pl.CostEstimate(flops=10**7, bytes_accessed=16 * MIB, transcendentals=0),
        name="pair",
    )(
        far_features,
        far_signs.reshape(bits_shape),
        pltpu.with_memory_space_constraint(own, pltpu.VMEM),
    )

    pairs = iter(zip(places[::2], places[1::2]))
    mine = [[next(pairs) for _ in pieces] for pieces in firsts]
    sent = [
        [swap(pick(one, table), mask) for one, mask in zip(some[:-1], masks(steps[0]))]
        for some, (_, _, steps) in zip(mine, chunks)
    ]
    kept = [pick(some[-1], table) for some in mine]
    for turn in range(1, max(len(steps) for _, _, steps in chunks) + 1):
        for n, (_, _, steps) in enumerate(chunks):
            if turn > len(steps):
                continue
            sums = functools.reduce(jnp.add, sent[n], kept[n])
            if turn < len(steps):
                listed = masks(steps[turn])
                per = sums.shape[0] // len(listed)
                sent[n] = [
                    swap(sums[i * per : i * per + per], move) for i, move in enumerate(listed[:-1])
                ]
                sums = sums[-per:]
            kept[n] = sums
    sketch = jnp.concatenate(kept, 0)

    gram = lax.dot_general(
        sketch,
        sketch,
        (((0,), (0,)), ((), ())),
        precision=lax.Precision.HIGHEST,
        preferred_element_type=F32,
    ) / total
    for bit in range(bits):
        gram = gram + swap(gram, 1 << bit)

    return pl.pallas_call(
        finish_kernel,
        out_shape=(
            jax.ShapeDtypeStruct((own_count, width), F32),
            jax.ShapeDtypeStruct((width, width), F32),
        ),
        in_specs=[vmem, vmem],
        out_specs=(vmem, vmem),
        name="finish",
    )(gram, sketch)


def solution(mesh):
    placed = (P(("exa", "exb"), None), P(("exa", "exb")), P(), P())
    return jax.shard_map(
        per_device,
        mesh=mesh,
        in_specs=placed,
        out_specs=(P(("exa", "exb"), None), P()),
        check_vma=False,
    )
```

time: 141 us -> 114 us (0.81)
  local copies, waits for them, and re-layouts: 22.9 us -> 2.56 us
  Pallas kernels: 42.4 us -> 30.9 us
  other arithmetic: 9.06 us -> 1.79 us
  starting transfers between devices: 19.1 us -> 25.9 us
  waiting for transfers between devices: 44.9 us -> 51.4 us
    unnamed x22 -> x6, local copies, waits for them, and re-layouts: 16.6 us -> 2.44 us
    pallas_call x6, Pallas kernels: 34.4 us -> 22.9 us  [the longest x4 13.2 us: pick(): pl.pallas_call(pick_kernel, out_shape=jax.ShapeDtypeStruct((count, table....]
    ppermute x15 -> x17, starting transfers between devices: 19.1 us -> 25.9 us  [the longest x8 15.8 us: swap(): return lax.ppermute(value, 'exa', bit_perm(n_outer, mask // n_inner))]
    ppermute x15 -> x17, waiting for transfers between devices: 44.9 us -> 51.4 us  [the longest x9 32.7 us: swap(): return lax.ppermute(value, 'exb', bit_perm(n_inner, mask))]
    gather x8 -> x0, local copies, waits for them, and re-layouts: 4.49 us -> none  [the longest x4 2.25 us: take(): jnp.take(sign_blocks[:, start:start + count], blocks, axis=0).reshape(-1)]
    add x14 -> x11, other arithmetic: 4.25 us -> 1.07 us  [the longest x5 0.67 us: per_device(): gram = gram + swap(gram, 1 << bit)]
    mul x2 -> x0, other arithmetic: 2.13 us -> none  [the longest x1 1.22 us: per_device(): sign_all = (1 - 2 * parity(source & myself, bits)).astype(F32) * scale]
  transfers between devices with their start and end apart: 15 -> 17, of which waited for: 12 -> 11; matrix products, arithmetic and copies ran while one was open for 11% -> 1% of each run, Pallas kernels for 14% -> 13%
where the time goes in v2:
time: 114 us
  waiting for transfers between devices  51.4 us (45%)
  Pallas kernels  30.9 us (27%)
  starting transfers between devices  25.9 us (23%)
  local copies, waits for them, and re-layouts  2.56 us (2%)
  other arithmetic  1.79 us (2%)
    ppermute x9, waiting for transfers between devices, swap(): return lax.ppermute(value, 'exb', bit_perm(n_inner, mask))  32.7 us
    ppermute x8, waiting for transfers between devices, swap(): return lax.ppermute(value, 'exa', bit_perm(n_outer, mask // n_inner))  18.7 us
    ppermute x8, starting transfers between devices, swap(): return lax.ppermute(value, 'exa', bit_perm(n_outer, mask // n_inner))  15.8 us
    pallas_call x4, Pallas kernels, pick(): pl.pallas_call(pick_kernel, out_shape=jax.ShapeDtypeStruct((count, table....  13.2 us
    ppermute x9, starting transfers between devices, swap(): return lax.ppermute(value, 'exb', bit_perm(n_inner, mask))  10.1 us
    pallas_call x1, Pallas kernels, per_device(): pl.pallas_call(finish_kernel, out_shape=(jax.ShapeDtypeStruct((own_count,...  7.97 us
    pallas_call x1, Pallas kernels, per_device(): pl.pallas_call(pair_kernel, out_shape=jax.ShapeDtypeStruct((2 * rows_dev,...  5.1 us
    pallas_call x1, Pallas kernels, per_device(): pl.pallas_call(functools.partial(own_kernel, 1.0 / math.sqrt(rows_dev * n...  4.64 us
  transfers between devices with their start and end apart: 17, of which 11 were waited for; matrix products, arithmetic and copies ran while one was open for 1% of the time, Pallas kernels for 13%

profile of v2, /device:TPU:0, one launch (start us, length us, event | category | flops | bytes accessed | tf_op | source)
XLA Modules:
  0.0 113.9 jit_solution(5922062501701256654)
XLA Ops:
  3.7 4.6 %own.1 = (f32[8192,128]{1,0:T(8,128)S(1)}, s32[1,2048]{1,0:T(1,128)S(1)}, f32[1,2048]{1,0:T(1,128)S(1)}, s32[1,2048]{1,0:T(1,128)S(1)}, f32[1,2048]{1,0:T(1,128)...) custom-call(f32[8192,128]{1,0:T(8,128)} %x_ref.1, ...), custom_call_target="tpu_custom_call" | custom-call | flops 10000000 | bytes 12582912 | tf_op jit(solution)/shard_map/own/pallas_call | solution.py:324
  8.3 5.1 %pair.1.table_ref = f32[16384,128]{1,0:T(8,128)S(1)} custom-call(f32[8192,128]{1,0:T(8,128)} %collective-permute-done.x_ref, s32[64,128]{1,0:T(8,128)S(1)} %bitcast.8, f32[8192,128]{1,0:T(8,128)S(1)} %get-tuple-element.13.own_ref), custom_call_target="tpu_custom_call" | custom-call | flops 10000000 | bytes 16777216 | tf_op jit(solution)/shard_map/pair/pallas_call | solution.py:346
  13.4 3.3 %pick.5 = f32[2048,128]{1,0:T(8,128)S(1)} custom-call(s32[1,2048]{1,0:T(1,128)S(1)} %get-tuple-element.14.row_ref, f32[1,2048]{1,0:T(1,128)S(1)} %get-tuple-element.15.sign_ref, f32[16384,128]{1,0:T(8,128)S(1)} %pair.1.table_ref), custom_call_target="tpu_custom_call" | custom-call | flops 262144 | bytes 12582912 | tf_op jit(solution)/shard_map/pick/pallas_call | solution.py:185
  16.7 3.0 %collective-permute-start.2 = (f32[2048,128]{1,0:T(8,128)S(1)}, f32[2048,128]{1,0:T(8,128)S(1)}, u32[]{:S(2)}, u32[]{:S(2)}) collective-permute-start(f32[2048,128]{1,0:T(8,128)S(1)} %pick.5), channel_id=1, source_target_pairs={{0,2},{1,3},{2,0},{3,1},{4,6},{5,7},{6,4},{7,5},{8,10},{9,11},{10,... | collective-permute-start | bytes 3145736 | tf_op jit(solution)/shard_map/ppermute | solution.py:273
  19.7 3.3 %pick.7 = f32[2048,128]{1,0:T(8,128)S(1)} custom-call(s32[1,2048]{1,0:T(1,128)S(1)} %get-tuple-element.18.row_ref, f32[1,2048]{1,0:T(1,128)S(1)} %get-tuple-element.19.sign_ref, f32[16384,128]{1,0:T(8,128)S(1)} %pair.1.table_ref), custom_call_target="tpu_custom_call" | custom-call | flops 262144 | bytes 12582912 | tf_op jit(solution)/shard_map/pick/pallas_call | solution.py:185
  23.0 1.6 %collective-permute-start.7 = (f32[2048,128]{1,0:T(8,128)S(1)}, f32[2048,128]{1,0:T(8,128)S(1)}, u32[]{:S(2)}, u32[]{:S(2)}) collective-permute-start(f32[2048,128]{1,0:T(8,128)S(1)} %pick.7), channel_id=1, source_target_pairs={{0,4},{1,5},{2,6},{3,7},{4,0},{5,1},{6,2},{7,3},{8,12},{9,13},{10,... | collective-permute-start | bytes 3145736 | tf_op jit(solution)/shard_map/ppermute | solution.py:273
  24.6 3.3 %pick.4 = f32[2048,128]{1,0:T(8,128)S(1)} custom-call(s32[1,2048]{1,0:T(1,128)S(1)} %get-tuple-element.11.row_ref, f32[1,2048]{1,0:T(1,128)S(1)} %get-tuple-element.12.sign_ref, f32[16384,128]{1,0:T(8,128)S(1)} %pair.1.table_ref), custom_call_target="tpu_custom_call" | custom-call | flops 262144 | bytes 12582912 | tf_op jit(solution)/shard_map/pick/pallas_call | solution.py:185
  27.9 15.2 %collective-permute-done.2 = f32[2048,128]{1,0:T(8,128)S(1)} collective-permute-done((f32[2048,128]{1,0:T(8,128)S(1)}, f32[2048,128]{1,0:T(8,128)S(1)}, u32[]{:S(2)}, u32[]{:S(2)}) %collective-permute-start.2) | collective-permute-done | bytes 1048608 | tf_op jit(solution)/shard_map/ppermute | solution.py:273
  43.3 1.8 %collective-permute-start.3 = (f32[1024,128]{1,0:T(8,128)S(1)}, f32[1024,128]{1,0:T(8,128)S(1)}, u32[]{:S(2)}, u32[]{:S(2)}) collective-permute-start(f32[1024,128]{1,0:T(8,128)S(1)} %slice.49), channel_id=1, source_target_pairs={{0,4},{1,5},{2,6},{3,7},{4,0},{5,1},{6,2},{7,3},{8,12},{9,13},{10,... | collective-permute-start | bytes 1572872 | tf_op jit(solution)/shard_map/ppermute | solution.py:273
  45.1 3.3 %pick.6 = f32[2048,128]{1,0:T(8,128)S(1)} custom-call(s32[1,2048]{1,0:T(1,128)S(1)} %get-tuple-element.16.row_ref, f32[1,2048]{1,0:T(1,128)S(1)} %get-tuple-element.17.sign_ref, f32[16384,128]{1,0:T(8,128)S(1)} %pair.1.table_ref), custom_call_target="tpu_custom_call" | custom-call | flops 262144 | bytes 12582912 | tf_op jit(solution)/shard_map/pick/pallas_call | solution.py:185
  50.1 9.0 %collective-permute-done.3 = f32[1024,128]{1,0:T(8,128)S(1)} collective-permute-done((f32[1024,128]{1,0:T(8,128)S(1)}, f32[1024,128]{1,0:T(8,128)S(1)}, u32[]{:S(2)}, u32[]{:S(2)}) %collective-permute-start.3) | collective-permute-done | bytes 524320 | tf_op jit(solution)/shard_map/ppermute | solution.py:273
  59.3 3.7 %collective-permute-start.4 = (f32[256,128]{1,0:T(8,128)S(1)}, f32[256,128]{1,0:T(8,128)S(1)}, u32[]{:S(2)}, u32[]{:S(2)}) collective-permute-start(f32[256,128]{1,0:T(8,128)S(1)} %get-tuple-element.20), channel_id=1, source_target_pairs={{0,24},{8,16},{16,8},{24,0},{1,25},{9,17},{17,9},{25,1},{2,26},{10... | collective-permute-start | bytes 393224 | tf_op jit(solution)/shard_map/ppermute | solution.py:274
  63.9 3.7 %collective-permute-start.9 = (f32[256,128]{1,0:T(8,128)S(1)}, f32[256,128]{1,0:T(8,128)S(1)}, u32[]{:S(2)}, u32[]{:S(2)}) collective-permute-start(f32[256,128]{1,0:T(8,128)S(1)} %get-tuple-element.23), channel_id=1, source_target_pairs={{0,24},{8,16},{16,8},{24,0},{1,25},{9,17},{17,9},{25,1},{2,26},{10... | collective-permute-start | bytes 393224 | tf_op jit(solution)/shard_map/ppermute | solution.py:274
  67.7 5.4 %collective-permute-start.10 = (f32[256,128]{1,0:T(8,128)S(1)}, f32[256,128]{1,0:T(8,128)S(1)}, u32[]{:S(2)}, u32[]{:S(2)}) collective-permute-start(f32[256,128]{1,0:T(8,128)S(1)} %get-tuple-element.25), channel_id=1, source_target_pairs={{0,16},{8,24},{16,0},{24,8},{1,17},{9,25},{17,1},{25,9},{2,18},{10... | collective-permute-start | bytes 393224 | tf_op jit(solution)/shard_map/ppermute | solution.py:274
  73.1 5.3 %collective-permute-done.5 = f32[256,128]{1,0:T(8,128)S(1)} collective-permute-done((f32[256,128]{1,0:T(8,128)S(1)}, f32[256,128]{1,0:T(8,128)S(1)}, u32[]{:S(2)}, u32[]{:S(2)}) %collective-permute-start.5) | collective-permute-done | bytes 131104 | tf_op jit(solution)/shard_map/ppermute | solution.py:274
  78.4 6.0 %collective-permute-done.10 = f32[256,128]{1,0:T(8,128)S(1)} collective-permute-done((f32[256,128]{1,0:T(8,128)S(1)}, f32[256,128]{1,0:T(8,128)S(1)}, u32[]{:S(2)}, u32[]{:S(2)}) %collective-permute-start.10) | collective-permute-done | bytes 131104 | tf_op jit(solution)/shard_map/ppermute | solution.py:274
  85.1 1.2 %collective-permute-done.12 = f32[128,128]{1,0:T(8,128)S(1)} collective-permute-done((f32[128,128]{1,0:T(8,128)S(1)}, f32[128,128]{1,0:T(8,128)S(1)}, u32[]{:S(2)}, u32[]{:S(2)}) %collective-permute-start.12) | collective-permute-done | bytes 65568 | tf_op jit(solution)/shard_map/ppermute | solution.py:273
  86.9 3.7 %collective-permute-done.13 = f32[128,128]{1,0:T(8,128)S(1)} collective-permute-done((f32[128,128]{1,0:T(8,128)S(1)}, f32[128,128]{1,0:T(8,128)S(1)}, u32[]{:S(2)}, u32[]{:S(2)}) %collective-permute-start.13) | collective-permute-done | bytes 65568 | tf_op jit(solution)/shard_map/ppermute | solution.py:273
  90.7 1.6 %collective-permute-start.14 = (f32[128,128]{1,0:T(8,128)S(1)}, f32[128,128]{1,0:T(8,128)S(1)}, u32[]{:S(2)}, u32[]{:S(2)}) collective-permute-start(f32[128,128]{1,0:T(8,128)S(1)} %add.60), channel_id=1, source_target_pairs={{0,4},{1,5},{2,6},{3,7},{4,0},{5,1},{6,2},{7,3},{8,12},{9,13},{10,... | collective-permute-start | bytes 196616 | tf_op jit(solution)/shard_map/ppermute | solution.py:273
  92.2 2.7 %collective-permute-done.14 = f32[128,128]{1,0:T(8,128)S(1)} collective-permute-done((f32[128,128]{1,0:T(8,128)S(1)}, f32[128,128]{1,0:T(8,128)S(1)}, u32[]{:S(2)}, u32[]{:S(2)}) %collective-permute-start.14) | collective-permute-done | bytes 65568 | tf_op jit(solution)/shard_map/ppermute | solution.py:273
  95.2 4.1 %collective-permute-done.15 = f32[128,128]{1,0:T(8,128)S(1)} collective-permute-done((f32[128,128]{1,0:T(8,128)S(1)}, f32[128,128]{1,0:T(8,128)S(1)}, u32[]{:S(2)}, u32[]{:S(2)}) %collective-permute-start.15) | collective-permute-done | bytes 65568 | tf_op jit(solution)/shard_map/ppermute | solution.py:274
  99.3 2.0 %collective-permute-start.16 = (f32[128,128]{1,0:T(8,128)S(1)}, f32[128,128]{1,0:T(8,128)S(1)}, u32[]{:S(2)}, u32[]{:S(2)}) collective-permute-start(f32[128,128]{1,0:T(8,128)S(1)} %add.62), channel_id=1, source_target_pairs={{0,16},{8,24},{16,0},{24,8},{1,17},{9,25},{17,1},{25,9},{2,18},{10... | collective-permute-start | bytes 196616 | tf_op jit(solution)/shard_map/ppermute | solution.py:274
  102.1 3.2 %collective-permute-done.16 = f32[128,128]{1,0:T(8,128)S(1)} collective-permute-done((f32[128,128]{1,0:T(8,128)S(1)}, f32[128,128]{1,0:T(8,128)S(1)}, u32[]{:S(2)}, u32[]{:S(2)}) %collective-permute-start.16) | collective-permute-done | bytes 65568 | tf_op jit(solution)/shard_map/ppermute | solution.py:274
  105.9 8.0 %finish.1 = (f32[512,128]{1,0:T(8,128)}, f32[128,128]{1,0:T(8,128)}) custom-call(f32[128,128]{1,0:T(8,128)} %add.63.gram_ref, f32[512,128]{1,0:T(8,128)} %pad_maximum_fusion.sketch_ref), custom_call_target="tpu_custom_call" | custom-call | tf_op jit(solution)/shard_map/finish/pallas_call | solution.py:393
  (40 shorter events, 9.0 us)
Async XLA Ops:
  0.6 7.7 %collective-permute-start = (f32[8192,128]{1,0:T(8,128)}, f32[8192,128]{1,0:T(8,128)}, u32[]{:S(2)}, u32[]{:S(2)}) collective-permute-start(f32[8192,128]{1,0:T(8,128)} %x_ref.1), channel_id=1, source_target_pairs={{0,1},{1,0},{2,3},{3,2},{4,5},{5,4},{6,7},{7,6},{8,9},{9,8},{10,11... | collective-permute-start | bytes 12582920 | tf_op jit(solution)/shard_map/ppermute | solution.py:273
  1.1 7.2 %collective-permute-start.1 = (s32[8192]{0:T(1024)}, s32[8192]{0:T(1024)S(1)}, u32[]{:S(2)}, u32[]{:S(2)}) collective-permute-start(s32[8192]{0:T(1024)} %param.5), channel_id=1, source_target_pairs={{0,1},{1,0},{2,3},{3,2},{4,5},{5,4},{6,7},{7,6},{8,9},{9,8},{10,11... | collective-permute-start | bytes 98312 | tf_op jit(solution)/shard_map/ppermute | solution.py:273
  1.2 0.8 copy-start
  2.1 0.8 copy-start.1
  2.9 0.8 copy-start.2
  16.7 26.4 %collective-permute-start.2 = (f32[2048,128]{1,0:T(8,128)S(1)}, f32[2048,128]{1,0:T(8,128)S(1)}, u32[]{:S(2)}, u32[]{:S(2)}) collective-permute-start(f32[2048,128]{1,0:T(8,128)S(1)} %pick.5), channel_id=1, source_target_pairs={{0,2},{1,3},{2,0},{3,1},{4,6},{5,7},{6,4},{7,5},{8,10},{9,11},{10,... | collective-permute-start | bytes 3145736 | tf_op jit(solution)/shard_map/ppermute | solution.py:273
  23.0 26.1 %collective-permute-start.7 = (f32[2048,128]{1,0:T(8,128)S(1)}, f32[2048,128]{1,0:T(8,128)S(1)}, u32[]{:S(2)}, u32[]{:S(2)}) collective-permute-start(f32[2048,128]{1,0:T(8,128)S(1)} %pick.7), channel_id=1, source_target_pairs={{0,4},{1,5},{2,6},{3,7},{4,0},{5,1},{6,2},{7,3},{8,12},{9,13},{10,... | collective-permute-start | bytes 3145736 | tf_op jit(solution)/shard_map/ppermute | solution.py:273
  43.3 15.9 %collective-permute-start.3 = (f32[1024,128]{1,0:T(8,128)S(1)}, f32[1024,128]{1,0:T(8,128)S(1)}, u32[]{:S(2)}, u32[]{:S(2)}) collective-permute-start(f32[1024,128]{1,0:T(8,128)S(1)} %slice.49), channel_id=1, source_target_pairs={{0,4},{1,5},{2,6},{3,7},{4,0},{5,1},{6,2},{7,3},{8,12},{9,13},{10,... | collective-permute-start | bytes 1572872 | tf_op jit(solution)/shard_map/ppermute | solution.py:273
  49.3 14.4 %collective-permute-start.8 = (f32[1024,128]{1,0:T(8,128)S(1)}, f32[1024,128]{1,0:T(8,128)S(1)}, u32[]{:S(2)}, u32[]{:S(2)}) collective-permute-start(f32[1024,128]{1,0:T(8,128)S(1)} %slice.55), channel_id=1, source_target_pairs={{0,2},{1,3},{2,0},{3,1},{4,6},{5,7},{6,4},{7,5},{8,10},{9,11},{10,... | collective-permute-start | bytes 1572872 | tf_op jit(solution)/shard_map/ppermute | solution.py:273
  59.3 8.4 %collective-permute-start.4 = (f32[256,128]{1,0:T(8,128)S(1)}, f32[256,128]{1,0:T(8,128)S(1)}, u32[]{:S(2)}, u32[]{:S(2)}) collective-permute-start(f32[256,128]{1,0:T(8,128)S(1)} %get-tuple-element.20), channel_id=1, source_target_pairs={{0,24},{8,16},{16,8},{24,0},{1,25},{9,17},{17,9},{25,1},{2,26},{10... | collective-permute-start | bytes 393224 | tf_op jit(solution)/shard_map/ppermute | solution.py:274
  63.0 10.1 %collective-permute-start.6 = (f32[256,128]{1,0:T(8,128)S(1)}, f32[256,128]{1,0:T(8,128)S(1)}, u32[]{:S(2)}, u32[]{:S(2)}) collective-permute-start(f32[256,128]{1,0:T(8,128)S(1)} %get-tuple-element.21), channel_id=1, source_target_pairs={{0,8},{8,0},{16,24},{24,16},{1,9},{9,1},{17,25},{25,17},{2,10},{10... | collective-permute-start | bytes 393224 | tf_op jit(solution)/shard_map/ppermute | solution.py:274
  63.0 15.4 %collective-permute-start.5 = (f32[256,128]{1,0:T(8,128)S(1)}, f32[256,128]{1,0:T(8,128)S(1)}, u32[]{:S(2)}, u32[]{:S(2)}) collective-permute-start(f32[256,128]{1,0:T(8,128)S(1)} %get-tuple-element.22), channel_id=1, source_target_pairs={{0,16},{8,24},{16,0},{24,8},{1,17},{9,25},{17,1},{25,9},{2,18},{10... | collective-permute-start | bytes 393224 | tf_op jit(solution)/shard_map/ppermute | solution.py:274
  63.9 14.5 %collective-permute-start.9 = (f32[256,128]{1,0:T(8,128)S(1)}, f32[256,128]{1,0:T(8,128)S(1)}, u32[]{:S(2)}, u32[]{:S(2)}) collective-permute-start(f32[256,128]{1,0:T(8,128)S(1)} %get-tuple-element.23), channel_id=1, source_target_pairs={{0,24},{8,16},{16,8},{24,0},{1,25},{9,17},{17,9},{25,1},{2,26},{10... | collective-permute-start | bytes 393224 | tf_op jit(solution)/shard_map/ppermute | solution.py:274
  67.5 10.9 %collective-permute-start.11 = (f32[256,128]{1,0:T(8,128)S(1)}, f32[256,128]{1,0:T(8,128)S(1)}, u32[]{:S(2)}, u32[]{:S(2)}) collective-permute-start(f32[256,128]{1,0:T(8,128)S(1)} %get-tuple-element.24), channel_id=1, source_target_pairs={{0,8},{8,0},{16,24},{24,16},{1,9},{9,1},{17,25},{25,17},{2,10},{10... | collective-permute-start | bytes 393224 | tf_op jit(solution)/shard_map/ppermute | solution.py:274
  67.7 16.7 %collective-permute-start.10 = (f32[256,128]{1,0:T(8,128)S(1)}, f32[256,128]{1,0:T(8,128)S(1)}, u32[]{:S(2)}, u32[]{:S(2)}) collective-permute-start(f32[256,128]{1,0:T(8,128)S(1)} %get-tuple-element.25), channel_id=1, source_target_pairs={{0,16},{8,24},{16,0},{24,8},{1,17},{9,25},{17,1},{25,9},{2,18},{10... | collective-permute-start | bytes 393224 | tf_op jit(solution)/shard_map/ppermute | solution.py:274
  85.0 1.3 %collective-permute-start.12 = (f32[128,128]{1,0:T(8,128)S(1)}, f32[128,128]{1,0:T(8,128)S(1)}, u32[]{:S(2)}, u32[]{:S(2)}) collective-permute-start(f32[128,128]{1,0:T(8,128)S(1)} %convolution_multiply_fusion), channel_id=1, source_target_pairs={{0,1},{1,0},{2,3},{3,2},{4,5},{5,4},{6,7},{7,6},{8,9},{9,8},{10,11... | collective-permute-start | bytes 196616 | tf_op jit(solution)/shard_map/ppermute | solution.py:273
  86.3 4.3 %collective-permute-start.13 = (f32[128,128]{1,0:T(8,128)S(1)}, f32[128,128]{1,0:T(8,128)S(1)}, u32[]{:S(2)}, u32[]{:S(2)}) collective-permute-start(f32[128,128]{1,0:T(8,128)S(1)} %add.59), channel_id=1, source_target_pairs={{0,2},{1,3},{2,0},{3,1},{4,6},{5,7},{6,4},{7,5},{8,10},{9,11},{10,... | collective-permute-start | bytes 196616 | tf_op jit(solution)/shard_map/ppermute | solution.py:273
  90.7 4.3 %collective-permute-start.14 = (f32[128,128]{1,0:T(8,128)S(1)}, f32[128,128]{1,0:T(8,128)S(1)}, u32[]{:S(2)}, u32[]{:S(2)}) collective-permute-start(f32[128,128]{1,0:T(8,128)S(1)} %add.60), channel_id=1, source_target_pairs={{0,4},{1,5},{2,6},{3,7},{4,0},{5,1},{6,2},{7,3},{8,12},{9,13},{10,... | collective-permute-start | bytes 196616 | tf_op jit(solution)/shard_map/ppermute | solution.py:273
  95.0 4.3 %collective-permute-start.15 = (f32[128,128]{1,0:T(8,128)S(1)}, f32[128,128]{1,0:T(8,128)S(1)}, u32[]{:S(2)}, u32[]{:S(2)}) collective-permute-start(f32[128,128]{1,0:T(8,128)S(1)} %add.61), channel_id=1, source_target_pairs={{0,8},{8,0},{16,24},{24,16},{1,9},{9,1},{17,25},{25,17},{2,10},{10... | collective-permute-start | bytes 196616 | tf_op jit(solution)/shard_map/ppermute | solution.py:274
  99.3 5.9 %collective-permute-start.16 = (f32[128,128]{1,0:T(8,128)S(1)}, f32[128,128]{1,0:T(8,128)S(1)}, u32[]{:S(2)}, u32[]{:S(2)}) collective-permute-start(f32[128,128]{1,0:T(8,128)S(1)} %add.62), channel_id=1, source_target_pairs={{0,16},{8,24},{16,0},{24,8},{1,17},{9,25},{17,1},{25,9},{2,18},{10... | collective-permute-start | bytes 196616 | tf_op jit(solution)/shard_map/ppermute | solution.py:274

commit v3 on v2

--- a/solution.py
+++ b/solution.py
@@ -130,22 +130,22 @@
 
 
 def own_kernel(
-    scale, spans, x_ref, bits_ref, me_ref, source_ref, offset_ref, out_ref, *refs
+    scale, targets, pieces, x_ref, bits_ref, me_ref, source_ref, offset_ref, out_ref, *refs
 ):
     x, mid, words, sems = refs[-4:]
     rows_dev = x.shape[0]
     me = me_ref[0]
-    for n, span in enumerate(spans):
-        row_ref, sign_ref = refs[2 * n], refs[2 * n + 1]
-        to = 0
-        for target, block, start, count in span:
-            at = pl.multiple_of((me ^ target) * block + start, math.gcd(128, start, count))
-            source = source_ref[:, pl.ds(at, count)]
-            offset = offset_ref[:, pl.ds(at, count)]
-            row_ref[:, to : to + count] = table_row(offset) + (source & 1) * rows_dev
-            odd = parity(source & me, 16) != 0
-            sign_ref[:, to : to + count] = jnp.where(odd, -scale, scale)
-            to += count
+    block = source_ref.shape[1] // targets
+    for target in range(0, targets, 2):
+        at = pl.multiple_of((me ^ target) * block, math.gcd(128, block))
+        source = source_ref[:, pl.ds(at, block)]
+        rows = table_row(offset_ref[:, pl.ds(at, block)]) + (source & 1) * rows_dev
+        signs = jnp.where(parity(source & me, 16) != 0, -scale, scale)
+        for n, (which, start, count) in enumerate(pieces):
+            if target in which:
+                to = which.index(target) * count
+                refs[2 * n][:, to : to + count] = rows[:, start : start + count]
+                refs[2 * n + 1][:, to : to + count] = signs[:, start : start + count]
 
     def emit(row, value):
         out_ref[pl.ds(row, SUB), :] = value
@@ -164,7 +164,8 @@
     mix_blocks(x_ref, bits_ref, x, mid, words, sems, emit)
 
 
-def pick_kernel(row_ref, sign_ref, table_ref, out_ref):
+def pick_kernel(row_ref, sign_ref, table_ref, *refs):
+    out_ref = refs[-1]
     count = out_ref.shape[0]
     unroll = math.gcd(count, 32)
 
@@ -177,7 +178,7 @@
     lax.fori_loop(0, count // unroll, some, 0)
 
 
-def pick(places, table):
+def pick(places, table, after=()):
     rows, signs = places
     count = rows.shape[1]
     vmem = pl.BlockSpec(memory_space=pltpu.VMEM)
@@ -185,14 +186,14 @@
     return pl.pallas_call(
         pick_kernel,
         out_shape=jax.ShapeDtypeStruct((count, table.shape[1]), F32),
-        in_specs=[smem, smem, vmem],
+        in_specs=[smem, smem, vmem] + [pl.BlockSpec(memory_space=pl.ANY)] * len(after),
         out_specs=vmem,
         compiler_params=pltpu.CompilerParams(vmem_limit_bytes=14 * MIB),
         cost_estimate=pl.CostEstimate(
-            flops=count * 128, bytes_accessed=count * 6 * 1024, transcendentals=0
+            flops=1024, bytes_accessed=1024, transcendentals=0
         ),
         name="pick",
-    )(rows, signs, pltpu.with_memory_space_constraint(table, pltpu.VMEM))
+    )(rows, signs, pltpu.with_memory_space_constraint(table, pltpu.VMEM), *after)
 
 
 def factor_panel(left, right, at):
@@ -275,11 +276,12 @@
 
     outer = tuple(range(inner_bits, bits))
     inner = [(bit,) for bit in range(1, inner_bits)]
-    chunk_rows = own_count // 2
-    chunks = [
-        (0, chunk_rows, inner + [outer]),
-        (chunk_rows, chunk_rows, inner[::-1] + [outer]),
-    ]
+    back = inner[::-1]
+    orders = [(16, inner[:1] + [outer[:1]] + inner[1:] + [outer[1:]]), (16, back[:1] + [outer[:1]] + back[1:] + [outer[1:]]), (16, inner + [(bit,) for bit in outer]), (16, back + [(bit,) for bit in outer])]
+    chunks, start = [], 0
+    for share, steps in orders:
+        chunks.append((start, own_count * share // 64, steps))
+        start += own_count * share // 64
 
     def masks(step):
         listed = [0]
@@ -300,7 +302,7 @@
         per = len(listed) // len(moves)
         firsts.append(
             [
-                [(e, own_count, start, count) for e in listed[i * per : i * per + per]]
+                (listed[i * per : i * per + per], start, count)
                 for i in range(len(moves))
             ]
         )
@@ -317,12 +319,12 @@
     ]
     bits_shape = (rows_dev // 128, 128)
     place_shapes = [
-        jax.ShapeDtypeStruct((1, sum(count for _, _, _, count in piece)), kind)
-        for piece in flat
+        jax.ShapeDtypeStruct((1, len(which) * count), kind)
+        for which, _, count in flat
         for kind in (I32, F32)
     ]
     own, *places = pl.pallas_call(
-        functools.partial(own_kernel, 1.0 / math.sqrt(rows_dev * n_all), flat),
+        functools.partial(own_kernel, 1.0 / math.sqrt(rows_dev * n_all), n_all, flat),
         out_shape=[jax.ShapeDtypeStruct((rows_dev, width), F32)] + place_shapes,
         in_specs=[
             pl.BlockSpec(memory_space=pl.ANY),
@@ -364,7 +366,11 @@
         [swap(pick(one, table), mask) for one, mask in zip(some[:-1], masks(steps[0]))]
         for some, (_, _, steps) in zip(mine, chunks)
     ]
-    kept = [pick(some[-1], table) for some in mine]
+    waits = [None,None,0,1]
+    kept = [
+        pick(some[-1], table, () if wait is None else (sent[wait][0],))
+        for some, wait in zip(mine, waits)
+    ]
     for turn in range(1, max(len(steps) for _, _, steps in chunks) + 1):
         for n, (_, _, steps) in enumerate(chunks):
             if turn > len(steps):

time: 114 us -> 97.8 us (0.86)
  waiting for transfers between devices: 51.4 us -> 28.2 us
  starting transfers between devices: 25.9 us -> 30.5 us
  Pallas kernels: 30.9 us -> 32.9 us
    ppermute x9 -> x13, waiting for transfers between devices: 32.7 us -> 15.5 us  [swap(): return lax.ppermute(value, 'exb', bit_perm(n_inner, mask))]
    ppermute x8 -> x10, waiting for transfers between devices: 18.7 us -> 12.7 us  [swap(): return lax.ppermute(value, 'exa', bit_perm(n_outer, mask // n_inner))]
    ppermute x9 -> x13, starting transfers between devices: 10.1 us -> 14.8 us  [swap(): return lax.ppermute(value, 'exb', bit_perm(n_inner, mask))]
    pallas_call x4 -> x8, Pallas kernels: 13.2 us -> 15.3 us  [pick(): pl.pallas_call(pick_kernel, out_shape=jax.ShapeDtypeStruct((count, table....]
    ppermute x8 -> x10, starting transfers between devices: 15.8 us -> 15.7 us  [swap(): return lax.ppermute(value, 'exa', bit_perm(n_outer, mask // n_inner))]
  transfers between devices with their start and end apart: 17 -> 23, of which waited for: 11 -> 15; matrix products, arithmetic and copies ran while one was open for 1% -> 1% of each run, Pallas kernels for 13% -> 18%
where the time goes in v3:
time: 97.8 us; the launch traced here: 97.5 us
  Pallas kernels  32.9 us (34%)
  starting transfers between devices  30.5 us (31%)
  waiting for transfers between devices  28.2 us (29%)
  local copies, waits for them, and re-layouts  2.58 us (3%)
  other arithmetic  1.85 us (2%)
    ppermute x10, starting transfers between devices, swap(): return lax.ppermute(value, 'exa', bit_perm(n_outer, mask // n_inner))  15.7 us
    ppermute x13, waiting for transfers between devices, swap(): return lax.ppermute(value, 'exb', bit_perm(n_inner, mask))  15.5 us
    pallas_call x8, Pallas kernels, pick(): pl.pallas_call(pick_kernel, out_shape=jax.ShapeDtypeStruct((count, table....  15.3 us
    ppermute x13, starting transfers between devices, swap(): return lax.ppermute(value, 'exb', bit_perm(n_inner, mask))  14.8 us
    ppermute x10, waiting for transfers between devices, swap(): return lax.ppermute(value, 'exa', bit_perm(n_outer, mask // n_inner))  12.7 us
    pallas_call x1, Pallas kernels, per_device(): pl.pallas_call(finish_kernel, out_shape=(jax.ShapeDtypeStruct((own_count,...  7.98 us
    pallas_call x1, Pallas kernels, per_device(): pl.pallas_call(pair_kernel, out_shape=jax.ShapeDtypeStruct((2 * rows_dev,...  5.1 us
    pallas_call x1, Pallas kernels, per_device(): pl.pallas_call(functools.partial(own_kernel, 1.0 / math.sqrt(rows_dev * n...  4.57 us
  transfers between devices with their start and end apart: 23, of which 15 were waited for; matrix products, arithmetic and copies ran while one was open for 1% of the time, Pallas kernels for 18%

profile of v3, /device:TPU:0, one launch (start us, length us, event | category | flops | bytes accessed | tf_op | source)
XLA Modules:
  0.0 97.5 jit_solution(3483262436411141352)
XLA Ops:
  3.7 4.6 %own.1 = (f32[8192,128]{1,0:T(8,128)S(1)}, s32[1,1024]{1,0:T(1,128)S(1)}, f32[1,1024]{1,0:T(1,128)S(1)}, s32[1,1024]{1,0:T(1,128)S(1)}, f32[1,1024]{1,0:T(1,128)...) custom-call(f32[8192,128]{1,0:T(8,128)} %x_ref.1, ...), custom_call_target="tpu_custom_call" | custom-call | flops 10000000 | bytes 12582912 | tf_op jit(solution)/shard_map/own/pallas_call | solution.py:326
  8.3 5.1 %pair.1.table_ref = f32[16384,128]{1,0:T(8,128)S(1)} custom-call(f32[8192,128]{1,0:T(8,128)} %collective-permute-done.x_ref, s32[64,128]{1,0:T(8,128)S(1)} %bitcast.8, f32[8192,128]{1,0:T(8,128)S(1)} %get-tuple-element.21.own_ref), custom_call_target="tpu_custom_call" | custom-call | flops 10000000 | bytes 16777216 | tf_op jit(solution)/shard_map/pair/pallas_call | solution.py:348
  13.4 1.9 %pick.9 = f32[1024,128]{1,0:T(8,128)S(1)} custom-call(s32[1,1024]{1,0:T(1,128)S(1)} %get-tuple-element.22.row_ref, f32[1,1024]{1,0:T(1,128)S(1)} %get-tuple-element.23.sign_ref, f32[16384,128]{1,0:T(8,128)S(1)} %pair.1.table_ref), custom_call_target="tpu_custom_call" | custom-call | flops 1024 | bytes 1024 | tf_op jit(solution)/shard_map/pick/pallas_call | solution.py:186
  15.3 2.9 %collective-permute-start.2 = (f32[1024,128]{1,0:T(8,128)S(1)}, f32[1024,128]{1,0:T(8,128)S(1)}, u32[]{:S(2)}, u32[]{:S(2)}) collective-permute-start(f32[1024,128]{1,0:T(8,128)S(1)} %pick.9), channel_id=1, source_target_pairs={{0,2},{1,3},{2,0},{3,1},{4,6},{5,7},{6,4},{7,5},{8,10},{9,11},{10,... | collective-permute-start | bytes 1572872 | tf_op jit(solution)/shard_map/ppermute | solution.py:274
  18.3 1.9 %pick.11 = f32[1024,128]{1,0:T(8,128)S(1)} custom-call(s32[1,1024]{1,0:T(1,128)S(1)} %get-tuple-element.26.row_ref, f32[1,1024]{1,0:T(1,128)S(1)} %get-tuple-element.27.sign_ref, f32[16384,128]{1,0:T(8,128)S(1)} %pair.1.table_ref), custom_call_target="tpu_custom_call" | custom-call | flops 1024 | bytes 1024 | tf_op jit(solution)/shard_map/pick/pallas_call | solution.py:186
  21.8 1.9 %pick.13 = f32[1024,128]{1,0:T(8,128)S(1)} custom-call(s32[1,1024]{1,0:T(1,128)S(1)} %get-tuple-element.30.row_ref, f32[1,1024]{1,0:T(1,128)S(1)} %get-tuple-element.31.sign_ref, f32[16384,128]{1,0:T(8,128)S(1)} %pair.1.table_ref), custom_call_target="tpu_custom_call" | custom-call | flops 1024 | bytes 1024 | tf_op jit(solution)/shard_map/pick/pallas_call | solution.py:186
  24.3 1.9 %pick.15 = f32[1024,128]{1,0:T(8,128)S(1)} custom-call(s32[1,1024]{1,0:T(1,128)S(1)} %get-tuple-element.34.row_ref, f32[1,1024]{1,0:T(1,128)S(1)} %get-tuple-element.35.sign_ref, f32[16384,128]{1,0:T(8,128)S(1)} %pair.1.table_ref), custom_call_target="tpu_custom_call" | custom-call | flops 1024 | bytes 1024 | tf_op jit(solution)/shard_map/pick/pallas_call | solution.py:186
  26.3 1.9 %pick.8 = f32[1024,128]{1,0:T(8,128)S(1)} custom-call(s32[1,1024]{1,0:T(1,128)S(1)} %get-tuple-element.19.row_ref, f32[1,1024]{1,0:T(1,128)S(1)} %get-tuple-element.20.sign_ref, f32[16384,128]{1,0:T(8,128)S(1)} %pair.1.table_ref), custom_call_target="tpu_custom_call" | custom-call | flops 1024 | bytes 1024 | tf_op jit(solution)/shard_map/pick/pallas_call | solution.py:186
  28.2 2.8 %collective-permute-done.2.refs_0_ = f32[1024,128]{1,0:T(8,128)S(1)} collective-permute-done((f32[1024,128]{1,0:T(8,128)S(1)}, f32[1024,128]{1,0:T(8,128)S(1)}, u32[]{:S(2)}, u32[]{:S(2)}) %collective-permute-start.2) | collective-permute-done | bytes 524320 | tf_op jit(solution)/shard_map/ppermute | solution.py:274
  31.1 2.2 %collective-permute-start.3 = (f32[512,128]{1,0:T(8,128)S(1)}, f32[512,128]{1,0:T(8,128)S(1)}, u32[]{:S(2)}, u32[]{:S(2)}) collective-permute-start(f32[512,128]{1,0:T(8,128)S(1)} %slice.97), channel_id=1, source_target_pairs={{0,8},{8,0},{16,24},{24,16},{1,9},{9,1},{17,25},{25,17},{2,10},{10... | collective-permute-start | bytes 786440 | tf_op jit(solution)/shard_map/ppermute | solution.py:275
  33.3 1.9 %pick.10 = f32[1024,128]{1,0:T(8,128)S(1)} custom-call(s32[1,1024]{1,0:T(1,128)S(1)} %get-tuple-element.24.row_ref, f32[1,1024]{1,0:T(1,128)S(1)} %get-tuple-element.25.sign_ref, f32[16384,128]{1,0:T(8,128)S(1)} %pair.1.table_ref), custom_call_target="tpu_custom_call" | custom-call | flops 1024 | bytes 1024 | tf_op jit(solution)/shard_map/pick/pallas_call | solution.py:186
  36.8 1.9 %pick.12 = f32[1024,128]{1,0:T(8,128)S(1)} custom-call(s32[1,1024]{1,0:T(1,128)S(1)} %get-tuple-element.28.row_ref, f32[1,1024]{1,0:T(1,128)S(1)} %get-tuple-element.29.sign_ref, f32[16384,128]{1,0:T(8,128)S(1)} %pair.1.table_ref, f32[1024,128]{1,0:T(8,128)S(1)} %collective-permute-done.2.refs_0_), custom_call_target="tpu_custom_call" | custom-call | flops 1024 | bytes 1024 | tf_op jit(solution)/shard_map/pick/pallas_call | solution.py:186
  38.7 3.0 %collective-permute-done.10 = f32[1024,128]{1,0:T(8,128)S(1)} collective-permute-done((f32[1024,128]{1,0:T(8,128)S(1)}, f32[1024,128]{1,0:T(8,128)S(1)}, u32[]{:S(2)}, u32[]{:S(2)}) %collective-permute-start.10) | collective-permute-done | bytes 524320 | tf_op jit(solution)/shard_map/ppermute | solution.py:274
  41.8 1.8 %collective-permute-start.11 = (f32[512,128]{1,0:T(8,128)S(1)}, f32[512,128]{1,0:T(8,128)S(1)}, u32[]{:S(2)}, u32[]{:S(2)}) collective-permute-start(f32[512,128]{1,0:T(8,128)S(1)} %slice.109), channel_id=1, source_target_pairs={{0,4},{1,5},{2,6},{3,7},{4,0},{5,1},{6,2},{7,3},{8,12},{9,13},{10,... | collective-permute-start | bytes 786440 | tf_op jit(solution)/shard_map/ppermute | solution.py:274
  43.7 1.9 %pick.14 = f32[1024,128]{1,0:T(8,128)S(1)} custom-call(s32[1,1024]{1,0:T(1,128)S(1)} %get-tuple-element.32.row_ref, f32[1,1024]{1,0:T(1,128)S(1)} %get-tuple-element.33.sign_ref, f32[16384,128]{1,0:T(8,128)S(1)} %pair.1.table_ref, f32[1024,128]{1,0:T(8,128)S(1)} %collective-permute-done.6.refs_0_), custom_call_target="tpu_custom_call" | custom-call | flops 1024 | bytes 1024 | tf_op jit(solution)/shard_map/pick/pallas_call | solution.py:186
  48.2 2.1 %collective-permute-start.8 = (f32[256,128]{1,0:T(8,128)S(1)}, f32[256,128]{1,0:T(8,128)S(1)}, u32[]{:S(2)}, u32[]{:S(2)}) collective-permute-start(f32[256,128]{1,0:T(8,128)S(1)} %slice.105), channel_id=1, source_target_pairs={{0,2},{1,3},{2,0},{3,1},{4,6},{5,7},{6,4},{7,5},{8,10},{9,11},{10,... | collective-permute-start | bytes 393224 | tf_op jit(solution)/shard_map/ppermute | solution.py:274
  56.1 2.7 %collective-permute-start.5 = (f32[128,128]{1,0:T(8,128)S(1)}, f32[128,128]{1,0:T(8,128)S(1)}, u32[]{:S(2)}, u32[]{:S(2)}) collective-permute-start(f32[128,128]{1,0:T(8,128)S(1)} %slice.101), channel_id=1, source_target_pairs={{0,16},{8,24},{16,0},{24,8},{1,17},{9,25},{17,1},{25,9},{2,18},{10... | collective-permute-start | bytes 196616 | tf_op jit(solution)/shard_map/ppermute | solution.py:275
  59.2 2.7 %collective-permute-start.13 = (f32[128,128]{1,0:T(8,128)S(1)}, f32[128,128]{1,0:T(8,128)S(1)}, u32[]{:S(2)}, u32[]{:S(2)}) collective-permute-start(f32[128,128]{1,0:T(8,128)S(1)} %slice.113), channel_id=1, source_target_pairs={{0,16},{8,24},{16,0},{24,8},{1,17},{9,25},{17,1},{25,9},{2,18},{10... | collective-permute-start | bytes 196616 | tf_op jit(solution)/shard_map/ppermute | solution.py:275
  63.2 2.3 %collective-permute-done.5 = f32[128,128]{1,0:T(8,128)S(1)} collective-permute-done((f32[128,128]{1,0:T(8,128)S(1)}, f32[128,128]{1,0:T(8,128)S(1)}, u32[]{:S(2)}, u32[]{:S(2)}) %collective-permute-start.5) | collective-permute-done | bytes 65568 | tf_op jit(solution)/shard_map/ppermute | solution.py:275
  72.0 2.7 %collective-permute-done.19 = f32[128,128]{1,0:T(8,128)S(1)} collective-permute-done((f32[128,128]{1,0:T(8,128)S(1)}, f32[128,128]{1,0:T(8,128)S(1)}, u32[]{:S(2)}, u32[]{:S(2)}) %collective-permute-start.19) | collective-permute-done | bytes 65568 | tf_op jit(solution)/shard_map/ppermute | solution.py:274
  76.3 2.7 %collective-permute-done.20 = f32[128,128]{1,0:T(8,128)S(1)} collective-permute-done((f32[128,128]{1,0:T(8,128)S(1)}, f32[128,128]{1,0:T(8,128)S(1)}, u32[]{:S(2)}, u32[]{:S(2)}) %collective-permute-start.20) | collective-permute-done | bytes 65568 | tf_op jit(solution)/shard_map/ppermute | solution.py:274
  79.2 4.3 %collective-permute-done.21 = f32[128,128]{1,0:T(8,128)S(1)} collective-permute-done((f32[128,128]{1,0:T(8,128)S(1)}, f32[128,128]{1,0:T(8,128)S(1)}, u32[]{:S(2)}, u32[]{:S(2)}) %collective-permute-start.21) | collective-permute-done | bytes 65568 | tf_op jit(solution)/shard_map/ppermute | solution.py:275
  85.7 3.3 %collective-permute-done.22 = f32[128,128]{1,0:T(8,128)S(1)} collective-permute-done((f32[128,128]{1,0:T(8,128)S(1)}, f32[128,128]{1,0:T(8,128)S(1)}, u32[]{:S(2)}, u32[]{:S(2)}) %collective-permute-start.22) | collective-permute-done | bytes 65568 | tf_op jit(solution)/shard_map/ppermute | solution.py:275
  89.6 8.0 %finish.1 = (f32[512,128]{1,0:T(8,128)}, f32[128,128]{1,0:T(8,128)}) custom-call(f32[128,128]{1,0:T(8,128)} %add.87.gram_ref, f32[512,128]{1,0:T(8,128)} %pad_maximum_fusion.sketch_ref), custom_call_target="tpu_custom_call" | custom-call | tf_op jit(solution)/shard_map/finish/pallas_call | solution.py:399
  (74 shorter events, 28.3 us)
Async XLA Ops:
  0.6 7.7 %collective-permute-start = (f32[8192,128]{1,0:T(8,128)}, f32[8192,128]{1,0:T(8,128)}, u32[]{:S(2)}, u32[]{:S(2)}) collective-permute-start(f32[8192,128]{1,0:T(8,128)} %x_ref.1), channel_id=1, source_target_pairs={{0,1},{1,0},{2,3},{3,2},{4,5},{5,4},{6,7},{7,6},{8,9},{9,8},{10,11... | collective-permute-start | bytes 12582920 | tf_op jit(solution)/shard_map/ppermute | solution.py:274
  1.1 7.1 %collective-permute-start.1 = (s32[8192]{0:T(1024)}, s32[8192]{0:T(1024)S(1)}, u32[]{:S(2)}, u32[]{:S(2)}) collective-permute-start(s32[8192]{0:T(1024)} %param.5), channel_id=1, source_target_pairs={{0,1},{1,0},{2,3},{3,2},{4,5},{5,4},{6,7},{7,6},{8,9},{9,8},{10,11... | collective-permute-start | bytes 98312 | tf_op jit(solution)/shard_map/ppermute | solution.py:274
  1.2 0.8 copy-start
  15.3 15.6 %collective-permute-start.2 = (f32[1024,128]{1,0:T(8,128)S(1)}, f32[1024,128]{1,0:T(8,128)S(1)}, u32[]{:S(2)}, u32[]{:S(2)}) collective-permute-start(f32[1024,128]{1,0:T(8,128)S(1)} %pick.9), channel_id=1, source_target_pairs={{0,2},{1,3},{2,0},{3,1},{4,6},{5,7},{6,4},{7,5},{8,10},{9,11},{10,... | collective-permute-start | bytes 1572872 | tf_op jit(solution)/shard_map/ppermute | solution.py:274
  20.2 15.0 %collective-permute-start.6 = (f32[1024,128]{1,0:T(8,128)S(1)}, f32[1024,128]{1,0:T(8,128)S(1)}, u32[]{:S(2)}, u32[]{:S(2)}) collective-permute-start(f32[1024,128]{1,0:T(8,128)S(1)} %pick.11), channel_id=1, source_target_pairs={{0,4},{1,5},{2,6},{3,7},{4,0},{5,1},{6,2},{7,3},{8,12},{9,13},{10,... | collective-permute-start | bytes 1572872 | tf_op jit(solution)/shard_map/ppermute | solution.py:274
  23.7 18.0 %collective-permute-start.10 = (f32[1024,128]{1,0:T(8,128)S(1)}, f32[1024,128]{1,0:T(8,128)S(1)}, u32[]{:S(2)}, u32[]{:S(2)}) collective-permute-start(f32[1024,128]{1,0:T(8,128)S(1)} %pick.13), channel_id=1, source_target_pairs={{0,2},{1,3},{2,0},{3,1},{4,6},{5,7},{6,4},{7,5},{8,10},{9,11},{10,... | collective-permute-start | bytes 1572872 | tf_op jit(solution)/shard_map/ppermute | solution.py:274
  26.2 20.0 %collective-permute-start.14 = (f32[1024,128]{1,0:T(8,128)S(1)}, f32[1024,128]{1,0:T(8,128)S(1)}, u32[]{:S(2)}, u32[]{:S(2)}) collective-permute-start(f32[1024,128]{1,0:T(8,128)S(1)} %pick.15), channel_id=1, source_target_pairs={{0,4},{1,5},{2,6},{3,7},{4,0},{5,1},{6,2},{7,3},{8,12},{9,13},{10,... | collective-permute-start | bytes 1572872 | tf_op jit(solution)/shard_map/ppermute | solution.py:274
  31.1 16.2 %collective-permute-start.3 = (f32[512,128]{1,0:T(8,128)S(1)}, f32[512,128]{1,0:T(8,128)S(1)}, u32[]{:S(2)}, u32[]{:S(2)}) collective-permute-start(f32[512,128]{1,0:T(8,128)S(1)} %slice.97), channel_id=1, source_target_pairs={{0,8},{8,0},{16,24},{24,16},{1,9},{9,1},{17,25},{25,17},{2,10},{10... | collective-permute-start | bytes 786440 | tf_op jit(solution)/shard_map/ppermute | solution.py:275
  35.3 12.8 %collective-permute-start.7 = (f32[512,128]{1,0:T(8,128)S(1)}, f32[512,128]{1,0:T(8,128)S(1)}, u32[]{:S(2)}, u32[]{:S(2)}) collective-permute-start(f32[512,128]{1,0:T(8,128)S(1)} %slice.103), channel_id=1, source_target_pairs={{0,8},{8,0},{16,24},{24,16},{1,9},{9,1},{17,25},{25,17},{2,10},{10... | collective-permute-start | bytes 786440 | tf_op jit(solution)/shard_map/ppermute | solution.py:275
  41.8 10.0 %collective-permute-start.11 = (f32[512,128]{1,0:T(8,128)S(1)}, f32[512,128]{1,0:T(8,128)S(1)}, u32[]{:S(2)}, u32[]{:S(2)}) collective-permute-start(f32[512,128]{1,0:T(8,128)S(1)} %slice.109), channel_id=1, source_target_pairs={{0,4},{1,5},{2,6},{3,7},{4,0},{5,1},{6,2},{7,3},{8,12},{9,13},{10,... | collective-permute-start | bytes 786440 | tf_op jit(solution)/shard_map/ppermute | solution.py:274
  46.3 8.1 %collective-permute-start.15 = (f32[512,128]{1,0:T(8,128)S(1)}, f32[512,128]{1,0:T(8,128)S(1)}, u32[]{:S(2)}, u32[]{:S(2)}) collective-permute-start(f32[512,128]{1,0:T(8,128)S(1)} %slice.115), channel_id=1, source_target_pairs={{0,2},{1,3},{2,0},{3,1},{4,6},{5,7},{6,4},{7,5},{8,10},{9,11},{10,... | collective-permute-start | bytes 786440 | tf_op jit(solution)/shard_map/ppermute | solution.py:274
  47.3 8.8 %collective-permute-start.4 = (f32[256,128]{1,0:T(8,128)S(1)}, f32[256,128]{1,0:T(8,128)S(1)}, u32[]{:S(2)}, u32[]{:S(2)}) collective-permute-start(f32[256,128]{1,0:T(8,128)S(1)} %slice.99), channel_id=1, source_target_pairs={{0,4},{1,5},{2,6},{3,7},{4,0},{5,1},{6,2},{7,3},{8,12},{9,13},{10,... | collective-permute-start | bytes 393224 | tf_op jit(solution)/shard_map/ppermute | solution.py:274
  48.2 10.6 %collective-permute-start.8 = (f32[256,128]{1,0:T(8,128)S(1)}, f32[256,128]{1,0:T(8,128)S(1)}, u32[]{:S(2)}, u32[]{:S(2)}) collective-permute-start(f32[256,128]{1,0:T(8,128)S(1)} %slice.105), channel_id=1, source_target_pairs={{0,2},{1,3},{2,0},{3,1},{4,6},{5,7},{6,4},{7,5},{8,10},{9,11},{10,... | collective-permute-start | bytes 393224 | tf_op jit(solution)/shard_map/ppermute | solution.py:274
  51.8 7.4 %collective-permute-start.12 = (f32[256,128]{1,0:T(8,128)S(1)}, f32[256,128]{1,0:T(8,128)S(1)}, u32[]{:S(2)}, u32[]{:S(2)}) collective-permute-start(f32[256,128]{1,0:T(8,128)S(1)} %slice.111), channel_id=1, source_target_pairs={{0,8},{8,0},{16,24},{24,16},{1,9},{9,1},{17,25},{25,17},{2,10},{10... | collective-permute-start | bytes 393224 | tf_op jit(solution)/shard_map/ppermute | solution.py:275
  54.4 7.5 %collective-permute-start.16 = (f32[256,128]{1,0:T(8,128)S(1)}, f32[256,128]{1,0:T(8,128)S(1)}, u32[]{:S(2)}, u32[]{:S(2)}) collective-permute-start(f32[256,128]{1,0:T(8,128)S(1)} %slice.117), channel_id=1, source_target_pairs={{0,8},{8,0},{16,24},{24,16},{1,9},{9,1},{17,25},{25,17},{2,10},{10... | collective-permute-start | bytes 393224 | tf_op jit(solution)/shard_map/ppermute | solution.py:275
  56.1 9.4 %collective-permute-start.5 = (f32[128,128]{1,0:T(8,128)S(1)}, f32[128,128]{1,0:T(8,128)S(1)}, u32[]{:S(2)}, u32[]{:S(2)}) collective-permute-start(f32[128,128]{1,0:T(8,128)S(1)} %slice.101), channel_id=1, source_target_pairs={{0,16},{8,24},{16,0},{24,8},{1,17},{9,25},{17,1},{25,9},{2,18},{10... | collective-permute-start | bytes 196616 | tf_op jit(solution)/shard_map/ppermute | solution.py:275
  58.8 7.5 %collective-permute-start.9 = (f32[128,128]{1,0:T(8,128)S(1)}, f32[128,128]{1,0:T(8,128)S(1)}, u32[]{:S(2)}, u32[]{:S(2)}) collective-permute-start(f32[128,128]{1,0:T(8,128)S(1)} %slice.107), channel_id=1, source_target_pairs={{0,16},{8,24},{16,0},{24,8},{1,17},{9,25},{17,1},{25,9},{2,18},{10... | collective-permute-start | bytes 196616 | tf_op jit(solution)/shard_map/ppermute | solution.py:275
  59.2 8.5 %collective-permute-start.13 = (f32[128,128]{1,0:T(8,128)S(1)}, f32[128,128]{1,0:T(8,128)S(1)}, u32[]{:S(2)}, u32[]{:S(2)}) collective-permute-start(f32[128,128]{1,0:T(8,128)S(1)} %slice.113), channel_id=1, source_target_pairs={{0,16},{8,24},{16,0},{24,8},{1,17},{9,25},{17,1},{25,9},{2,18},{10... | collective-permute-start | bytes 196616 | tf_op jit(solution)/shard_map/ppermute | solution.py:275
  61.9 6.5 %collective-permute-start.17 = (f32[128,128]{1,0:T(8,128)S(1)}, f32[128,128]{1,0:T(8,128)S(1)}, u32[]{:S(2)}, u32[]{:S(2)}) collective-permute-start(f32[128,128]{1,0:T(8,128)S(1)} %slice.119), channel_id=1, source_target_pairs={{0,16},{8,24},{16,0},{24,8},{1,17},{9,25},{17,1},{25,9},{2,18},{10... | collective-permute-start | bytes 196616 | tf_op jit(solution)/shard_map/ppermute | solution.py:275
  69.1 1.3 %collective-permute-start.18 = (f32[128,128]{1,0:T(8,128)S(1)}, f32[128,128]{1,0:T(8,128)S(1)}, u32[]{:S(2)}, u32[]{:S(2)}) collective-permute-start(f32[128,128]{1,0:T(8,128)S(1)} %convolution_multiply_fusion), channel_id=1, source_target_pairs={{0,1},{1,0},{2,3},{3,2},{4,5},{5,4},{6,7},{7,6},{8,9},{9,8},{10,11... | collective-permute-start | bytes 196616 | tf_op jit(solution)/shard_map/ppermute | solution.py:274
  70.4 4.3 %collective-permute-start.19 = (f32[128,128]{1,0:T(8,128)S(1)}, f32[128,128]{1,0:T(8,128)S(1)}, u32[]{:S(2)}, u32[]{:S(2)}) collective-permute-start(f32[128,128]{1,0:T(8,128)S(1)} %add.83), channel_id=1, source_target_pairs={{0,2},{1,3},{2,0},{3,1},{4,6},{5,7},{6,4},{7,5},{8,10},{9,11},{10,... | collective-permute-start | bytes 196616 | tf_op jit(solution)/shard_map/ppermute | solution.py:274
  74.8 4.3 %collective-permute-start.20 = (f32[128,128]{1,0:T(8,128)S(1)}, f32[128,128]{1,0:T(8,128)S(1)}, u32[]{:S(2)}, u32[]{:S(2)}) collective-permute-start(f32[128,128]{1,0:T(8,128)S(1)} %add.84), channel_id=1, source_target_pairs={{0,4},{1,5},{2,6},{3,7},{4,0},{5,1},{6,2},{7,3},{8,12},{9,13},{10,... | collective-permute-start | bytes 196616 | tf_op jit(solution)/shard_map/ppermute | solution.py:274
  79.1 4.3 %collective-permute-start.21 = (f32[128,128]{1,0:T(8,128)S(1)}, f32[128,128]{1,0:T(8,128)S(1)}, u32[]{:S(2)}, u32[]{:S(2)}) collective-permute-start(f32[128,128]{1,0:T(8,128)S(1)} %add.85), channel_id=1, source_target_pairs={{0,8},{8,0},{16,24},{24,16},{1,9},{9,1},{17,25},{25,17},{2,10},{10... | collective-permute-start | bytes 196616 | tf_op jit(solution)/shard_map/ppermute | solution.py:275
  83.5 5.5 %collective-permute-start.22 = (f32[128,128]{1,0:T(8,128)S(1)}, f32[128,128]{1,0:T(8,128)S(1)}, u32[]{:S(2)}, u32[]{:S(2)}) collective-permute-start(f32[128,128]{1,0:T(8,128)S(1)} %add.86), channel_id=1, source_target_pairs={{0,16},{8,24},{16,0},{24,8},{1,17},{9,25},{17,1},{25,9},{2,18},{10... | collective-permute-start | bytes 196616 | tf_op jit(solution)/shard_map/ppermute | solution.py:275
  (2 other events, 1.6 us)

commit v4 on v3

--- a/solution.py
+++ b/solution.py
@@ -196,41 +196,64 @@
     )(rows, signs, pltpu.with_memory_space_constraint(table, pltpu.VMEM), *after)
 
 
-def factor_panel(left, right, at):
+def factor_panel(left, right, next_left, next_right, at):
     shape = left.shape
     rows = lax.broadcasted_iota(I32, shape, 0)
-    column = [jnp.broadcast_to(left[:, at + i : at + i + 1], shape) for i in range(SUB)]
+
+    def lane(x, i):
+        return jnp.broadcast_to(x[:, at + i : at + i + 1], shape)
+
+    def row(x, i):
+        return jnp.broadcast_to(x[i : i + 1, :], shape)
+
+    more = next_left is not None
+    column = [lane(left, i) for i in range(SUB)]
+    below = [lane(next_left, i) for i in range(SUB)] if more else []
     pivots = jnp.ones_like(left)
     for i in range(SUB):
-        pivot = jnp.broadcast_to(column[i][i : i + 1, :], shape)
+        pivot = row(column[i], i)
         pivots = jnp.where(rows == i, pivot, pivots)
+        inverse = 1.0 / pivot
+        ratio = jnp.where(rows > i, column[i], 0.0) * inverse
+        if more:
+            next_ratio = below[i] * inverse
+        for j in range(i + 1, SUB):
+            top = row(column[j], i)
+            column[j] = column[j] - ratio * top
+            if more:
+                below[j] = below[j] - next_ratio * top
+        top, unit = row(left, i), row(right, i)
+        if more:
+            next_left = next_left - next_ratio * top
+            next_right = next_right - next_ratio * unit
         if i < SUB - 1:
-            ratio = jnp.where(rows > i, column[i] * (1.0 / pivot), 0.0)
-            for j in range(i + 1, SUB):
-                column[j] = column[j] - ratio * jnp.broadcast_to(column[j][i : i + 1, :], shape)
-            left = left - ratio * jnp.broadcast_to(left[i : i + 1, :], shape)
-            right = right - ratio * jnp.broadcast_to(right[i : i + 1, :], shape)
+            left = left - ratio * top
+            right = right - ratio * unit
     scale = lax.rsqrt(pivots)
-    return left * scale, right * scale
+    return left * scale, right * scale, next_left, next_right
 
 
 def factor(gram):
     n = gram.shape[0]
-    rest = gram
     unit = (
         lax.broadcasted_iota(I32, (n, n), 0) == lax.broadcasted_iota(I32, (n, n), 1)
     ).astype(F32)
     lanes = lax.broadcasted_iota(I32, (SUB, n), 1)
     panel_rows = lax.broadcasted_iota(I32, (SUB, n), 0)
+    left, right = gram[:SUB], unit[:SUB]
+    rest, unit = gram[SUB:], unit[SUB:]
     uppers, inverses = [], []
     for at in range(0, n, SUB):
-        left, right = factor_panel(rest[:SUB], unit[:SUB], at)
-        left = jnp.where(lanes >= panel_rows + at, left, 0.0)
-        uppers.append(left)
-        inverses.append(right)
-        if at + SUB < n:
-            h, m, l = split3(left)
-            uh, um, ul = split3(right)
+        more = at + SUB < n
+        next_left, next_right = (rest[:SUB], unit[:SUB]) if more else (None, None)
+        done_left, done_right, left, right = factor_panel(left, right, next_left, next_right, at)
+        done_left = jnp.where(lanes >= panel_rows + at, done_left, 0.0)
+        uppers.append(done_left)
+        inverses.append(done_right)
+        rest, unit = rest[SUB:], unit[SUB:]
+        if at + 2 * SUB < n:
+            h, m, l = split3(done_left)
+            uh, um, ul = split3(done_right)
             terms = jnp.concatenate([h, h, m, h, l, m], 0)
             others = jnp.concatenate(
                 [
@@ -239,9 +262,9 @@
                 ],
                 1,
             )
-            change = jnp.dot(terms.T[at + SUB :], others, preferred_element_type=F32)
-            rest = rest[SUB:] - change[:, :n]
-            unit = unit[SUB:] - change[:, n:]
+            change = jnp.dot(terms.T[at + 2 * SUB :], others, preferred_element_type=F32)
+            rest = rest - change[:, :n]
+            unit = unit - change[:, n:]
     return jnp.concatenate(uppers, 0), jnp.concatenate(inverses, 0)
 
 
@@ -393,8 +416,13 @@
         precision=lax.Precision.HIGHEST,
         preferred_element_type=F32,
     ) / total
-    for bit in range(bits):
-        gram = gram + swap(gram, 1 << bit)
+    groups = [(0,)] + [tuple(range(b, min(b + 2, inner_bits))) for b in range(1, inner_bits, 2)]
+    for group in groups + [(bit,) for bit in outer]:
+        near = gram + swap(gram, 1 << group[0])
+        if len(group) == 2:
+            far = 1 << group[1]
+            near = near + (swap(gram, far) + swap(gram, far | 1 << group[0]))
+        gram = near
 
     return pl.pallas_call(
         finish_kernel,

time: 97.8 us -> 94.6 us (0.967)
  Pallas kernels: 32.9 us -> 31.1 us
  waiting for transfers between devices: 28.2 us -> 27.1 us
    pallas_call x1, Pallas kernels: 7.98 us -> 6.15 us  [per_device(): pl.pallas_call(finish_kernel, out_shape=(jax.ShapeDtypeStruct((own_count,...]
    ppermute x13 -> x14, waiting for transfers between devices: 15.5 us -> 13.9 us  [swap(): return lax.ppermute(value, 'exb', bit_perm(n_inner, mask))]
    ppermute x13 -> x14, starting transfers between devices: 14.8 us -> 15.1 us  [swap(): return lax.ppermute(value, 'exb', bit_perm(n_inner, mask))]
  transfers between devices with their start and end apart: 23 -> 24, of which waited for: 15 -> 16; matrix products, arithmetic and copies ran while one was open for 1% -> 1% of each run, Pallas kernels for 18% -> 19%
where the time goes in v4:
time: 94.6 us; the launch traced here: 94.3 us
  Pallas kernels  31.1 us (33%)
  starting transfers between devices  30.2 us (32%)
  waiting for transfers between devices  27.1 us (29%)
  local copies, waits for them, and re-layouts  2.58 us (3%)
  other arithmetic  1.83 us (2%)
    pallas_call x8, Pallas kernels, pick(): pl.pallas_call(pick_kernel, out_shape=jax.ShapeDtypeStruct((count, table....  15.3 us
    ppermute x14, starting transfers between devices, swap(): return lax.ppermute(value, 'exb', bit_perm(n_inner, mask))  15.1 us
    ppermute x10, starting transfers between devices, swap(): return lax.ppermute(value, 'exa', bit_perm(n_outer, mask // n_inner))  15.1 us
    ppermute x14, waiting for transfers between devices, swap(): return lax.ppermute(value, 'exb', bit_perm(n_inner, mask))  13.9 us
    ppermute x10, waiting for transfers between devices, swap(): return lax.ppermute(value, 'exa', bit_perm(n_outer, mask // n_inner))  13.2 us
    pallas_call x1, Pallas kernels, per_device(): pl.pallas_call(finish_kernel, out_shape=(jax.ShapeDtypeStruct((own_count,...  6.15 us
    pallas_call x1, Pallas kernels, per_device(): pl.pallas_call(pair_kernel, out_shape=jax.ShapeDtypeStruct((2 * rows_dev,...  5.1 us
    pallas_call x1, Pallas kernels, per_device(): pl.pallas_call(functools.partial(own_kernel, 1.0 / math.sqrt(rows_dev * n...  4.57 us
  transfers between devices with their start and end apart: 24, of which 16 were waited for; matrix products, arithmetic and copies ran while one was open for 1% of the time, Pallas kernels for 19%

profile of v4, /device:TPU:0, one launch (start us, length us, event | category | flops | bytes accessed | tf_op | source)
XLA Modules:
  0.0 94.3 jit_solution(17611393049437778629)
XLA Ops:
  3.7 4.6 %own.1 = (f32[8192,128]{1,0:T(8,128)S(1)}, s32[1,1024]{1,0:T(1,128)S(1)}, f32[1,1024]{1,0:T(1,128)S(1)}, s32[1,1024]{1,0:T(1,128)S(1)}, f32[1,1024]{1,0:T(1,128)...) custom-call(f32[8192,128]{1,0:T(8,128)} %x_ref.1, ...), custom_call_target="tpu_custom_call" | custom-call | flops 10000000 | bytes 12582912 | tf_op jit(solution)/shard_map/own/pallas_call | solution.py:349
  8.3 5.1 %pair.1.table_ref = f32[16384,128]{1,0:T(8,128)S(1)} custom-call(f32[8192,128]{1,0:T(8,128)} %collective-permute-done.x_ref, s32[64,128]{1,0:T(8,128)S(1)} %bitcast.8, f32[8192,128]{1,0:T(8,128)S(1)} %get-tuple-element.21.own_ref), custom_call_target="tpu_custom_call" | custom-call | flops 10000000 | bytes 16777216 | tf_op jit(solution)/shard_map/pair/pallas_call | solution.py:371
  13.4 1.9 %pick.9 = f32[1024,128]{1,0:T(8,128)S(1)} custom-call(s32[1,1024]{1,0:T(1,128)S(1)} %get-tuple-element.22.row_ref, f32[1,1024]{1,0:T(1,128)S(1)} %get-tuple-element.23.sign_ref, f32[16384,128]{1,0:T(8,128)S(1)} %pair.1.table_ref), custom_call_target="tpu_custom_call" | custom-call | flops 1024 | bytes 1024 | tf_op jit(solution)/shard_map/pick/pallas_call | solution.py:186
  15.3 2.9 %collective-permute-start.2 = (f32[1024,128]{1,0:T(8,128)S(1)}, f32[1024,128]{1,0:T(8,128)S(1)}, u32[]{:S(2)}, u32[]{:S(2)}) collective-permute-start(f32[1024,128]{1,0:T(8,128)S(1)} %pick.9), channel_id=1, source_target_pairs={{0,2},{1,3},{2,0},{3,1},{4,6},{5,7},{6,4},{7,5},{8,10},{9,11},{10,... | collective-permute-start | bytes 1572872 | tf_op jit(solution)/shard_map/ppermute | solution.py:297
  18.3 1.9 %pick.11 = f32[1024,128]{1,0:T(8,128)S(1)} custom-call(s32[1,1024]{1,0:T(1,128)S(1)} %get-tuple-element.26.row_ref, f32[1,1024]{1,0:T(1,128)S(1)} %get-tuple-element.27.sign_ref, f32[16384,128]{1,0:T(8,128)S(1)} %pair.1.table_ref), custom_call_target="tpu_custom_call" | custom-call | flops 1024 | bytes 1024 | tf_op jit(solution)/shard_map/pick/pallas_call | solution.py:186
  21.8 1.9 %pick.13 = f32[1024,128]{1,0:T(8,128)S(1)} custom-call(s32[1,1024]{1,0:T(1,128)S(1)} %get-tuple-element.30.row_ref, f32[1,1024]{1,0:T(1,128)S(1)} %get-tuple-element.31.sign_ref, f32[16384,128]{1,0:T(8,128)S(1)} %pair.1.table_ref), custom_call_target="tpu_custom_call" | custom-call | flops 1024 | bytes 1024 | tf_op jit(solution)/shard_map/pick/pallas_call | solution.py:186
  24.3 1.9 %pick.15 = f32[1024,128]{1,0:T(8,128)S(1)} custom-call(s32[1,1024]{1,0:T(1,128)S(1)} %get-tuple-element.34.row_ref, f32[1,1024]{1,0:T(1,128)S(1)} %get-tuple-element.35.sign_ref, f32[16384,128]{1,0:T(8,128)S(1)} %pair.1.table_ref), custom_call_target="tpu_custom_call" | custom-call | flops 1024 | bytes 1024 | tf_op jit(solution)/shard_map/pick/pallas_call | solution.py:186
  26.3 1.9 %pick.8 = f32[1024,128]{1,0:T(8,128)S(1)} custom-call(s32[1,1024]{1,0:T(1,128)S(1)} %get-tuple-element.19.row_ref, f32[1,1024]{1,0:T(1,128)S(1)} %get-tuple-element.20.sign_ref, f32[16384,128]{1,0:T(8,128)S(1)} %pair.1.table_ref), custom_call_target="tpu_custom_call" | custom-call | flops 1024 | bytes 1024 | tf_op jit(solution)/shard_map/pick/pallas_call | solution.py:186
  28.2 2.8 %collective-permute-done.2.refs_0_ = f32[1024,128]{1,0:T(8,128)S(1)} collective-permute-done((f32[1024,128]{1,0:T(8,128)S(1)}, f32[1024,128]{1,0:T(8,128)S(1)}, u32[]{:S(2)}, u32[]{:S(2)}) %collective-permute-start.2) | collective-permute-done | bytes 524320 | tf_op jit(solution)/shard_map/ppermute | solution.py:297
  31.1 2.2 %collective-permute-start.3 = (f32[512,128]{1,0:T(8,128)S(1)}, f32[512,128]{1,0:T(8,128)S(1)}, u32[]{:S(2)}, u32[]{:S(2)}) collective-permute-start(f32[512,128]{1,0:T(8,128)S(1)} %slice.97), channel_id=1, source_target_pairs={{0,8},{8,0},{16,24},{24,16},{1,9},{9,1},{17,25},{25,17},{2,10},{10... | collective-permute-start | bytes 786440 | tf_op jit(solution)/shard_map/ppermute | solution.py:298
  33.3 1.9 %pick.10 = f32[1024,128]{1,0:T(8,128)S(1)} custom-call(s32[1,1024]{1,0:T(1,128)S(1)} %get-tuple-element.24.row_ref, f32[1,1024]{1,0:T(1,128)S(1)} %get-tuple-element.25.sign_ref, f32[16384,128]{1,0:T(8,128)S(1)} %pair.1.table_ref), custom_call_target="tpu_custom_call" | custom-call | flops 1024 | bytes 1024 | tf_op jit(solution)/shard_map/pick/pallas_call | solution.py:186
  36.8 1.9 %pick.12 = f32[1024,128]{1,0:T(8,128)S(1)} custom-call(s32[1,1024]{1,0:T(1,128)S(1)} %get-tuple-element.28.row_ref, f32[1,1024]{1,0:T(1,128)S(1)} %get-tuple-element.29.sign_ref, f32[16384,128]{1,0:T(8,128)S(1)} %pair.1.table_ref, f32[1024,128]{1,0:T(8,128)S(1)} %collective-permute-done.2.refs_0_), custom_call_target="tpu_custom_call" | custom-call | flops 1024 | bytes 1024 | tf_op jit(solution)/shard_map/pick/pallas_call | solution.py:186
  38.7 3.0 %collective-permute-done.10 = f32[1024,128]{1,0:T(8,128)S(1)} collective-permute-done((f32[1024,128]{1,0:T(8,128)S(1)}, f32[1024,128]{1,0:T(8,128)S(1)}, u32[]{:S(2)}, u32[]{:S(2)}) %collective-permute-start.10) | collective-permute-done | bytes 524320 | tf_op jit(solution)/shard_map/ppermute | solution.py:297
  41.8 1.8 %collective-permute-start.11 = (f32[512,128]{1,0:T(8,128)S(1)}, f32[512,128]{1,0:T(8,128)S(1)}, u32[]{:S(2)}, u32[]{:S(2)}) collective-permute-start(f32[512,128]{1,0:T(8,128)S(1)} %slice.109), channel_id=1, source_target_pairs={{0,4},{1,5},{2,6},{3,7},{4,0},{5,1},{6,2},{7,3},{8,12},{9,13},{10,... | collective-permute-start | bytes 786440 | tf_op jit(solution)/shard_map/ppermute | solution.py:297
  43.7 1.9 %pick.14 = f32[1024,128]{1,0:T(8,128)S(1)} custom-call(s32[1,1024]{1,0:T(1,128)S(1)} %get-tuple-element.32.row_ref, f32[1,1024]{1,0:T(1,128)S(1)} %get-tuple-element.33.sign_ref, f32[16384,128]{1,0:T(8,128)S(1)} %pair.1.table_ref, f32[1024,128]{1,0:T(8,128)S(1)} %collective-permute-done.6.refs_0_), custom_call_target="tpu_custom_call" | custom-call | flops 1024 | bytes 1024 | tf_op jit(solution)/shard_map/pick/pallas_call | solution.py:186
  48.2 2.1 %collective-permute-start.8 = (f32[256,128]{1,0:T(8,128)S(1)}, f32[256,128]{1,0:T(8,128)S(1)}, u32[]{:S(2)}, u32[]{:S(2)}) collective-permute-start(f32[256,128]{1,0:T(8,128)S(1)} %slice.105), channel_id=1, source_target_pairs={{0,2},{1,3},{2,0},{3,1},{4,6},{5,7},{6,4},{7,5},{8,10},{9,11},{10,... | collective-permute-start | bytes 393224 | tf_op jit(solution)/shard_map/ppermute | solution.py:297
  51.8 1.8 %collective-permute-start.12 = (f32[256,128]{1,0:T(8,128)S(1)}, f32[256,128]{1,0:T(8,128)S(1)}, u32[]{:S(2)}, u32[]{:S(2)}) collective-permute-start(f32[256,128]{1,0:T(8,128)S(1)} %slice.111), channel_id=1, source_target_pairs={{0,8},{8,0},{16,24},{24,16},{1,9},{9,1},{17,25},{25,17},{2,10},{10... | collective-permute-start | bytes 393224 | tf_op jit(solution)/shard_map/ppermute | solution.py:298
  56.1 2.7 %collective-permute-start.5 = (f32[128,128]{1,0:T(8,128)S(1)}, f32[128,128]{1,0:T(8,128)S(1)}, u32[]{:S(2)}, u32[]{:S(2)}) collective-permute-start(f32[128,128]{1,0:T(8,128)S(1)} %slice.101), channel_id=1, source_target_pairs={{0,16},{8,24},{16,0},{24,8},{1,17},{9,25},{17,1},{25,9},{2,18},{10... | collective-permute-start | bytes 196616 | tf_op jit(solution)/shard_map/ppermute | solution.py:298
  59.2 2.7 %collective-permute-start.13 = (f32[128,128]{1,0:T(8,128)S(1)}, f32[128,128]{1,0:T(8,128)S(1)}, u32[]{:S(2)}, u32[]{:S(2)}) collective-permute-start(f32[128,128]{1,0:T(8,128)S(1)} %slice.113), channel_id=1, source_target_pairs={{0,16},{8,24},{16,0},{24,8},{1,17},{9,25},{17,1},{25,9},{2,18},{10... | collective-permute-start | bytes 196616 | tf_op jit(solution)/shard_map/ppermute | solution.py:298
  63.2 2.3 %collective-permute-done.5 = f32[128,128]{1,0:T(8,128)S(1)} collective-permute-done((f32[128,128]{1,0:T(8,128)S(1)}, f32[128,128]{1,0:T(8,128)S(1)}, u32[]{:S(2)}, u32[]{:S(2)}) %collective-permute-start.5) | collective-permute-done | bytes 65568 | tf_op jit(solution)/shard_map/ppermute | solution.py:298
  74.0 1.8 %collective-permute-done.21 = f32[128,128]{1,0:T(8,128)S(1)} collective-permute-done((f32[128,128]{1,0:T(8,128)S(1)}, f32[128,128]{1,0:T(8,128)S(1)}, u32[]{:S(2)}, u32[]{:S(2)}) %collective-permute-start.21) | collective-permute-done | bytes 65568 | tf_op jit(solution)/shard_map/ppermute | solution.py:297
  77.9 4.3 %collective-permute-done.22 = f32[128,128]{1,0:T(8,128)S(1)} collective-permute-done((f32[128,128]{1,0:T(8,128)S(1)}, f32[128,128]{1,0:T(8,128)S(1)}, u32[]{:S(2)}, u32[]{:S(2)}) %collective-permute-start.22) | collective-permute-done | bytes 65568 | tf_op jit(solution)/shard_map/ppermute | solution.py:298
  83.7 3.8 %collective-permute-done.23 = f32[128,128]{1,0:T(8,128)S(1)} collective-permute-done((f32[128,128]{1,0:T(8,128)S(1)}, f32[128,128]{1,0:T(8,128)S(1)}, u32[]{:S(2)}, u32[]{:S(2)}) %collective-permute-start.23) | collective-permute-done | bytes 65568 | tf_op jit(solution)/shard_map/ppermute | solution.py:298
  88.1 6.1 %finish.1 = (f32[512,128]{1,0:T(8,128)}, f32[128,128]{1,0:T(8,128)}) custom-call(f32[128,128]{1,0:T(8,128)} %add.91.gram_ref, f32[512,128]{1,0:T(8,128)} %pad_maximum_fusion.sketch_ref), custom_call_target="tpu_custom_call" | custom-call | tf_op jit(solution)/shard_map/finish/pallas_call | solution.py:427
  (75 shorter events, 28.3 us)
Async XLA Ops:
  0.6 7.7 %collective-permute-start = (f32[8192,128]{1,0:T(8,128)}, f32[8192,128]{1,0:T(8,128)}, u32[]{:S(2)}, u32[]{:S(2)}) collective-permute-start(f32[8192,128]{1,0:T(8,128)} %x_ref.1), channel_id=1, source_target_pairs={{0,1},{1,0},{2,3},{3,2},{4,5},{5,4},{6,7},{7,6},{8,9},{9,8},{10,11... | collective-permute-start | bytes 12582920 | tf_op jit(solution)/shard_map/ppermute | solution.py:297
  1.1 7.1 %collective-permute-start.1 = (s32[8192]{0:T(1024)}, s32[8192]{0:T(1024)S(1)}, u32[]{:S(2)}, u32[]{:S(2)}) collective-permute-start(s32[8192]{0:T(1024)} %param.5), channel_id=1, source_target_pairs={{0,1},{1,0},{2,3},{3,2},{4,5},{5,4},{6,7},{7,6},{8,9},{9,8},{10,11... | collective-permute-start | bytes 98312 | tf_op jit(solution)/shard_map/ppermute | solution.py:297
  15.3 15.6 %collective-permute-start.2 = (f32[1024,128]{1,0:T(8,128)S(1)}, f32[1024,128]{1,0:T(8,128)S(1)}, u32[]{:S(2)}, u32[]{:S(2)}) collective-permute-start(f32[1024,128]{1,0:T(8,128)S(1)} %pick.9), channel_id=1, source_target_pairs={{0,2},{1,3},{2,0},{3,1},{4,6},{5,7},{6,4},{7,5},{8,10},{9,11},{10,... | collective-permute-start | bytes 1572872 | tf_op jit(solution)/shard_map/ppermute | solution.py:297
  20.2 15.0 %collective-permute-start.6 = (f32[1024,128]{1,0:T(8,128)S(1)}, f32[1024,128]{1,0:T(8,128)S(1)}, u32[]{:S(2)}, u32[]{:S(2)}) collective-permute-start(f32[1024,128]{1,0:T(8,128)S(1)} %pick.11), channel_id=1, source_target_pairs={{0,4},{1,5},{2,6},{3,7},{4,0},{5,1},{6,2},{7,3},{8,12},{9,13},{10,... | collective-permute-start | bytes 1572872 | tf_op jit(solution)/shard_map/ppermute | solution.py:297
  23.7 18.0 %collective-permute-start.10 = (f32[1024,128]{1,0:T(8,128)S(1)}, f32[1024,128]{1,0:T(8,128)S(1)}, u32[]{:S(2)}, u32[]{:S(2)}) collective-permute-start(f32[1024,128]{1,0:T(8,128)S(1)} %pick.13), channel_id=1, source_target_pairs={{0,2},{1,3},{2,0},{3,1},{4,6},{5,7},{6,4},{7,5},{8,10},{9,11},{10,... | collective-permute-start | bytes 1572872 | tf_op jit(solution)/shard_map/ppermute | solution.py:297
  26.2 20.0 %collective-permute-start.14 = (f32[1024,128]{1,0:T(8,128)S(1)}, f32[1024,128]{1,0:T(8,128)S(1)}, u32[]{:S(2)}, u32[]{:S(2)}) collective-permute-start(f32[1024,128]{1,0:T(8,128)S(1)} %pick.15), channel_id=1, source_target_pairs={{0,4},{1,5},{2,6},{3,7},{4,0},{5,1},{6,2},{7,3},{8,12},{9,13},{10,... | collective-permute-start | bytes 1572872 | tf_op jit(solution)/shard_map/ppermute | solution.py:297
  31.1 16.2 %collective-permute-start.3 = (f32[512,128]{1,0:T(8,128)S(1)}, f32[512,128]{1,0:T(8,128)S(1)}, u32[]{:S(2)}, u32[]{:S(2)}) collective-permute-start(f32[512,128]{1,0:T(8,128)S(1)} %slice.97), channel_id=1, source_target_pairs={{0,8},{8,0},{16,24},{24,16},{1,9},{9,1},{17,25},{25,17},{2,10},{10... | collective-permute-start | bytes 786440 | tf_op jit(solution)/shard_map/ppermute | solution.py:298
  35.3 12.8 %collective-permute-start.7 = (f32[512,128]{1,0:T(8,128)S(1)}, f32[512,128]{1,0:T(8,128)S(1)}, u32[]{:S(2)}, u32[]{:S(2)}) collective-permute-start(f32[512,128]{1,0:T(8,128)S(1)} %slice.103), channel_id=1, source_target_pairs={{0,8},{8,0},{16,24},{24,16},{1,9},{9,1},{17,25},{25,17},{2,10},{10... | collective-permute-start | bytes 786440 | tf_op jit(solution)/shard_map/ppermute | solution.py:298
  41.8 10.0 %collective-permute-start.11 = (f32[512,128]{1,0:T(8,128)S(1)}, f32[512,128]{1,0:T(8,128)S(1)}, u32[]{:S(2)}, u32[]{:S(2)}) collective-permute-start(f32[512,128]{1,0:T(8,128)S(1)} %slice.109), channel_id=1, source_target_pairs={{0,4},{1,5},{2,6},{3,7},{4,0},{5,1},{6,2},{7,3},{8,12},{9,13},{10,... | collective-permute-start | bytes 786440 | tf_op jit(solution)/shard_map/ppermute | solution.py:297
  46.3 8.1 %collective-permute-start.15 = (f32[512,128]{1,0:T(8,128)S(1)}, f32[512,128]{1,0:T(8,128)S(1)}, u32[]{:S(2)}, u32[]{:S(2)}) collective-permute-start(f32[512,128]{1,0:T(8,128)S(1)} %slice.115), channel_id=1, source_target_pairs={{0,2},{1,3},{2,0},{3,1},{4,6},{5,7},{6,4},{7,5},{8,10},{9,11},{10,... | collective-permute-start | bytes 786440 | tf_op jit(solution)/shard_map/ppermute | solution.py:297
  47.3 8.8 %collective-permute-start.4 = (f32[256,128]{1,0:T(8,128)S(1)}, f32[256,128]{1,0:T(8,128)S(1)}, u32[]{:S(2)}, u32[]{:S(2)}) collective-permute-start(f32[256,128]{1,0:T(8,128)S(1)} %slice.99), channel_id=1, source_target_pairs={{0,4},{1,5},{2,6},{3,7},{4,0},{5,1},{6,2},{7,3},{8,12},{9,13},{10,... | collective-permute-start | bytes 393224 | tf_op jit(solution)/shard_map/ppermute | solution.py:297
  48.2 10.6 %collective-permute-start.8 = (f32[256,128]{1,0:T(8,128)S(1)}, f32[256,128]{1,0:T(8,128)S(1)}, u32[]{:S(2)}, u32[]{:S(2)}) collective-permute-start(f32[256,128]{1,0:T(8,128)S(1)} %slice.105), channel_id=1, source_target_pairs={{0,2},{1,3},{2,0},{3,1},{4,6},{5,7},{6,4},{7,5},{8,10},{9,11},{10,... | collective-permute-start | bytes 393224 | tf_op jit(solution)/shard_map/ppermute | solution.py:297
  51.8 7.4 %collective-permute-start.12 = (f32[256,128]{1,0:T(8,128)S(1)}, f32[256,128]{1,0:T(8,128)S(1)}, u32[]{:S(2)}, u32[]{:S(2)}) collective-permute-start(f32[256,128]{1,0:T(8,128)S(1)} %slice.111), channel_id=1, source_target_pairs={{0,8},{8,0},{16,24},{24,16},{1,9},{9,1},{17,25},{25,17},{2,10},{10... | collective-permute-start | bytes 393224 | tf_op jit(solution)/shard_map/ppermute | solution.py:298
  54.4 7.5 %collective-permute-start.16 = (f32[256,128]{1,0:T(8,128)S(1)}, f32[256,128]{1,0:T(8,128)S(1)}, u32[]{:S(2)}, u32[]{:S(2)}) collective-permute-start(f32[256,128]{1,0:T(8,128)S(1)} %slice.117), channel_id=1, source_target_pairs={{0,8},{8,0},{16,24},{24,16},{1,9},{9,1},{17,25},{25,17},{2,10},{10... | collective-permute-start | bytes 393224 | tf_op jit(solution)/shard_map/ppermute | solution.py:298
  56.1 9.4 %collective-permute-start.5 = (f32[128,128]{1,0:T(8,128)S(1)}, f32[128,128]{1,0:T(8,128)S(1)}, u32[]{:S(2)}, u32[]{:S(2)}) collective-permute-start(f32[128,128]{1,0:T(8,128)S(1)} %slice.101), channel_id=1, source_target_pairs={{0,16},{8,24},{16,0},{24,8},{1,17},{9,25},{17,1},{25,9},{2,18},{10... | collective-permute-start | bytes 196616 | tf_op jit(solution)/shard_map/ppermute | solution.py:298
  58.8 7.5 %collective-permute-start.9 = (f32[128,128]{1,0:T(8,128)S(1)}, f32[128,128]{1,0:T(8,128)S(1)}, u32[]{:S(2)}, u32[]{:S(2)}) collective-permute-start(f32[128,128]{1,0:T(8,128)S(1)} %slice.107), channel_id=1, source_target_pairs={{0,16},{8,24},{16,0},{24,8},{1,17},{9,25},{17,1},{25,9},{2,18},{10... | collective-permute-start | bytes 196616 | tf_op jit(solution)/shard_map/ppermute | solution.py:298
  59.2 8.5 %collective-permute-start.13 = (f32[128,128]{1,0:T(8,128)S(1)}, f32[128,128]{1,0:T(8,128)S(1)}, u32[]{:S(2)}, u32[]{:S(2)}) collective-permute-start(f32[128,128]{1,0:T(8,128)S(1)} %slice.113), channel_id=1, source_target_pairs={{0,16},{8,24},{16,0},{24,8},{1,17},{9,25},{17,1},{25,9},{2,18},{10... | collective-permute-start | bytes 196616 | tf_op jit(solution)/shard_map/ppermute | solution.py:298
  61.9 6.5 %collective-permute-start.17 = (f32[128,128]{1,0:T(8,128)S(1)}, f32[128,128]{1,0:T(8,128)S(1)}, u32[]{:S(2)}, u32[]{:S(2)}) collective-permute-start(f32[128,128]{1,0:T(8,128)S(1)} %slice.119), channel_id=1, source_target_pairs={{0,16},{8,24},{16,0},{24,8},{1,17},{9,25},{17,1},{25,9},{2,18},{10... | collective-permute-start | bytes 196616 | tf_op jit(solution)/shard_map/ppermute | solution.py:298
  69.1 1.3 %collective-permute-start.18 = (f32[128,128]{1,0:T(8,128)S(1)}, f32[128,128]{1,0:T(8,128)S(1)}, u32[]{:S(2)}, u32[]{:S(2)}) collective-permute-start(f32[128,128]{1,0:T(8,128)S(1)} %convolution_multiply_fusion), channel_id=1, source_target_pairs={{0,1},{1,0},{2,3},{3,2},{4,5},{5,4},{6,7},{7,6},{8,9},{9,8},{10,11... | collective-permute-start | bytes 196616 | tf_op jit(solution)/shard_map/ppermute | solution.py:297
  70.4 5.3 %collective-permute-start.21 = (f32[128,128]{1,0:T(8,128)S(1)}, f32[128,128]{1,0:T(8,128)S(1)}, u32[]{:S(2)}, u32[]{:S(2)}) collective-permute-start(f32[128,128]{1,0:T(8,128)S(1)} %add.86), channel_id=1, source_target_pairs={{0,6},{1,7},{2,4},{3,5},{4,2},{5,3},{6,0},{7,1},{8,14},{9,15},{10,... | collective-permute-start | bytes 196616 | tf_op jit(solution)/shard_map/ppermute | solution.py:297
  71.9 5.0 %collective-permute-start.20 = (f32[128,128]{1,0:T(8,128)S(1)}, f32[128,128]{1,0:T(8,128)S(1)}, u32[]{:S(2)}, u32[]{:S(2)}) collective-permute-start(f32[128,128]{1,0:T(8,128)S(1)} %add.86), channel_id=1, source_target_pairs={{0,4},{1,5},{2,6},{3,7},{4,0},{5,1},{6,2},{7,3},{8,12},{9,13},{10,... | collective-permute-start | bytes 196616 | tf_op jit(solution)/shard_map/ppermute | solution.py:297
  73.5 4.3 %collective-permute-start.19 = (f32[128,128]{1,0:T(8,128)S(1)}, f32[128,128]{1,0:T(8,128)S(1)}, u32[]{:S(2)}, u32[]{:S(2)}) collective-permute-start(f32[128,128]{1,0:T(8,128)S(1)} %add.86), channel_id=1, source_target_pairs={{0,2},{1,3},{2,0},{3,1},{4,6},{5,7},{6,4},{7,5},{8,10},{9,11},{10,... | collective-permute-start | bytes 196616 | tf_op jit(solution)/shard_map/ppermute | solution.py:297
  77.8 4.3 %collective-permute-start.22 = (f32[128,128]{1,0:T(8,128)S(1)}, f32[128,128]{1,0:T(8,128)S(1)}, u32[]{:S(2)}, u32[]{:S(2)}) collective-permute-start(f32[128,128]{1,0:T(8,128)S(1)} %add_add_fusion), channel_id=1, source_target_pairs={{0,8},{8,0},{16,24},{24,16},{1,9},{9,1},{17,25},{25,17},{2,10},{10... | collective-permute-start | bytes 196616 | tf_op jit(solution)/shard_map/ppermute | solution.py:298
  82.1 5.4 %collective-permute-start.23 = (f32[128,128]{1,0:T(8,128)S(1)}, f32[128,128]{1,0:T(8,128)S(1)}, u32[]{:S(2)}, u32[]{:S(2)}) collective-permute-start(f32[128,128]{1,0:T(8,128)S(1)} %add.90), channel_id=1, source_target_pairs={{0,16},{8,24},{16,0},{24,8},{1,17},{9,25},{17,1},{25,9},{2,18},{10... | collective-permute-start | bytes 196616 | tf_op jit(solution)/shard_map/ppermute | solution.py:298
  (3 other events, 2.4 us)

commit v5 on v4

--- a/solution.py
+++ b/solution.py
@@ -67,7 +67,7 @@
             out_ref[pl.ds(base + SUB * v, SUB), :] = part
         return carry
 
-    lax.fori_loop(0, BLOCK // GROUP, signed_group, 0)
+    lax.fori_loop(0, BLOCK // GROUP, signed_group, 0, unroll=True)
 
     def within_group(m, carry):
         base = pl.multiple_of(at + m * SUB * SUB, SUB * SUB)
@@ -81,7 +81,7 @@
                 out_ref[pl.ds(base + spot + SUB * t, SUB), :] = parts[SUB * k + t]
         return carry
 
-    lax.fori_loop(0, GROUP // (SUB * SUB), within_group, 0)
+    lax.fori_loop(0, GROUP // (SUB * SUB), within_group, 0, unroll=True)
 
 
 def spread_signs(bits_ref, word_ref):
@@ -268,8 +268,8 @@
     return jnp.concatenate(uppers, 0), jnp.concatenate(inverses, 0)
 
 
-def finish_kernel(gram_ref, sketch_ref, q_ref, upper_ref):
-    upper, inverse = factor(gram_ref[...])
+def finish_kernel(gram_ref, far_ref, sketch_ref, q_ref, upper_ref):
+    upper, inverse = factor(gram_ref[...] + far_ref[...])
     upper_ref[...] = upper
     q_ref[...] = lax.dot_general(
         sketch_ref[...],
@@ -417,7 +417,7 @@
         preferred_element_type=F32,
     ) / total
     groups = [(0,)] + [tuple(range(b, min(b + 2, inner_bits))) for b in range(1, inner_bits, 2)]
-    for group in groups + [(bit,) for bit in outer]:
+    for group in groups + [(bit,) for bit in outer[:-1]]:
         near = gram + swap(gram, 1 << group[0])
         if len(group) == 2:
             far = 1 << group[1]
@@ -430,10 +430,10 @@
             jax.ShapeDtypeStruct((own_count, width), F32),
             jax.ShapeDtypeStruct((width, width), F32),
         ),
-        in_specs=[vmem, vmem],
+        in_specs=[vmem, vmem, vmem],
         out_specs=(vmem, vmem),
         name="finish",
-    )(gram, sketch)
+    )(gram, pltpu.with_memory_space_constraint(swap(gram, 1 << outer[-1]), pltpu.VMEM), sketch)
 
 
 def solution(mesh):

time: 94.6 us -> 93.6 us (0.989)
    unnamed x6 -> x8, local copies, waits for them, and re-layouts: 2.44 us -> 2.44 us
where the time goes in v5:
time: 93.6 us; the launch traced here: 93.3 us
  Pallas kernels  30.3 us (32%)
  starting transfers between devices  30.2 us (32%)
  waiting for transfers between devices  27.4 us (29%)
  local copies, waits for them, and re-layouts  2.58 us (3%)
  other arithmetic  1.23 us (1%)
  between operations  0.94 us (1%)
    pallas_call x8, Pallas kernels, pick(): pl.pallas_call(pick_kernel, out_shape=jax.ShapeDtypeStruct((count, table....  15.3 us
    ppermute x14, starting transfers between devices, swap(): return lax.ppermute(value, 'exb', bit_perm(n_inner, mask))  15.1 us
    ppermute x10, starting transfers between devices, swap(): return lax.ppermute(value, 'exa', bit_perm(n_outer, mask // n_inner))  15.1 us
    ppermute x14, waiting for transfers between devices, swap(): return lax.ppermute(value, 'exb', bit_perm(n_inner, mask))  14.2 us
    ppermute x10, waiting for transfers between devices, swap(): return lax.ppermute(value, 'exa', bit_perm(n_outer, mask // n_inner))  13.2 us
    pallas_call x1, Pallas kernels, per_device(): pl.pallas_call(finish_kernel, out_shape=(jax.ShapeDtypeStruct((own_count,...  6.15 us
    pallas_call x1, Pallas kernels, per_device(): pl.pallas_call(pair_kernel, out_shape=jax.ShapeDtypeStruct((2 * rows_dev,...  4.73 us
    pallas_call x1, Pallas kernels, per_device(): pl.pallas_call(functools.partial(own_kernel, 1.0 / math.sqrt(rows_dev * n...  4.2 us
  transfers between devices with their start and end apart: 24, of which 16 were waited for; matrix products, arithmetic and copies ran while one was open for 1% of the time, Pallas kernels for 19%

profile of v5, /device:TPU:0, one launch (start us, length us, event | category | flops | bytes accessed | tf_op | source)
XLA Modules:
  0.0 93.3 jit_solution(376069685102402951)
XLA Ops:
  3.7 4.2 %own.1 = (f32[8192,128]{1,0:T(8,128)S(1)}, s32[1,1024]{1,0:T(1,128)S(1)}, f32[1,1024]{1,0:T(1,128)S(1)}, s32[1,1024]{1,0:T(1,128)S(1)}, f32[1,1024]{1,0:T(1,128)...) custom-call(f32[8192,128]{1,0:T(8,128)} %x_ref.1, ...), custom_call_target="tpu_custom_call" | custom-call | flops 10000000 | bytes 12582912 | tf_op jit(solution)/shard_map/own/pallas_call | solution.py:349
  8.3 4.7 %pair.1.table_ref = f32[16384,128]{1,0:T(8,128)S(1)} custom-call(f32[8192,128]{1,0:T(8,128)} %collective-permute-done.x_ref, s32[64,128]{1,0:T(8,128)S(1)} %bitcast.8, f32[8192,128]{1,0:T(8,128)S(1)} %get-tuple-element.21.own_ref), custom_call_target="tpu_custom_call" | custom-call | flops 10000000 | bytes 16777216 | tf_op jit(solution)/shard_map/pair/pallas_call | solution.py:371
  13.1 1.9 %pick.9 = f32[1024,128]{1,0:T(8,128)S(1)} custom-call(s32[1,1024]{1,0:T(1,128)S(1)} %get-tuple-element.22.row_ref, f32[1,1024]{1,0:T(1,128)S(1)} %get-tuple-element.23.sign_ref, f32[16384,128]{1,0:T(8,128)S(1)} %pair.1.table_ref), custom_call_target="tpu_custom_call" | custom-call | flops 1024 | bytes 1024 | tf_op jit(solution)/shard_map/pick/pallas_call | solution.py:186
  15.0 2.9 %collective-permute-start.2 = (f32[1024,128]{1,0:T(8,128)S(1)}, f32[1024,128]{1,0:T(8,128)S(1)}, u32[]{:S(2)}, u32[]{:S(2)}) collective-permute-start(f32[1024,128]{1,0:T(8,128)S(1)} %pick.9), channel_id=1, source_target_pairs={{0,2},{1,3},{2,0},{3,1},{4,6},{5,7},{6,4},{7,5},{8,10},{9,11},{10,... | collective-permute-start | bytes 1572872 | tf_op jit(solution)/shard_map/ppermute | solution.py:297
  17.9 1.9 %pick.11 = f32[1024,128]{1,0:T(8,128)S(1)} custom-call(s32[1,1024]{1,0:T(1,128)S(1)} %get-tuple-element.26.row_ref, f32[1,1024]{1,0:T(1,128)S(1)} %get-tuple-element.27.sign_ref, f32[16384,128]{1,0:T(8,128)S(1)} %pair.1.table_ref), custom_call_target="tpu_custom_call" | custom-call | flops 1024 | bytes 1024 | tf_op jit(solution)/shard_map/pick/pallas_call | solution.py:186
  21.4 1.9 %pick.13 = f32[1024,128]{1,0:T(8,128)S(1)} custom-call(s32[1,1024]{1,0:T(1,128)S(1)} %get-tuple-element.30.row_ref, f32[1,1024]{1,0:T(1,128)S(1)} %get-tuple-element.31.sign_ref, f32[16384,128]{1,0:T(8,128)S(1)} %pair.1.table_ref), custom_call_target="tpu_custom_call" | custom-call | flops 1024 | bytes 1024 | tf_op jit(solution)/shard_map/pick/pallas_call | solution.py:186
  23.9 1.9 %pick.15 = f32[1024,128]{1,0:T(8,128)S(1)} custom-call(s32[1,1024]{1,0:T(1,128)S(1)} %get-tuple-element.34.row_ref, f32[1,1024]{1,0:T(1,128)S(1)} %get-tuple-element.35.sign_ref, f32[16384,128]{1,0:T(8,128)S(1)} %pair.1.table_ref), custom_call_target="tpu_custom_call" | custom-call | flops 1024 | bytes 1024 | tf_op jit(solution)/shard_map/pick/pallas_call | solution.py:186
  25.9 1.9 %pick.8 = f32[1024,128]{1,0:T(8,128)S(1)} custom-call(s32[1,1024]{1,0:T(1,128)S(1)} %get-tuple-element.19.row_ref, f32[1,1024]{1,0:T(1,128)S(1)} %get-tuple-element.20.sign_ref, f32[16384,128]{1,0:T(8,128)S(1)} %pair.1.table_ref), custom_call_target="tpu_custom_call" | custom-call | flops 1024 | bytes 1024 | tf_op jit(solution)/shard_map/pick/pallas_call | solution.py:186
  27.8 2.8 %collective-permute-done.2.refs_0_ = f32[1024,128]{1,0:T(8,128)S(1)} collective-permute-done((f32[1024,128]{1,0:T(8,128)S(1)}, f32[1024,128]{1,0:T(8,128)S(1)}, u32[]{:S(2)}, u32[]{:S(2)}) %collective-permute-start.2) | collective-permute-done | bytes 524320 | tf_op jit(solution)/shard_map/ppermute | solution.py:297
  30.7 2.2 %collective-permute-start.3 = (f32[512,128]{1,0:T(8,128)S(1)}, f32[512,128]{1,0:T(8,128)S(1)}, u32[]{:S(2)}, u32[]{:S(2)}) collective-permute-start(f32[512,128]{1,0:T(8,128)S(1)} %slice.97), channel_id=1, source_target_pairs={{0,8},{8,0},{16,24},{24,16},{1,9},{9,1},{17,25},{25,17},{2,10},{10... | collective-permute-start | bytes 786440 | tf_op jit(solution)/shard_map/ppermute | solution.py:298
  32.9 1.9 %pick.10 = f32[1024,128]{1,0:T(8,128)S(1)} custom-call(s32[1,1024]{1,0:T(1,128)S(1)} %get-tuple-element.24.row_ref, f32[1,1024]{1,0:T(1,128)S(1)} %get-tuple-element.25.sign_ref, f32[16384,128]{1,0:T(8,128)S(1)} %pair.1.table_ref), custom_call_target="tpu_custom_call" | custom-call | flops 1024 | bytes 1024 | tf_op jit(solution)/shard_map/pick/pallas_call | solution.py:186
  36.4 1.9 %pick.12 = f32[1024,128]{1,0:T(8,128)S(1)} custom-call(s32[1,1024]{1,0:T(1,128)S(1)} %get-tuple-element.28.row_ref, f32[1,1024]{1,0:T(1,128)S(1)} %get-tuple-element.29.sign_ref, f32[16384,128]{1,0:T(8,128)S(1)} %pair.1.table_ref, f32[1024,128]{1,0:T(8,128)S(1)} %collective-permute-done.2.refs_0_), custom_call_target="tpu_custom_call" | custom-call | flops 1024 | bytes 1024 | tf_op jit(solution)/shard_map/pick/pallas_call | solution.py:186
  38.3 3.0 %collective-permute-done.10 = f32[1024,128]{1,0:T(8,128)S(1)} collective-permute-done((f32[1024,128]{1,0:T(8,128)S(1)}, f32[1024,128]{1,0:T(8,128)S(1)}, u32[]{:S(2)}, u32[]{:S(2)}) %collective-permute-start.10) | collective-permute-done | bytes 524320 | tf_op jit(solution)/shard_map/ppermute | solution.py:297
  41.5 1.8 %collective-permute-start.11 = (f32[512,128]{1,0:T(8,128)S(1)}, f32[512,128]{1,0:T(8,128)S(1)}, u32[]{:S(2)}, u32[]{:S(2)}) collective-permute-start(f32[512,128]{1,0:T(8,128)S(1)} %slice.109), channel_id=1, source_target_pairs={{0,4},{1,5},{2,6},{3,7},{4,0},{5,1},{6,2},{7,3},{8,12},{9,13},{10,... | collective-permute-start | bytes 786440 | tf_op jit(solution)/shard_map/ppermute | solution.py:297
  43.3 1.9 %pick.14 = f32[1024,128]{1,0:T(8,128)S(1)} custom-call(s32[1,1024]{1,0:T(1,128)S(1)} %get-tuple-element.32.row_ref, f32[1,1024]{1,0:T(1,128)S(1)} %get-tuple-element.33.sign_ref, f32[16384,128]{1,0:T(8,128)S(1)} %pair.1.table_ref, f32[1024,128]{1,0:T(8,128)S(1)} %collective-permute-done.6.refs_0_), custom_call_target="tpu_custom_call" | custom-call | flops 1024 | bytes 1024 | tf_op jit(solution)/shard_map/pick/pallas_call | solution.py:186
  47.8 2.1 %collective-permute-start.8 = (f32[256,128]{1,0:T(8,128)S(1)}, f32[256,128]{1,0:T(8,128)S(1)}, u32[]{:S(2)}, u32[]{:S(2)}) collective-permute-start(f32[256,128]{1,0:T(8,128)S(1)} %slice.105), channel_id=1, source_target_pairs={{0,2},{1,3},{2,0},{3,1},{4,6},{5,7},{6,4},{7,5},{8,10},{9,11},{10,... | collective-permute-start | bytes 393224 | tf_op jit(solution)/shard_map/ppermute | solution.py:297
  51.5 1.8 %collective-permute-start.12 = (f32[256,128]{1,0:T(8,128)S(1)}, f32[256,128]{1,0:T(8,128)S(1)}, u32[]{:S(2)}, u32[]{:S(2)}) collective-permute-start(f32[256,128]{1,0:T(8,128)S(1)} %slice.111), channel_id=1, source_target_pairs={{0,8},{8,0},{16,24},{24,16},{1,9},{9,1},{17,25},{25,17},{2,10},{10... | collective-permute-start | bytes 393224 | tf_op jit(solution)/shard_map/ppermute | solution.py:298
  55.7 2.7 %collective-permute-start.5 = (f32[128,128]{1,0:T(8,128)S(1)}, f32[128,128]{1,0:T(8,128)S(1)}, u32[]{:S(2)}, u32[]{:S(2)}) collective-permute-start(f32[128,128]{1,0:T(8,128)S(1)} %slice.101), channel_id=1, source_target_pairs={{0,16},{8,24},{16,0},{24,8},{1,17},{9,25},{17,1},{25,9},{2,18},{10... | collective-permute-start | bytes 196616 | tf_op jit(solution)/shard_map/ppermute | solution.py:298
  58.9 2.7 %collective-permute-start.13 = (f32[128,128]{1,0:T(8,128)S(1)}, f32[128,128]{1,0:T(8,128)S(1)}, u32[]{:S(2)}, u32[]{:S(2)}) collective-permute-start(f32[128,128]{1,0:T(8,128)S(1)} %slice.113), channel_id=1, source_target_pairs={{0,16},{8,24},{16,0},{24,8},{1,17},{9,25},{17,1},{25,9},{2,18},{10... | collective-permute-start | bytes 196616 | tf_op jit(solution)/shard_map/ppermute | solution.py:298
  62.9 2.3 %collective-permute-done.5 = f32[128,128]{1,0:T(8,128)S(1)} collective-permute-done((f32[128,128]{1,0:T(8,128)S(1)}, f32[128,128]{1,0:T(8,128)S(1)}, u32[]{:S(2)}, u32[]{:S(2)}) %collective-permute-start.5) | collective-permute-done | bytes 65568 | tf_op jit(solution)/shard_map/ppermute | solution.py:298
  73.6 1.8 %collective-permute-done.21 = f32[128,128]{1,0:T(8,128)S(1)} collective-permute-done((f32[128,128]{1,0:T(8,128)S(1)}, f32[128,128]{1,0:T(8,128)S(1)}, u32[]{:S(2)}, u32[]{:S(2)}) %collective-permute-start.21) | collective-permute-done | bytes 65568 | tf_op jit(solution)/shard_map/ppermute | solution.py:297
  77.5 4.3 %collective-permute-done.22 = f32[128,128]{1,0:T(8,128)S(1)} collective-permute-done((f32[128,128]{1,0:T(8,128)S(1)}, f32[128,128]{1,0:T(8,128)S(1)}, u32[]{:S(2)}, u32[]{:S(2)}) %collective-permute-start.22) | collective-permute-done | bytes 65568 | tf_op jit(solution)/shard_map/ppermute | solution.py:298
  83.4 3.8 %collective-permute-done.23.far_ref = f32[128,128]{1,0:T(8,128)S(1)} collective-permute-done((f32[128,128]{1,0:T(8,128)S(1)}, f32[128,128]{1,0:T(8,128)S(1)}, u32[]{:S(2)}, u32[]{:S(2)}) %collective-permute-start.23) | collective-permute-done | bytes 65568 | tf_op jit(solution)/shard_map/ppermute | solution.py:298
  87.2 6.1 %finish.1 = (f32[512,128]{1,0:T(8,128)}, f32[128,128]{1,0:T(8,128)}) custom-call(f32[128,128]{1,0:T(8,128)} %copy-done.3, f32[128,128]{1,0:T(8,128)S(1)} %collective-permute-done.23.far_ref, f32[512,128]{1,0:T(8,128)} %pad_maximum_fusion.sketch_ref), custom_call_target="tpu_custom_call" | custom-call | tf_op jit(solution)/shard_map/finish/pallas_call | solution.py:427
  (76 shorter events, 28.0 us)
Async XLA Ops:
  0.6 7.7 %collective-permute-start = (f32[8192,128]{1,0:T(8,128)}, f32[8192,128]{1,0:T(8,128)}, u32[]{:S(2)}, u32[]{:S(2)}) collective-permute-start(f32[8192,128]{1,0:T(8,128)} %x_ref.1), channel_id=1, source_target_pairs={{0,1},{1,0},{2,3},{3,2},{4,5},{5,4},{6,7},{7,6},{8,9},{9,8},{10,11... | collective-permute-start | bytes 12582920 | tf_op jit(solution)/shard_map/ppermute | solution.py:297
  1.1 6.7 %collective-permute-start.1 = (s32[8192]{0:T(1024)}, s32[8192]{0:T(1024)S(1)}, u32[]{:S(2)}, u32[]{:S(2)}) collective-permute-start(s32[8192]{0:T(1024)} %param.5), channel_id=1, source_target_pairs={{0,1},{1,0},{2,3},{3,2},{4,5},{5,4},{6,7},{7,6},{8,9},{9,8},{10,11... | collective-permute-start | bytes 98312 | tf_op jit(solution)/shard_map/ppermute | solution.py:297
  15.0 15.6 %collective-permute-start.2 = (f32[1024,128]{1,0:T(8,128)S(1)}, f32[1024,128]{1,0:T(8,128)S(1)}, u32[]{:S(2)}, u32[]{:S(2)}) collective-permute-start(f32[1024,128]{1,0:T(8,128)S(1)} %pick.9), channel_id=1, source_target_pairs={{0,2},{1,3},{2,0},{3,1},{4,6},{5,7},{6,4},{7,5},{8,10},{9,11},{10,... | collective-permute-start | bytes 1572872 | tf_op jit(solution)/shard_map/ppermute | solution.py:297
  19.8 15.0 %collective-permute-start.6 = (f32[1024,128]{1,0:T(8,128)S(1)}, f32[1024,128]{1,0:T(8,128)S(1)}, u32[]{:S(2)}, u32[]{:S(2)}) collective-permute-start(f32[1024,128]{1,0:T(8,128)S(1)} %pick.11), channel_id=1, source_target_pairs={{0,4},{1,5},{2,6},{3,7},{4,0},{5,1},{6,2},{7,3},{8,12},{9,13},{10,... | collective-permute-start | bytes 1572872 | tf_op jit(solution)/shard_map/ppermute | solution.py:297
  23.3 18.0 %collective-permute-start.10 = (f32[1024,128]{1,0:T(8,128)S(1)}, f32[1024,128]{1,0:T(8,128)S(1)}, u32[]{:S(2)}, u32[]{:S(2)}) collective-permute-start(f32[1024,128]{1,0:T(8,128)S(1)} %pick.13), channel_id=1, source_target_pairs={{0,2},{1,3},{2,0},{3,1},{4,6},{5,7},{6,4},{7,5},{8,10},{9,11},{10,... | collective-permute-start | bytes 1572872 | tf_op jit(solution)/shard_map/ppermute | solution.py:297
  25.8 20.0 %collective-permute-start.14 = (f32[1024,128]{1,0:T(8,128)S(1)}, f32[1024,128]{1,0:T(8,128)S(1)}, u32[]{:S(2)}, u32[]{:S(2)}) collective-permute-start(f32[1024,128]{1,0:T(8,128)S(1)} %pick.15), channel_id=1, source_target_pairs={{0,4},{1,5},{2,6},{3,7},{4,0},{5,1},{6,2},{7,3},{8,12},{9,13},{10,... | collective-permute-start | bytes 1572872 | tf_op jit(solution)/shard_map/ppermute | solution.py:297
  30.7 16.2 %collective-permute-start.3 = (f32[512,128]{1,0:T(8,128)S(1)}, f32[512,128]{1,0:T(8,128)S(1)}, u32[]{:S(2)}, u32[]{:S(2)}) collective-permute-start(f32[512,128]{1,0:T(8,128)S(1)} %slice.97), channel_id=1, source_target_pairs={{0,8},{8,0},{16,24},{24,16},{1,9},{9,1},{17,25},{25,17},{2,10},{10... | collective-permute-start | bytes 786440 | tf_op jit(solution)/shard_map/ppermute | solution.py:298
  34.9 12.8 %collective-permute-start.7 = (f32[512,128]{1,0:T(8,128)S(1)}, f32[512,128]{1,0:T(8,128)S(1)}, u32[]{:S(2)}, u32[]{:S(2)}) collective-permute-start(f32[512,128]{1,0:T(8,128)S(1)} %slice.103), channel_id=1, source_target_pairs={{0,8},{8,0},{16,24},{24,16},{1,9},{9,1},{17,25},{25,17},{2,10},{10... | collective-permute-start | bytes 786440 | tf_op jit(solution)/shard_map/ppermute | solution.py:298
  41.5 10.0 %collective-permute-start.11 = (f32[512,128]{1,0:T(8,128)S(1)}, f32[512,128]{1,0:T(8,128)S(1)}, u32[]{:S(2)}, u32[]{:S(2)}) collective-permute-start(f32[512,128]{1,0:T(8,128)S(1)} %slice.109), channel_id=1, source_target_pairs={{0,4},{1,5},{2,6},{3,7},{4,0},{5,1},{6,2},{7,3},{8,12},{9,13},{10,... | collective-permute-start | bytes 786440 | tf_op jit(solution)/shard_map/ppermute | solution.py:297
  45.9 8.1 %collective-permute-start.15 = (f32[512,128]{1,0:T(8,128)S(1)}, f32[512,128]{1,0:T(8,128)S(1)}, u32[]{:S(2)}, u32[]{:S(2)}) collective-permute-start(f32[512,128]{1,0:T(8,128)S(1)} %slice.115), channel_id=1, source_target_pairs={{0,2},{1,3},{2,0},{3,1},{4,6},{5,7},{6,4},{7,5},{8,10},{9,11},{10,... | collective-permute-start | bytes 786440 | tf_op jit(solution)/shard_map/ppermute | solution.py:297
  46.9 8.8 %collective-permute-start.4 = (f32[256,128]{1,0:T(8,128)S(1)}, f32[256,128]{1,0:T(8,128)S(1)}, u32[]{:S(2)}, u32[]{:S(2)}) collective-permute-start(f32[256,128]{1,0:T(8,128)S(1)} %slice.99), channel_id=1, source_target_pairs={{0,4},{1,5},{2,6},{3,7},{4,0},{5,1},{6,2},{7,3},{8,12},{9,13},{10,... | collective-permute-start | bytes 393224 | tf_op jit(solution)/shard_map/ppermute | solution.py:297
  47.8 10.6 %collective-permute-start.8 = (f32[256,128]{1,0:T(8,128)S(1)}, f32[256,128]{1,0:T(8,128)S(1)}, u32[]{:S(2)}, u32[]{:S(2)}) collective-permute-start(f32[256,128]{1,0:T(8,128)S(1)} %slice.105), channel_id=1, source_target_pairs={{0,2},{1,3},{2,0},{3,1},{4,6},{5,7},{6,4},{7,5},{8,10},{9,11},{10,... | collective-permute-start | bytes 393224 | tf_op jit(solution)/shard_map/ppermute | solution.py:297
  51.5 7.4 %collective-permute-start.12 = (f32[256,128]{1,0:T(8,128)S(1)}, f32[256,128]{1,0:T(8,128)S(1)}, u32[]{:S(2)}, u32[]{:S(2)}) collective-permute-start(f32[256,128]{1,0:T(8,128)S(1)} %slice.111), channel_id=1, source_target_pairs={{0,8},{8,0},{16,24},{24,16},{1,9},{9,1},{17,25},{25,17},{2,10},{10... | collective-permute-start | bytes 393224 | tf_op jit(solution)/shard_map/ppermute | solution.py:298
  54.1 7.5 %collective-permute-start.16 = (f32[256,128]{1,0:T(8,128)S(1)}, f32[256,128]{1,0:T(8,128)S(1)}, u32[]{:S(2)}, u32[]{:S(2)}) collective-permute-start(f32[256,128]{1,0:T(8,128)S(1)} %slice.117), channel_id=1, source_target_pairs={{0,8},{8,0},{16,24},{24,16},{1,9},{9,1},{17,25},{25,17},{2,10},{10... | collective-permute-start | bytes 393224 | tf_op jit(solution)/shard_map/ppermute | solution.py:298
  55.7 9.4 %collective-permute-start.5 = (f32[128,128]{1,0:T(8,128)S(1)}, f32[128,128]{1,0:T(8,128)S(1)}, u32[]{:S(2)}, u32[]{:S(2)}) collective-permute-start(f32[128,128]{1,0:T(8,128)S(1)} %slice.101), channel_id=1, source_target_pairs={{0,16},{8,24},{16,0},{24,8},{1,17},{9,25},{17,1},{25,9},{2,18},{10... | collective-permute-start | bytes 196616 | tf_op jit(solution)/shard_map/ppermute | solution.py:298
  58.4 7.5 %collective-permute-start.9 = (f32[128,128]{1,0:T(8,128)S(1)}, f32[128,128]{1,0:T(8,128)S(1)}, u32[]{:S(2)}, u32[]{:S(2)}) collective-permute-start(f32[128,128]{1,0:T(8,128)S(1)} %slice.107), channel_id=1, source_target_pairs={{0,16},{8,24},{16,0},{24,8},{1,17},{9,25},{17,1},{25,9},{2,18},{10... | collective-permute-start | bytes 196616 | tf_op jit(solution)/shard_map/ppermute | solution.py:298
  58.9 8.5 %collective-permute-start.13 = (f32[128,128]{1,0:T(8,128)S(1)}, f32[128,128]{1,0:T(8,128)S(1)}, u32[]{:S(2)}, u32[]{:S(2)}) collective-permute-start(f32[128,128]{1,0:T(8,128)S(1)} %slice.113), channel_id=1, source_target_pairs={{0,16},{8,24},{16,0},{24,8},{1,17},{9,25},{17,1},{25,9},{2,18},{10... | collective-permute-start | bytes 196616 | tf_op jit(solution)/shard_map/ppermute | solution.py:298
  61.6 6.5 %collective-permute-start.17 = (f32[128,128]{1,0:T(8,128)S(1)}, f32[128,128]{1,0:T(8,128)S(1)}, u32[]{:S(2)}, u32[]{:S(2)}) collective-permute-start(f32[128,128]{1,0:T(8,128)S(1)} %slice.119), channel_id=1, source_target_pairs={{0,16},{8,24},{16,0},{24,8},{1,17},{9,25},{17,1},{25,9},{2,18},{10... | collective-permute-start | bytes 196616 | tf_op jit(solution)/shard_map/ppermute | solution.py:298
  68.7 1.3 %collective-permute-start.18 = (f32[128,128]{1,0:T(8,128)S(1)}, f32[128,128]{1,0:T(8,128)S(1)}, u32[]{:S(2)}, u32[]{:S(2)}) collective-permute-start(f32[128,128]{1,0:T(8,128)S(1)} %convolution_multiply_fusion), channel_id=1, source_target_pairs={{0,1},{1,0},{2,3},{3,2},{4,5},{5,4},{6,7},{7,6},{8,9},{9,8},{10,11... | collective-permute-start | bytes 196616 | tf_op jit(solution)/shard_map/ppermute | solution.py:297
  70.0 5.3 %collective-permute-start.21 = (f32[128,128]{1,0:T(8,128)S(1)}, f32[128,128]{1,0:T(8,128)S(1)}, u32[]{:S(2)}, u32[]{:S(2)}) collective-permute-start(f32[128,128]{1,0:T(8,128)S(1)} %add.83), channel_id=1, source_target_pairs={{0,6},{1,7},{2,4},{3,5},{4,2},{5,3},{6,0},{7,1},{8,14},{9,15},{10,... | collective-permute-start | bytes 196616 | tf_op jit(solution)/shard_map/ppermute | solution.py:297
  71.6 5.0 %collective-permute-start.20 = (f32[128,128]{1,0:T(8,128)S(1)}, f32[128,128]{1,0:T(8,128)S(1)}, u32[]{:S(2)}, u32[]{:S(2)}) collective-permute-start(f32[128,128]{1,0:T(8,128)S(1)} %add.83), channel_id=1, source_target_pairs={{0,4},{1,5},{2,6},{3,7},{4,0},{5,1},{6,2},{7,3},{8,12},{9,13},{10,... | collective-permute-start | bytes 196616 | tf_op jit(solution)/shard_map/ppermute | solution.py:297
  73.1 4.3 %collective-permute-start.19 = (f32[128,128]{1,0:T(8,128)S(1)}, f32[128,128]{1,0:T(8,128)S(1)}, u32[]{:S(2)}, u32[]{:S(2)}) collective-permute-start(f32[128,128]{1,0:T(8,128)S(1)} %add.83), channel_id=1, source_target_pairs={{0,2},{1,3},{2,0},{3,1},{4,6},{5,7},{6,4},{7,5},{8,10},{9,11},{10,... | collective-permute-start | bytes 196616 | tf_op jit(solution)/shard_map/ppermute | solution.py:297
  77.4 4.3 %collective-permute-start.22 = (f32[128,128]{1,0:T(8,128)S(1)}, f32[128,128]{1,0:T(8,128)S(1)}, u32[]{:S(2)}, u32[]{:S(2)}) collective-permute-start(f32[128,128]{1,0:T(8,128)S(1)} %add_add_fusion), channel_id=1, source_target_pairs={{0,8},{8,0},{16,24},{24,16},{1,9},{9,1},{17,25},{25,17},{2,10},{10... | collective-permute-start | bytes 196616 | tf_op jit(solution)/shard_map/ppermute | solution.py:298
  81.8 5.4 %collective-permute-start.23 = (f32[128,128]{1,0:T(8,128)S(1)}, f32[128,128]{1,0:T(8,128)S(1)}, u32[]{:S(2)}, u32[]{:S(2)}) collective-permute-start(f32[128,128]{1,0:T(8,128)S(1)} %add.87.gram_ref), channel_id=1, source_target_pairs={{0,16},{8,24},{16,0},{24,8},{1,17},{9,25},{17,1},{25,9},{2,18},{10... | collective-permute-start | bytes 196616 | tf_op jit(solution)/shard_map/ppermute | solution.py:298
  (4 other events, 7.8 us)

commit v6 on v5

--- a/solution.py
+++ b/solution.py
@@ -167,7 +167,7 @@
 def pick_kernel(row_ref, sign_ref, table_ref, *refs):
     out_ref = refs[-1]
     count = out_ref.shape[0]
-    unroll = math.gcd(count, 32)
+    unroll = math.gcd(count, 64)
 
     def some(i, carry):
         for u in range(unroll):
@@ -417,7 +417,7 @@
         preferred_element_type=F32,
     ) / total
     groups = [(0,)] + [tuple(range(b, min(b + 2, inner_bits))) for b in range(1, inner_bits, 2)]
-    for group in groups + [(bit,) for bit in outer[:-1]]:
+    for group in groups + [(bit,) for bit in outer[1:]]:
         near = gram + swap(gram, 1 << group[0])
         if len(group) == 2:
             far = 1 << group[1]
@@ -433,7 +433,7 @@
         in_specs=[vmem, vmem, vmem],
         out_specs=(vmem, vmem),
         name="finish",
-    )(gram, pltpu.with_memory_space_constraint(swap(gram, 1 << outer[-1]), pltpu.VMEM), sketch)
+    )(gram, pltpu.with_memory_space_constraint(swap(gram, 1 << outer[0]), pltpu.VMEM), sketch)
 
 
 def solution(mesh):

time: 93.6 us -> 93.4 us (level)
  waiting for transfers between devices: 27.4 us -> 28.7 us
  transfers between devices with their start and end apart: 24 -> 24, of which waited for: 16 -> 16; matrix products, arithmetic and copies ran while one was open for 1% -> 1% of each run, Pallas kernels for 19% -> 18%
where the time goes in v6:
time: 93.4 us; the launch traced here: 93.1 us
  Pallas kernels  29.7 us (32%)
  starting transfers between devices  29.4 us (31%)
  waiting for transfers between devices  28.7 us (31%)
  local copies, waits for them, and re-layouts  2.58 us (3%)
  other arithmetic  1.23 us (1%)
  between operations  0.94 us (1%)
    ppermute x14, starting transfers between devices, swap(): return lax.ppermute(value, 'exb', bit_perm(n_inner, mask))  15.1 us
    ppermute x14, waiting for transfers between devices, swap(): return lax.ppermute(value, 'exb', bit_perm(n_inner, mask))  14.7 us
    pallas_call x8, Pallas kernels, pick(): pl.pallas_call(pick_kernel, out_shape=jax.ShapeDtypeStruct((count, table....  14.6 us
    ppermute x10, starting transfers between devices, swap(): return lax.ppermute(value, 'exa', bit_perm(n_outer, mask // n_inner))  14.4 us
    ppermute x10, waiting for transfers between devices, swap(): return lax.ppermute(value, 'exa', bit_perm(n_outer, mask // n_inner))  14 us
    pallas_call x1, Pallas kernels, per_device(): pl.pallas_call(finish_kernel, out_shape=(jax.ShapeDtypeStruct((own_count,...  6.15 us
    pallas_call x1, Pallas kernels, per_device(): pl.pallas_call(pair_kernel, out_shape=jax.ShapeDtypeStruct((2 * rows_dev,...  4.73 us
    pallas_call x1, Pallas kernels, per_device(): pl.pallas_call(functools.partial(own_kernel, 1.0 / math.sqrt(rows_dev * n...  4.2 us
  transfers between devices with their start and end apart: 24, of which 16 were waited for; matrix products, arithmetic and copies ran while one was open for 1% of the time, Pallas kernels for 18%

profile of v6, /device:TPU:0, one launch (start us, length us, event | category | flops | bytes accessed | tf_op | source)
XLA Modules:
  0.0 93.1 jit_solution(5643604213909726125)
XLA Ops:
  3.7 4.2 %own.1 = (f32[8192,128]{1,0:T(8,128)S(1)}, s32[1,1024]{1,0:T(1,128)S(1)}, f32[1,1024]{1,0:T(1,128)S(1)}, s32[1,1024]{1,0:T(1,128)S(1)}, f32[1,1024]{1,0:T(1,128)...) custom-call(f32[8192,128]{1,0:T(8,128)} %x_ref.1, ...), custom_call_target="tpu_custom_call" | custom-call | flops 10000000 | bytes 12582912 | tf_op jit(solution)/shard_map/own/pallas_call | solution.py:349
  8.3 4.7 %pair.1.table_ref = f32[16384,128]{1,0:T(8,128)S(1)} custom-call(f32[8192,128]{1,0:T(8,128)} %collective-permute-done.x_ref, s32[64,128]{1,0:T(8,128)S(1)} %bitcast.8, f32[8192,128]{1,0:T(8,128)S(1)} %get-tuple-element.21.own_ref), custom_call_target="tpu_custom_call" | custom-call | flops 10000000 | bytes 16777216 | tf_op jit(solution)/shard_map/pair/pallas_call | solution.py:371
  13.1 1.8 %pick.9 = f32[1024,128]{1,0:T(8,128)S(1)} custom-call(s32[1,1024]{1,0:T(1,128)S(1)} %get-tuple-element.22.row_ref, f32[1,1024]{1,0:T(1,128)S(1)} %get-tuple-element.23.sign_ref, f32[16384,128]{1,0:T(8,128)S(1)} %pair.1.table_ref), custom_call_target="tpu_custom_call" | custom-call | flops 1024 | bytes 1024 | tf_op jit(solution)/shard_map/pick/pallas_call | solution.py:186
  14.9 2.9 %collective-permute-start.2 = (f32[1024,128]{1,0:T(8,128)S(1)}, f32[1024,128]{1,0:T(8,128)S(1)}, u32[]{:S(2)}, u32[]{:S(2)}) collective-permute-start(f32[1024,128]{1,0:T(8,128)S(1)} %pick.9), channel_id=1, source_target_pairs={{0,2},{1,3},{2,0},{3,1},{4,6},{5,7},{6,4},{7,5},{8,10},{9,11},{10,... | collective-permute-start | bytes 1572872 | tf_op jit(solution)/shard_map/ppermute | solution.py:297
  17.8 1.8 %pick.11 = f32[1024,128]{1,0:T(8,128)S(1)} custom-call(s32[1,1024]{1,0:T(1,128)S(1)} %get-tuple-element.26.row_ref, f32[1,1024]{1,0:T(1,128)S(1)} %get-tuple-element.27.sign_ref, f32[16384,128]{1,0:T(8,128)S(1)} %pair.1.table_ref), custom_call_target="tpu_custom_call" | custom-call | flops 1024 | bytes 1024 | tf_op jit(solution)/shard_map/pick/pallas_call | solution.py:186
  21.2 1.8 %pick.13 = f32[1024,128]{1,0:T(8,128)S(1)} custom-call(s32[1,1024]{1,0:T(1,128)S(1)} %get-tuple-element.30.row_ref, f32[1,1024]{1,0:T(1,128)S(1)} %get-tuple-element.31.sign_ref, f32[16384,128]{1,0:T(8,128)S(1)} %pair.1.table_ref), custom_call_target="tpu_custom_call" | custom-call | flops 1024 | bytes 1024 | tf_op jit(solution)/shard_map/pick/pallas_call | solution.py:186
  23.7 1.8 %pick.15 = f32[1024,128]{1,0:T(8,128)S(1)} custom-call(s32[1,1024]{1,0:T(1,128)S(1)} %get-tuple-element.34.row_ref, f32[1,1024]{1,0:T(1,128)S(1)} %get-tuple-element.35.sign_ref, f32[16384,128]{1,0:T(8,128)S(1)} %pair.1.table_ref), custom_call_target="tpu_custom_call" | custom-call | flops 1024 | bytes 1024 | tf_op jit(solution)/shard_map/pick/pallas_call | solution.py:186
  25.6 1.8 %pick.8 = f32[1024,128]{1,0:T(8,128)S(1)} custom-call(s32[1,1024]{1,0:T(1,128)S(1)} %get-tuple-element.19.row_ref, f32[1,1024]{1,0:T(1,128)S(1)} %get-tuple-element.20.sign_ref, f32[16384,128]{1,0:T(8,128)S(1)} %pair.1.table_ref), custom_call_target="tpu_custom_call" | custom-call | flops 1024 | bytes 1024 | tf_op jit(solution)/shard_map/pick/pallas_call | solution.py:186
  27.4 3.1 %collective-permute-done.2.refs_0_ = f32[1024,128]{1,0:T(8,128)S(1)} collective-permute-done((f32[1024,128]{1,0:T(8,128)S(1)}, f32[1024,128]{1,0:T(8,128)S(1)}, u32[]{:S(2)}, u32[]{:S(2)}) %collective-permute-start.2) | collective-permute-done | bytes 524320 | tf_op jit(solution)/shard_map/ppermute | solution.py:297
  30.6 2.2 %collective-permute-start.3 = (f32[512,128]{1,0:T(8,128)S(1)}, f32[512,128]{1,0:T(8,128)S(1)}, u32[]{:S(2)}, u32[]{:S(2)}) collective-permute-start(f32[512,128]{1,0:T(8,128)S(1)} %slice.97), channel_id=1, source_target_pairs={{0,8},{8,0},{16,24},{24,16},{1,9},{9,1},{17,25},{25,17},{2,10},{10... | collective-permute-start | bytes 786440 | tf_op jit(solution)/shard_map/ppermute | solution.py:298
  32.8 1.8 %pick.10 = f32[1024,128]{1,0:T(8,128)S(1)} custom-call(s32[1,1024]{1,0:T(1,128)S(1)} %get-tuple-element.24.row_ref, f32[1,1024]{1,0:T(1,128)S(1)} %get-tuple-element.25.sign_ref, f32[16384,128]{1,0:T(8,128)S(1)} %pair.1.table_ref), custom_call_target="tpu_custom_call" | custom-call | flops 1024 | bytes 1024 | tf_op jit(solution)/shard_map/pick/pallas_call | solution.py:186
  36.3 1.8 %pick.12 = f32[1024,128]{1,0:T(8,128)S(1)} custom-call(s32[1,1024]{1,0:T(1,128)S(1)} %get-tuple-element.28.row_ref, f32[1,1024]{1,0:T(1,128)S(1)} %get-tuple-element.29.sign_ref, f32[16384,128]{1,0:T(8,128)S(1)} %pair.1.table_ref, f32[1024,128]{1,0:T(8,128)S(1)} %collective-permute-done.2.refs_0_), custom_call_target="tpu_custom_call" | custom-call | flops 1024 | bytes 1024 | tf_op jit(solution)/shard_map/pick/pallas_call | solution.py:186
  38.1 3.2 %collective-permute-done.10 = f32[1024,128]{1,0:T(8,128)S(1)} collective-permute-done((f32[1024,128]{1,0:T(8,128)S(1)}, f32[1024,128]{1,0:T(8,128)S(1)}, u32[]{:S(2)}, u32[]{:S(2)}) %collective-permute-start.10) | collective-permute-done | bytes 524320 | tf_op jit(solution)/shard_map/ppermute | solution.py:297
  41.4 1.8 %collective-permute-start.11 = (f32[512,128]{1,0:T(8,128)S(1)}, f32[512,128]{1,0:T(8,128)S(1)}, u32[]{:S(2)}, u32[]{:S(2)}) collective-permute-start(f32[512,128]{1,0:T(8,128)S(1)} %slice.109), channel_id=1, source_target_pairs={{0,4},{1,5},{2,6},{3,7},{4,0},{5,1},{6,2},{7,3},{8,12},{9,13},{10,... | collective-permute-start | bytes 786440 | tf_op jit(solution)/shard_map/ppermute | solution.py:297
  43.2 1.8 %pick.14 = f32[1024,128]{1,0:T(8,128)S(1)} custom-call(s32[1,1024]{1,0:T(1,128)S(1)} %get-tuple-element.32.row_ref, f32[1,1024]{1,0:T(1,128)S(1)} %get-tuple-element.33.sign_ref, f32[16384,128]{1,0:T(8,128)S(1)} %pair.1.table_ref, f32[1024,128]{1,0:T(8,128)S(1)} %collective-permute-done.6.refs_0_), custom_call_target="tpu_custom_call" | custom-call | flops 1024 | bytes 1024 | tf_op jit(solution)/shard_map/pick/pallas_call | solution.py:186
  47.5 2.1 %collective-permute-start.8 = (f32[256,128]{1,0:T(8,128)S(1)}, f32[256,128]{1,0:T(8,128)S(1)}, u32[]{:S(2)}, u32[]{:S(2)}) collective-permute-start(f32[256,128]{1,0:T(8,128)S(1)} %slice.105), channel_id=1, source_target_pairs={{0,2},{1,3},{2,0},{3,1},{4,6},{5,7},{6,4},{7,5},{8,10},{9,11},{10,... | collective-permute-start | bytes 393224 | tf_op jit(solution)/shard_map/ppermute | solution.py:297
  51.2 1.7 %collective-permute-start.12 = (f32[256,128]{1,0:T(8,128)S(1)}, f32[256,128]{1,0:T(8,128)S(1)}, u32[]{:S(2)}, u32[]{:S(2)}) collective-permute-start(f32[256,128]{1,0:T(8,128)S(1)} %slice.111), channel_id=1, source_target_pairs={{0,8},{8,0},{16,24},{24,16},{1,9},{9,1},{17,25},{25,17},{2,10},{10... | collective-permute-start | bytes 393224 | tf_op jit(solution)/shard_map/ppermute | solution.py:298
  55.6 2.7 %collective-permute-start.5 = (f32[128,128]{1,0:T(8,128)S(1)}, f32[128,128]{1,0:T(8,128)S(1)}, u32[]{:S(2)}, u32[]{:S(2)}) collective-permute-start(f32[128,128]{1,0:T(8,128)S(1)} %slice.101), channel_id=1, source_target_pairs={{0,16},{8,24},{16,0},{24,8},{1,17},{9,25},{17,1},{25,9},{2,18},{10... | collective-permute-start | bytes 196616 | tf_op jit(solution)/shard_map/ppermute | solution.py:298
  58.7 2.7 %collective-permute-start.13 = (f32[128,128]{1,0:T(8,128)S(1)}, f32[128,128]{1,0:T(8,128)S(1)}, u32[]{:S(2)}, u32[]{:S(2)}) collective-permute-start(f32[128,128]{1,0:T(8,128)S(1)} %slice.113), channel_id=1, source_target_pairs={{0,16},{8,24},{16,0},{24,8},{1,17},{9,25},{17,1},{25,9},{2,18},{10... | collective-permute-start | bytes 196616 | tf_op jit(solution)/shard_map/ppermute | solution.py:298
  62.8 2.2 %collective-permute-done.5 = f32[128,128]{1,0:T(8,128)S(1)} collective-permute-done((f32[128,128]{1,0:T(8,128)S(1)}, f32[128,128]{1,0:T(8,128)S(1)}, u32[]{:S(2)}, u32[]{:S(2)}) %collective-permute-start.5) | collective-permute-done | bytes 65568 | tf_op jit(solution)/shard_map/ppermute | solution.py:298
  73.6 1.9 %collective-permute-done.21 = f32[128,128]{1,0:T(8,128)S(1)} collective-permute-done((f32[128,128]{1,0:T(8,128)S(1)}, f32[128,128]{1,0:T(8,128)S(1)}, u32[]{:S(2)}, u32[]{:S(2)}) %collective-permute-start.21) | collective-permute-done | bytes 65568 | tf_op jit(solution)/shard_map/ppermute | solution.py:297
  77.3 5.3 %collective-permute-done.22 = f32[128,128]{1,0:T(8,128)S(1)} collective-permute-done((f32[128,128]{1,0:T(8,128)S(1)}, f32[128,128]{1,0:T(8,128)S(1)}, u32[]{:S(2)}, u32[]{:S(2)}) %collective-permute-start.22) | collective-permute-done | bytes 65568 | tf_op jit(solution)/shard_map/ppermute | solution.py:298
  83.4 3.5 %collective-permute-done.23.far_ref = f32[128,128]{1,0:T(8,128)S(1)} collective-permute-done((f32[128,128]{1,0:T(8,128)S(1)}, f32[128,128]{1,0:T(8,128)S(1)}, u32[]{:S(2)}, u32[]{:S(2)}) %collective-permute-start.23) | collective-permute-done | bytes 65568 | tf_op jit(solution)/shard_map/ppermute | solution.py:298
  87.0 6.1 %finish.1 = (f32[512,128]{1,0:T(8,128)}, f32[128,128]{1,0:T(8,128)}) custom-call(f32[128,128]{1,0:T(8,128)} %copy-done.3, f32[128,128]{1,0:T(8,128)S(1)} %collective-permute-done.23.far_ref, f32[512,128]{1,0:T(8,128)} %pad_maximum_fusion.sketch_ref), custom_call_target="tpu_custom_call" | custom-call | tf_op jit(solution)/shard_map/finish/pallas_call | solution.py:427
  (76 shorter events, 27.2 us)
Async XLA Ops:
  0.6 7.7 %collective-permute-start = (f32[8192,128]{1,0:T(8,128)}, f32[8192,128]{1,0:T(8,128)}, u32[]{:S(2)}, u32[]{:S(2)}) collective-permute-start(f32[8192,128]{1,0:T(8,128)} %x_ref.1), channel_id=1, source_target_pairs={{0,1},{1,0},{2,3},{3,2},{4,5},{5,4},{6,7},{7,6},{8,9},{9,8},{10,11... | collective-permute-start | bytes 12582920 | tf_op jit(solution)/shard_map/ppermute | solution.py:297
  1.1 6.7 %collective-permute-start.1 = (s32[8192]{0:T(1024)}, s32[8192]{0:T(1024)S(1)}, u32[]{:S(2)}, u32[]{:S(2)}) collective-permute-start(s32[8192]{0:T(1024)} %param.5), channel_id=1, source_target_pairs={{0,1},{1,0},{2,3},{3,2},{4,5},{5,4},{6,7},{7,6},{8,9},{9,8},{10,11... | collective-permute-start | bytes 98312 | tf_op jit(solution)/shard_map/ppermute | solution.py:297
  14.9 15.6 %collective-permute-start.2 = (f32[1024,128]{1,0:T(8,128)S(1)}, f32[1024,128]{1,0:T(8,128)S(1)}, u32[]{:S(2)}, u32[]{:S(2)}) collective-permute-start(f32[1024,128]{1,0:T(8,128)S(1)} %pick.9), channel_id=1, source_target_pairs={{0,2},{1,3},{2,0},{3,1},{4,6},{5,7},{6,4},{7,5},{8,10},{9,11},{10,... | collective-permute-start | bytes 1572872 | tf_op jit(solution)/shard_map/ppermute | solution.py:297
  19.7 15.0 %collective-permute-start.6 = (f32[1024,128]{1,0:T(8,128)S(1)}, f32[1024,128]{1,0:T(8,128)S(1)}, u32[]{:S(2)}, u32[]{:S(2)}) collective-permute-start(f32[1024,128]{1,0:T(8,128)S(1)} %pick.11), channel_id=1, source_target_pairs={{0,4},{1,5},{2,6},{3,7},{4,0},{5,1},{6,2},{7,3},{8,12},{9,13},{10,... | collective-permute-start | bytes 1572872 | tf_op jit(solution)/shard_map/ppermute | solution.py:297
  23.1 18.2 %collective-permute-start.10 = (f32[1024,128]{1,0:T(8,128)S(1)}, f32[1024,128]{1,0:T(8,128)S(1)}, u32[]{:S(2)}, u32[]{:S(2)}) collective-permute-start(f32[1024,128]{1,0:T(8,128)S(1)} %pick.13), channel_id=1, source_target_pairs={{0,2},{1,3},{2,0},{3,1},{4,6},{5,7},{6,4},{7,5},{8,10},{9,11},{10,... | collective-permute-start | bytes 1572872 | tf_op jit(solution)/shard_map/ppermute | solution.py:297
  25.5 20.1 %collective-permute-start.14 = (f32[1024,128]{1,0:T(8,128)S(1)}, f32[1024,128]{1,0:T(8,128)S(1)}, u32[]{:S(2)}, u32[]{:S(2)}) collective-permute-start(f32[1024,128]{1,0:T(8,128)S(1)} %pick.15), channel_id=1, source_target_pairs={{0,4},{1,5},{2,6},{3,7},{4,0},{5,1},{6,2},{7,3},{8,12},{9,13},{10,... | collective-permute-start | bytes 1572872 | tf_op jit(solution)/shard_map/ppermute | solution.py:297
  30.6 16.1 %collective-permute-start.3 = (f32[512,128]{1,0:T(8,128)S(1)}, f32[512,128]{1,0:T(8,128)S(1)}, u32[]{:S(2)}, u32[]{:S(2)}) collective-permute-start(f32[512,128]{1,0:T(8,128)S(1)} %slice.97), channel_id=1, source_target_pairs={{0,8},{8,0},{16,24},{24,16},{1,9},{9,1},{17,25},{25,17},{2,10},{10... | collective-permute-start | bytes 786440 | tf_op jit(solution)/shard_map/ppermute | solution.py:298
  34.8 12.7 %collective-permute-start.7 = (f32[512,128]{1,0:T(8,128)S(1)}, f32[512,128]{1,0:T(8,128)S(1)}, u32[]{:S(2)}, u32[]{:S(2)}) collective-permute-start(f32[512,128]{1,0:T(8,128)S(1)} %slice.103), channel_id=1, source_target_pairs={{0,8},{8,0},{16,24},{24,16},{1,9},{9,1},{17,25},{25,17},{2,10},{10... | collective-permute-start | bytes 786440 | tf_op jit(solution)/shard_map/ppermute | solution.py:298
  41.4 9.8 %collective-permute-start.11 = (f32[512,128]{1,0:T(8,128)S(1)}, f32[512,128]{1,0:T(8,128)S(1)}, u32[]{:S(2)}, u32[]{:S(2)}) collective-permute-start(f32[512,128]{1,0:T(8,128)S(1)} %slice.109), channel_id=1, source_target_pairs={{0,4},{1,5},{2,6},{3,7},{4,0},{5,1},{6,2},{7,3},{8,12},{9,13},{10,... | collective-permute-start | bytes 786440 | tf_op jit(solution)/shard_map/ppermute | solution.py:297
  45.6 8.2 %collective-permute-start.15 = (f32[512,128]{1,0:T(8,128)S(1)}, f32[512,128]{1,0:T(8,128)S(1)}, u32[]{:S(2)}, u32[]{:S(2)}) collective-permute-start(f32[512,128]{1,0:T(8,128)S(1)} %slice.115), channel_id=1, source_target_pairs={{0,2},{1,3},{2,0},{3,1},{4,6},{5,7},{6,4},{7,5},{8,10},{9,11},{10,... | collective-permute-start | bytes 786440 | tf_op jit(solution)/shard_map/ppermute | solution.py:297
  46.8 8.8 %collective-permute-start.4 = (f32[256,128]{1,0:T(8,128)S(1)}, f32[256,128]{1,0:T(8,128)S(1)}, u32[]{:S(2)}, u32[]{:S(2)}) collective-permute-start(f32[256,128]{1,0:T(8,128)S(1)} %slice.99), channel_id=1, source_target_pairs={{0,4},{1,5},{2,6},{3,7},{4,0},{5,1},{6,2},{7,3},{8,12},{9,13},{10,... | collective-permute-start | bytes 393224 | tf_op jit(solution)/shard_map/ppermute | solution.py:297
  47.5 10.7 %collective-permute-start.8 = (f32[256,128]{1,0:T(8,128)S(1)}, f32[256,128]{1,0:T(8,128)S(1)}, u32[]{:S(2)}, u32[]{:S(2)}) collective-permute-start(f32[256,128]{1,0:T(8,128)S(1)} %slice.105), channel_id=1, source_target_pairs={{0,2},{1,3},{2,0},{3,1},{4,6},{5,7},{6,4},{7,5},{8,10},{9,11},{10,... | collective-permute-start | bytes 393224 | tf_op jit(solution)/shard_map/ppermute | solution.py:297
  51.2 7.5 %collective-permute-start.12 = (f32[256,128]{1,0:T(8,128)S(1)}, f32[256,128]{1,0:T(8,128)S(1)}, u32[]{:S(2)}, u32[]{:S(2)}) collective-permute-start(f32[256,128]{1,0:T(8,128)S(1)} %slice.111), channel_id=1, source_target_pairs={{0,8},{8,0},{16,24},{24,16},{1,9},{9,1},{17,25},{25,17},{2,10},{10... | collective-permute-start | bytes 393224 | tf_op jit(solution)/shard_map/ppermute | solution.py:298
  53.9 7.5 %collective-permute-start.16 = (f32[256,128]{1,0:T(8,128)S(1)}, f32[256,128]{1,0:T(8,128)S(1)}, u32[]{:S(2)}, u32[]{:S(2)}) collective-permute-start(f32[256,128]{1,0:T(8,128)S(1)} %slice.117), channel_id=1, source_target_pairs={{0,8},{8,0},{16,24},{24,16},{1,9},{9,1},{17,25},{25,17},{2,10},{10... | collective-permute-start | bytes 393224 | tf_op jit(solution)/shard_map/ppermute | solution.py:298
  55.6 9.5 %collective-permute-start.5 = (f32[128,128]{1,0:T(8,128)S(1)}, f32[128,128]{1,0:T(8,128)S(1)}, u32[]{:S(2)}, u32[]{:S(2)}) collective-permute-start(f32[128,128]{1,0:T(8,128)S(1)} %slice.101), channel_id=1, source_target_pairs={{0,16},{8,24},{16,0},{24,8},{1,17},{9,25},{17,1},{25,9},{2,18},{10... | collective-permute-start | bytes 196616 | tf_op jit(solution)/shard_map/ppermute | solution.py:298
  58.3 8.4 %collective-permute-start.9 = (f32[128,128]{1,0:T(8,128)S(1)}, f32[128,128]{1,0:T(8,128)S(1)}, u32[]{:S(2)}, u32[]{:S(2)}) collective-permute-start(f32[128,128]{1,0:T(8,128)S(1)} %slice.107), channel_id=1, source_target_pairs={{0,16},{8,24},{16,0},{24,8},{1,17},{9,25},{17,1},{25,9},{2,18},{10... | collective-permute-start | bytes 196616 | tf_op jit(solution)/shard_map/ppermute | solution.py:298
  58.7 8.7 %collective-permute-start.13 = (f32[128,128]{1,0:T(8,128)S(1)}, f32[128,128]{1,0:T(8,128)S(1)}, u32[]{:S(2)}, u32[]{:S(2)}) collective-permute-start(f32[128,128]{1,0:T(8,128)S(1)} %slice.113), channel_id=1, source_target_pairs={{0,16},{8,24},{16,0},{24,8},{1,17},{9,25},{17,1},{25,9},{2,18},{10... | collective-permute-start | bytes 196616 | tf_op jit(solution)/shard_map/ppermute | solution.py:298
  61.4 6.7 %collective-permute-start.17 = (f32[128,128]{1,0:T(8,128)S(1)}, f32[128,128]{1,0:T(8,128)S(1)}, u32[]{:S(2)}, u32[]{:S(2)}) collective-permute-start(f32[128,128]{1,0:T(8,128)S(1)} %slice.119), channel_id=1, source_target_pairs={{0,16},{8,24},{16,0},{24,8},{1,17},{9,25},{17,1},{25,9},{2,18},{10... | collective-permute-start | bytes 196616 | tf_op jit(solution)/shard_map/ppermute | solution.py:298
  68.7 1.3 %collective-permute-start.18 = (f32[128,128]{1,0:T(8,128)S(1)}, f32[128,128]{1,0:T(8,128)S(1)}, u32[]{:S(2)}, u32[]{:S(2)}) collective-permute-start(f32[128,128]{1,0:T(8,128)S(1)} %convolution_multiply_fusion), channel_id=1, source_target_pairs={{0,1},{1,0},{2,3},{3,2},{4,5},{5,4},{6,7},{7,6},{8,9},{9,8},{10,11... | collective-permute-start | bytes 196616 | tf_op jit(solution)/shard_map/ppermute | solution.py:297
  70.0 5.5 %collective-permute-start.21 = (f32[128,128]{1,0:T(8,128)S(1)}, f32[128,128]{1,0:T(8,128)S(1)}, u32[]{:S(2)}, u32[]{:S(2)}) collective-permute-start(f32[128,128]{1,0:T(8,128)S(1)} %add.83), channel_id=1, source_target_pairs={{0,6},{1,7},{2,4},{3,5},{4,2},{5,3},{6,0},{7,1},{8,14},{9,15},{10,... | collective-permute-start | bytes 196616 | tf_op jit(solution)/shard_map/ppermute | solution.py:297
  71.4 5.1 %collective-permute-start.20 = (f32[128,128]{1,0:T(8,128)S(1)}, f32[128,128]{1,0:T(8,128)S(1)}, u32[]{:S(2)}, u32[]{:S(2)}) collective-permute-start(f32[128,128]{1,0:T(8,128)S(1)} %add.83), channel_id=1, source_target_pairs={{0,4},{1,5},{2,6},{3,7},{4,0},{5,1},{6,2},{7,3},{8,12},{9,13},{10,... | collective-permute-start | bytes 196616 | tf_op jit(solution)/shard_map/ppermute | solution.py:297
  73.0 4.3 %collective-permute-start.19 = (f32[128,128]{1,0:T(8,128)S(1)}, f32[128,128]{1,0:T(8,128)S(1)}, u32[]{:S(2)}, u32[]{:S(2)}) collective-permute-start(f32[128,128]{1,0:T(8,128)S(1)} %add.83), channel_id=1, source_target_pairs={{0,2},{1,3},{2,0},{3,1},{4,6},{5,7},{6,4},{7,5},{8,10},{9,11},{10,... | collective-permute-start | bytes 196616 | tf_op jit(solution)/shard_map/ppermute | solution.py:297
  77.3 5.4 %collective-permute-start.22 = (f32[128,128]{1,0:T(8,128)S(1)}, f32[128,128]{1,0:T(8,128)S(1)}, u32[]{:S(2)}, u32[]{:S(2)}) collective-permute-start(f32[128,128]{1,0:T(8,128)S(1)} %add_add_fusion), channel_id=1, source_target_pairs={{0,16},{8,24},{16,0},{24,8},{1,17},{9,25},{17,1},{25,9},{2,18},{10... | collective-permute-start | bytes 196616 | tf_op jit(solution)/shard_map/ppermute | solution.py:298
  82.6 4.3 %collective-permute-start.23 = (f32[128,128]{1,0:T(8,128)S(1)}, f32[128,128]{1,0:T(8,128)S(1)}, u32[]{:S(2)}, u32[]{:S(2)}) collective-permute-start(f32[128,128]{1,0:T(8,128)S(1)} %add.87.gram_ref), channel_id=1, source_target_pairs={{0,8},{8,0},{16,24},{24,16},{1,9},{9,1},{17,25},{25,17},{2,10},{10... | collective-permute-start | bytes 196616 | tf_op jit(solution)/shard_map/ppermute | solution.py:298
  (4 other events, 6.8 us)

commit v7 on v6

--- a/solution.py
+++ b/solution.py
@@ -126,7 +126,7 @@
             emit(BLOCK * h + row, part)
         return carry
 
-    lax.fori_loop(0, BLOCK // SUB, across, 0, unroll=4)
+    lax.fori_loop(0, BLOCK // SUB, across, 0, unroll=8)
 
 
 def own_kernel(
@@ -167,7 +167,7 @@
 def pick_kernel(row_ref, sign_ref, table_ref, *refs):
     out_ref = refs[-1]
     count = out_ref.shape[0]
-    unroll = math.gcd(count, 64)
+    unroll = math.gcd(count, 128)
 
     def some(i, carry):
         for u in range(unroll):

time: 93.4 us -> 93.2 us (level)
  no operation moved by 1% of the time
where the time goes in v7:
time: 93.2 us; the launch traced here: 92.9 us
  starting transfers between devices  29.5 us (32%)
  Pallas kernels  29.1 us (31%)
  waiting for transfers between devices  29 us (31%)
  local copies, waits for them, and re-layouts  2.58 us (3%)
  other arithmetic  1.23 us (1%)
  between operations  0.94 us (1%)
    ppermute x14, starting transfers between devices, swap(): return lax.ppermute(value, 'exb', bit_perm(n_inner, mask))  15.1 us
    ppermute x14, waiting for transfers between devices, swap(): return lax.ppermute(value, 'exb', bit_perm(n_inner, mask))  15 us
    ppermute x10, starting transfers between devices, swap(): return lax.ppermute(value, 'exa', bit_perm(n_outer, mask // n_inner))  14.4 us
    pallas_call x8, Pallas kernels, pick(): pl.pallas_call(pick_kernel, out_shape=jax.ShapeDtypeStruct((count, table....  14.2 us
    ppermute x10, waiting for transfers between devices, swap(): return lax.ppermute(value, 'exa', bit_perm(n_outer, mask // n_inner))  14.1 us
    pallas_call x1, Pallas kernels, per_device(): pl.pallas_call(finish_kernel, out_shape=(jax.ShapeDtypeStruct((own_count,...  6.15 us
    pallas_call x1, Pallas kernels, per_device(): pl.pallas_call(pair_kernel, out_shape=jax.ShapeDtypeStruct((2 * rows_dev,...  4.6 us
    pallas_call x1, Pallas kernels, per_device(): pl.pallas_call(functools.partial(own_kernel, 1.0 / math.sqrt(rows_dev * n...  4.09 us
  transfers between devices with their start and end apart: 24, of which 16 were waited for; matrix products, arithmetic and copies ran while one was open for 1% of the time, Pallas kernels for 18%

profile of v7, /device:TPU:0, one launch (start us, length us, event | category | flops | bytes accessed | tf_op | source)
XLA Modules:
  0.0 92.9 jit_solution(8747987953451232916)
XLA Ops:
  3.7 4.1 %own.1 = (f32[8192,128]{1,0:T(8,128)S(1)}, s32[1,1024]{1,0:T(1,128)S(1)}, f32[1,1024]{1,0:T(1,128)S(1)}, s32[1,1024]{1,0:T(1,128)S(1)}, f32[1,1024]{1,0:T(1,128)...) custom-call(f32[8192,128]{1,0:T(8,128)} %x_ref.1, ...), custom_call_target="tpu_custom_call" | custom-call | flops 10000000 | bytes 12582912 | tf_op jit(solution)/shard_map/own/pallas_call | solution.py:349
  8.3 4.6 %pair.1.table_ref = f32[16384,128]{1,0:T(8,128)S(1)} custom-call(f32[8192,128]{1,0:T(8,128)} %collective-permute-done.x_ref, s32[64,128]{1,0:T(8,128)S(1)} %bitcast.8, f32[8192,128]{1,0:T(8,128)S(1)} %get-tuple-element.21.own_ref), custom_call_target="tpu_custom_call" | custom-call | flops 10000000 | bytes 16777216 | tf_op jit(solution)/shard_map/pair/pallas_call | solution.py:371
  12.9 1.8 %pick.9 = f32[1024,128]{1,0:T(8,128)S(1)} custom-call(s32[1,1024]{1,0:T(1,128)S(1)} %get-tuple-element.22.row_ref, f32[1,1024]{1,0:T(1,128)S(1)} %get-tuple-element.23.sign_ref, f32[16384,128]{1,0:T(8,128)S(1)} %pair.1.table_ref), custom_call_target="tpu_custom_call" | custom-call | flops 1024 | bytes 1024 | tf_op jit(solution)/shard_map/pick/pallas_call | solution.py:186
  14.7 2.9 %collective-permute-start.2 = (f32[1024,128]{1,0:T(8,128)S(1)}, f32[1024,128]{1,0:T(8,128)S(1)}, u32[]{:S(2)}, u32[]{:S(2)}) collective-permute-start(f32[1024,128]{1,0:T(8,128)S(1)} %pick.9), channel_id=1, source_target_pairs={{0,2},{1,3},{2,0},{3,1},{4,6},{5,7},{6,4},{7,5},{8,10},{9,11},{10,... | collective-permute-start | bytes 1572872 | tf_op jit(solution)/shard_map/ppermute | solution.py:297
  17.6 1.8 %pick.11 = f32[1024,128]{1,0:T(8,128)S(1)} custom-call(s32[1,1024]{1,0:T(1,128)S(1)} %get-tuple-element.26.row_ref, f32[1,1024]{1,0:T(1,128)S(1)} %get-tuple-element.27.sign_ref, f32[16384,128]{1,0:T(8,128)S(1)} %pair.1.table_ref), custom_call_target="tpu_custom_call" | custom-call | flops 1024 | bytes 1024 | tf_op jit(solution)/shard_map/pick/pallas_call | solution.py:186
  21.0 1.8 %pick.13 = f32[1024,128]{1,0:T(8,128)S(1)} custom-call(s32[1,1024]{1,0:T(1,128)S(1)} %get-tuple-element.30.row_ref, f32[1,1024]{1,0:T(1,128)S(1)} %get-tuple-element.31.sign_ref, f32[16384,128]{1,0:T(8,128)S(1)} %pair.1.table_ref), custom_call_target="tpu_custom_call" | custom-call | flops 1024 | bytes 1024 | tf_op jit(solution)/shard_map/pick/pallas_call | solution.py:186
  23.4 1.8 %pick.15 = f32[1024,128]{1,0:T(8,128)S(1)} custom-call(s32[1,1024]{1,0:T(1,128)S(1)} %get-tuple-element.34.row_ref, f32[1,1024]{1,0:T(1,128)S(1)} %get-tuple-element.35.sign_ref, f32[16384,128]{1,0:T(8,128)S(1)} %pair.1.table_ref), custom_call_target="tpu_custom_call" | custom-call | flops 1024 | bytes 1024 | tf_op jit(solution)/shard_map/pick/pallas_call | solution.py:186
  25.3 1.8 %pick.8 = f32[1024,128]{1,0:T(8,128)S(1)} custom-call(s32[1,1024]{1,0:T(1,128)S(1)} %get-tuple-element.19.row_ref, f32[1,1024]{1,0:T(1,128)S(1)} %get-tuple-element.20.sign_ref, f32[16384,128]{1,0:T(8,128)S(1)} %pair.1.table_ref), custom_call_target="tpu_custom_call" | custom-call | flops 1024 | bytes 1024 | tf_op jit(solution)/shard_map/pick/pallas_call | solution.py:186
  27.1 3.3 %collective-permute-done.2.refs_0_ = f32[1024,128]{1,0:T(8,128)S(1)} collective-permute-done((f32[1024,128]{1,0:T(8,128)S(1)}, f32[1024,128]{1,0:T(8,128)S(1)}, u32[]{:S(2)}, u32[]{:S(2)}) %collective-permute-start.2) | collective-permute-done | bytes 524320 | tf_op jit(solution)/shard_map/ppermute | solution.py:297
  30.4 2.2 %collective-permute-start.3 = (f32[512,128]{1,0:T(8,128)S(1)}, f32[512,128]{1,0:T(8,128)S(1)}, u32[]{:S(2)}, u32[]{:S(2)}) collective-permute-start(f32[512,128]{1,0:T(8,128)S(1)} %slice.97), channel_id=1, source_target_pairs={{0,8},{8,0},{16,24},{24,16},{1,9},{9,1},{17,25},{25,17},{2,10},{10... | collective-permute-start | bytes 786440 | tf_op jit(solution)/shard_map/ppermute | solution.py:298
  32.6 1.8 %pick.10 = f32[1024,128]{1,0:T(8,128)S(1)} custom-call(s32[1,1024]{1,0:T(1,128)S(1)} %get-tuple-element.24.row_ref, f32[1,1024]{1,0:T(1,128)S(1)} %get-tuple-element.25.sign_ref, f32[16384,128]{1,0:T(8,128)S(1)} %pair.1.table_ref), custom_call_target="tpu_custom_call" | custom-call | flops 1024 | bytes 1024 | tf_op jit(solution)/shard_map/pick/pallas_call | solution.py:186
  36.0 1.8 %pick.12 = f32[1024,128]{1,0:T(8,128)S(1)} custom-call(s32[1,1024]{1,0:T(1,128)S(1)} %get-tuple-element.28.row_ref, f32[1,1024]{1,0:T(1,128)S(1)} %get-tuple-element.29.sign_ref, f32[16384,128]{1,0:T(8,128)S(1)} %pair.1.table_ref, f32[1024,128]{1,0:T(8,128)S(1)} %collective-permute-done.2.refs_0_), custom_call_target="tpu_custom_call" | custom-call | flops 1024 | bytes 1024 | tf_op jit(solution)/shard_map/pick/pallas_call | solution.py:186
  37.8 3.3 %collective-permute-done.10 = f32[1024,128]{1,0:T(8,128)S(1)} collective-permute-done((f32[1024,128]{1,0:T(8,128)S(1)}, f32[1024,128]{1,0:T(8,128)S(1)}, u32[]{:S(2)}, u32[]{:S(2)}) %collective-permute-start.10) | collective-permute-done | bytes 524320 | tf_op jit(solution)/shard_map/ppermute | solution.py:297
  41.2 1.8 %collective-permute-start.11 = (f32[512,128]{1,0:T(8,128)S(1)}, f32[512,128]{1,0:T(8,128)S(1)}, u32[]{:S(2)}, u32[]{:S(2)}) collective-permute-start(f32[512,128]{1,0:T(8,128)S(1)} %slice.109), channel_id=1, source_target_pairs={{0,4},{1,5},{2,6},{3,7},{4,0},{5,1},{6,2},{7,3},{8,12},{9,13},{10,... | collective-permute-start | bytes 786440 | tf_op jit(solution)/shard_map/ppermute | solution.py:297
  43.0 1.8 %pick.14 = f32[1024,128]{1,0:T(8,128)S(1)} custom-call(s32[1,1024]{1,0:T(1,128)S(1)} %get-tuple-element.32.row_ref, f32[1,1024]{1,0:T(1,128)S(1)} %get-tuple-element.33.sign_ref, f32[16384,128]{1,0:T(8,128)S(1)} %pair.1.table_ref, f32[1024,128]{1,0:T(8,128)S(1)} %collective-permute-done.6.refs_0_), custom_call_target="tpu_custom_call" | custom-call | flops 1024 | bytes 1024 | tf_op jit(solution)/shard_map/pick/pallas_call | solution.py:186
  47.2 2.1 %collective-permute-start.8 = (f32[256,128]{1,0:T(8,128)S(1)}, f32[256,128]{1,0:T(8,128)S(1)}, u32[]{:S(2)}, u32[]{:S(2)}) collective-permute-start(f32[256,128]{1,0:T(8,128)S(1)} %slice.105), channel_id=1, source_target_pairs={{0,2},{1,3},{2,0},{3,1},{4,6},{5,7},{6,4},{7,5},{8,10},{9,11},{10,... | collective-permute-start | bytes 393224 | tf_op jit(solution)/shard_map/ppermute | solution.py:297
  51.0 1.7 %collective-permute-start.12 = (f32[256,128]{1,0:T(8,128)S(1)}, f32[256,128]{1,0:T(8,128)S(1)}, u32[]{:S(2)}, u32[]{:S(2)}) collective-permute-start(f32[256,128]{1,0:T(8,128)S(1)} %slice.111), channel_id=1, source_target_pairs={{0,8},{8,0},{16,24},{24,16},{1,9},{9,1},{17,25},{25,17},{2,10},{10... | collective-permute-start | bytes 393224 | tf_op jit(solution)/shard_map/ppermute | solution.py:298
  55.4 2.7 %collective-permute-start.5 = (f32[128,128]{1,0:T(8,128)S(1)}, f32[128,128]{1,0:T(8,128)S(1)}, u32[]{:S(2)}, u32[]{:S(2)}) collective-permute-start(f32[128,128]{1,0:T(8,128)S(1)} %slice.101), channel_id=1, source_target_pairs={{0,16},{8,24},{16,0},{24,8},{1,17},{9,25},{17,1},{25,9},{2,18},{10... | collective-permute-start | bytes 196616 | tf_op jit(solution)/shard_map/ppermute | solution.py:298
  58.5 2.7 %collective-permute-start.13 = (f32[128,128]{1,0:T(8,128)S(1)}, f32[128,128]{1,0:T(8,128)S(1)}, u32[]{:S(2)}, u32[]{:S(2)}) collective-permute-start(f32[128,128]{1,0:T(8,128)S(1)} %slice.113), channel_id=1, source_target_pairs={{0,16},{8,24},{16,0},{24,8},{1,17},{9,25},{17,1},{25,9},{2,18},{10... | collective-permute-start | bytes 196616 | tf_op jit(solution)/shard_map/ppermute | solution.py:298
  62.7 2.3 %collective-permute-done.5 = f32[128,128]{1,0:T(8,128)S(1)} collective-permute-done((f32[128,128]{1,0:T(8,128)S(1)}, f32[128,128]{1,0:T(8,128)S(1)}, u32[]{:S(2)}, u32[]{:S(2)}) %collective-permute-start.5) | collective-permute-done | bytes 65568 | tf_op jit(solution)/shard_map/ppermute | solution.py:298
  73.4 2.0 %collective-permute-done.21 = f32[128,128]{1,0:T(8,128)S(1)} collective-permute-done((f32[128,128]{1,0:T(8,128)S(1)}, f32[128,128]{1,0:T(8,128)S(1)}, u32[]{:S(2)}, u32[]{:S(2)}) %collective-permute-start.21) | collective-permute-done | bytes 65568 | tf_op jit(solution)/shard_map/ppermute | solution.py:297
  77.1 5.3 %collective-permute-done.22 = f32[128,128]{1,0:T(8,128)S(1)} collective-permute-done((f32[128,128]{1,0:T(8,128)S(1)}, f32[128,128]{1,0:T(8,128)S(1)}, u32[]{:S(2)}, u32[]{:S(2)}) %collective-permute-start.22) | collective-permute-done | bytes 65568 | tf_op jit(solution)/shard_map/ppermute | solution.py:298
  83.3 3.5 %collective-permute-done.23.far_ref = f32[128,128]{1,0:T(8,128)S(1)} collective-permute-done((f32[128,128]{1,0:T(8,128)S(1)}, f32[128,128]{1,0:T(8,128)S(1)}, u32[]{:S(2)}, u32[]{:S(2)}) %collective-permute-start.23) | collective-permute-done | bytes 65568 | tf_op jit(solution)/shard_map/ppermute | solution.py:298
  86.8 6.1 %finish.1 = (f32[512,128]{1,0:T(8,128)}, f32[128,128]{1,0:T(8,128)}) custom-call(f32[128,128]{1,0:T(8,128)} %copy-done.3, f32[128,128]{1,0:T(8,128)S(1)} %collective-permute-done.23.far_ref, f32[512,128]{1,0:T(8,128)} %pad_maximum_fusion.sketch_ref), custom_call_target="tpu_custom_call" | custom-call | tf_op jit(solution)/shard_map/finish/pallas_call | solution.py:427
  (76 shorter events, 27.1 us)
Async XLA Ops:
  0.6 7.7 %collective-permute-start = (f32[8192,128]{1,0:T(8,128)}, f32[8192,128]{1,0:T(8,128)}, u32[]{:S(2)}, u32[]{:S(2)}) collective-permute-start(f32[8192,128]{1,0:T(8,128)} %x_ref.1), channel_id=1, source_target_pairs={{0,1},{1,0},{2,3},{3,2},{4,5},{5,4},{6,7},{7,6},{8,9},{9,8},{10,11... | collective-permute-start | bytes 12582920 | tf_op jit(solution)/shard_map/ppermute | solution.py:297
  1.1 6.6 %collective-permute-start.1 = (s32[8192]{0:T(1024)}, s32[8192]{0:T(1024)S(1)}, u32[]{:S(2)}, u32[]{:S(2)}) collective-permute-start(s32[8192]{0:T(1024)} %param.5), channel_id=1, source_target_pairs={{0,1},{1,0},{2,3},{3,2},{4,5},{5,4},{6,7},{7,6},{8,9},{9,8},{10,11... | collective-permute-start | bytes 98312 | tf_op jit(solution)/shard_map/ppermute | solution.py:297
  14.7 15.6 %collective-permute-start.2 = (f32[1024,128]{1,0:T(8,128)S(1)}, f32[1024,128]{1,0:T(8,128)S(1)}, u32[]{:S(2)}, u32[]{:S(2)}) collective-permute-start(f32[1024,128]{1,0:T(8,128)S(1)} %pick.9), channel_id=1, source_target_pairs={{0,2},{1,3},{2,0},{3,1},{4,6},{5,7},{6,4},{7,5},{8,10},{9,11},{10,... | collective-permute-start | bytes 1572872 | tf_op jit(solution)/shard_map/ppermute | solution.py:297
  19.4 15.0 %collective-permute-start.6 = (f32[1024,128]{1,0:T(8,128)S(1)}, f32[1024,128]{1,0:T(8,128)S(1)}, u32[]{:S(2)}, u32[]{:S(2)}) collective-permute-start(f32[1024,128]{1,0:T(8,128)S(1)} %pick.11), channel_id=1, source_target_pairs={{0,4},{1,5},{2,6},{3,7},{4,0},{5,1},{6,2},{7,3},{8,12},{9,13},{10,... | collective-permute-start | bytes 1572872 | tf_op jit(solution)/shard_map/ppermute | solution.py:297
  22.8 18.3 %collective-permute-start.10 = (f32[1024,128]{1,0:T(8,128)S(1)}, f32[1024,128]{1,0:T(8,128)S(1)}, u32[]{:S(2)}, u32[]{:S(2)}) collective-permute-start(f32[1024,128]{1,0:T(8,128)S(1)} %pick.13), channel_id=1, source_target_pairs={{0,2},{1,3},{2,0},{3,1},{4,6},{5,7},{6,4},{7,5},{8,10},{9,11},{10,... | collective-permute-start | bytes 1572872 | tf_op jit(solution)/shard_map/ppermute | solution.py:297
  25.2 20.1 %collective-permute-start.14 = (f32[1024,128]{1,0:T(8,128)S(1)}, f32[1024,128]{1,0:T(8,128)S(1)}, u32[]{:S(2)}, u32[]{:S(2)}) collective-permute-start(f32[1024,128]{1,0:T(8,128)S(1)} %pick.15), channel_id=1, source_target_pairs={{0,4},{1,5},{2,6},{3,7},{4,0},{5,1},{6,2},{7,3},{8,12},{9,13},{10,... | collective-permute-start | bytes 1572872 | tf_op jit(solution)/shard_map/ppermute | solution.py:297
  30.4 16.0 %collective-permute-start.3 = (f32[512,128]{1,0:T(8,128)S(1)}, f32[512,128]{1,0:T(8,128)S(1)}, u32[]{:S(2)}, u32[]{:S(2)}) collective-permute-start(f32[512,128]{1,0:T(8,128)S(1)} %slice.97), channel_id=1, source_target_pairs={{0,8},{8,0},{16,24},{24,16},{1,9},{9,1},{17,25},{25,17},{2,10},{10... | collective-permute-start | bytes 786440 | tf_op jit(solution)/shard_map/ppermute | solution.py:298
  34.5 12.6 %collective-permute-start.7 = (f32[512,128]{1,0:T(8,128)S(1)}, f32[512,128]{1,0:T(8,128)S(1)}, u32[]{:S(2)}, u32[]{:S(2)}) collective-permute-start(f32[512,128]{1,0:T(8,128)S(1)} %slice.103), channel_id=1, source_target_pairs={{0,8},{8,0},{16,24},{24,16},{1,9},{9,1},{17,25},{25,17},{2,10},{10... | collective-permute-start | bytes 786440 | tf_op jit(solution)/shard_map/ppermute | solution.py:298
  41.2 9.7 %collective-permute-start.11 = (f32[512,128]{1,0:T(8,128)S(1)}, f32[512,128]{1,0:T(8,128)S(1)}, u32[]{:S(2)}, u32[]{:S(2)}) collective-permute-start(f32[512,128]{1,0:T(8,128)S(1)} %slice.109), channel_id=1, source_target_pairs={{0,4},{1,5},{2,6},{3,7},{4,0},{5,1},{6,2},{7,3},{8,12},{9,13},{10,... | collective-permute-start | bytes 786440 | tf_op jit(solution)/shard_map/ppermute | solution.py:297
  45.4 8.2 %collective-permute-start.15 = (f32[512,128]{1,0:T(8,128)S(1)}, f32[512,128]{1,0:T(8,128)S(1)}, u32[]{:S(2)}, u32[]{:S(2)}) collective-permute-start(f32[512,128]{1,0:T(8,128)S(1)} %slice.115), channel_id=1, source_target_pairs={{0,2},{1,3},{2,0},{3,1},{4,6},{5,7},{6,4},{7,5},{8,10},{9,11},{10,... | collective-permute-start | bytes 786440 | tf_op jit(solution)/shard_map/ppermute | solution.py:297
  46.5 8.8 %collective-permute-start.4 = (f32[256,128]{1,0:T(8,128)S(1)}, f32[256,128]{1,0:T(8,128)S(1)}, u32[]{:S(2)}, u32[]{:S(2)}) collective-permute-start(f32[256,128]{1,0:T(8,128)S(1)} %slice.99), channel_id=1, source_target_pairs={{0,4},{1,5},{2,6},{3,7},{4,0},{5,1},{6,2},{7,3},{8,12},{9,13},{10,... | collective-permute-start | bytes 393224 | tf_op jit(solution)/shard_map/ppermute | solution.py:297
  47.2 10.8 %collective-permute-start.8 = (f32[256,128]{1,0:T(8,128)S(1)}, f32[256,128]{1,0:T(8,128)S(1)}, u32[]{:S(2)}, u32[]{:S(2)}) collective-permute-start(f32[256,128]{1,0:T(8,128)S(1)} %slice.105), channel_id=1, source_target_pairs={{0,2},{1,3},{2,0},{3,1},{4,6},{5,7},{6,4},{7,5},{8,10},{9,11},{10,... | collective-permute-start | bytes 393224 | tf_op jit(solution)/shard_map/ppermute | solution.py:297
  51.0 7.5 %collective-permute-start.12 = (f32[256,128]{1,0:T(8,128)S(1)}, f32[256,128]{1,0:T(8,128)S(1)}, u32[]{:S(2)}, u32[]{:S(2)}) collective-permute-start(f32[256,128]{1,0:T(8,128)S(1)} %slice.111), channel_id=1, source_target_pairs={{0,8},{8,0},{16,24},{24,16},{1,9},{9,1},{17,25},{25,17},{2,10},{10... | collective-permute-start | bytes 393224 | tf_op jit(solution)/shard_map/ppermute | solution.py:298
  53.7 7.5 %collective-permute-start.16 = (f32[256,128]{1,0:T(8,128)S(1)}, f32[256,128]{1,0:T(8,128)S(1)}, u32[]{:S(2)}, u32[]{:S(2)}) collective-permute-start(f32[256,128]{1,0:T(8,128)S(1)} %slice.117), channel_id=1, source_target_pairs={{0,8},{8,0},{16,24},{24,16},{1,9},{9,1},{17,25},{25,17},{2,10},{10... | collective-permute-start | bytes 393224 | tf_op jit(solution)/shard_map/ppermute | solution.py:298
  55.4 9.6 %collective-permute-start.5 = (f32[128,128]{1,0:T(8,128)S(1)}, f32[128,128]{1,0:T(8,128)S(1)}, u32[]{:S(2)}, u32[]{:S(2)}) collective-permute-start(f32[128,128]{1,0:T(8,128)S(1)} %slice.101), channel_id=1, source_target_pairs={{0,16},{8,24},{16,0},{24,8},{1,17},{9,25},{17,1},{25,9},{2,18},{10... | collective-permute-start | bytes 196616 | tf_op jit(solution)/shard_map/ppermute | solution.py:298
  58.1 8.5 %collective-permute-start.9 = (f32[128,128]{1,0:T(8,128)S(1)}, f32[128,128]{1,0:T(8,128)S(1)}, u32[]{:S(2)}, u32[]{:S(2)}) collective-permute-start(f32[128,128]{1,0:T(8,128)S(1)} %slice.107), channel_id=1, source_target_pairs={{0,16},{8,24},{16,0},{24,8},{1,17},{9,25},{17,1},{25,9},{2,18},{10... | collective-permute-start | bytes 196616 | tf_op jit(solution)/shard_map/ppermute | solution.py:298
  58.5 8.7 %collective-permute-start.13 = (f32[128,128]{1,0:T(8,128)S(1)}, f32[128,128]{1,0:T(8,128)S(1)}, u32[]{:S(2)}, u32[]{:S(2)}) collective-permute-start(f32[128,128]{1,0:T(8,128)S(1)} %slice.113), channel_id=1, source_target_pairs={{0,16},{8,24},{16,0},{24,8},{1,17},{9,25},{17,1},{25,9},{2,18},{10... | collective-permute-start | bytes 196616 | tf_op jit(solution)/shard_map/ppermute | solution.py:298
  61.2 6.8 %collective-permute-start.17 = (f32[128,128]{1,0:T(8,128)S(1)}, f32[128,128]{1,0:T(8,128)S(1)}, u32[]{:S(2)}, u32[]{:S(2)}) collective-permute-start(f32[128,128]{1,0:T(8,128)S(1)} %slice.119), channel_id=1, source_target_pairs={{0,16},{8,24},{16,0},{24,8},{1,17},{9,25},{17,1},{25,9},{2,18},{10... | collective-permute-start | bytes 196616 | tf_op jit(solution)/shard_map/ppermute | solution.py:298
  68.6 1.3 %collective-permute-start.18 = (f32[128,128]{1,0:T(8,128)S(1)}, f32[128,128]{1,0:T(8,128)S(1)}, u32[]{:S(2)}, u32[]{:S(2)}) collective-permute-start(f32[128,128]{1,0:T(8,128)S(1)} %convolution_multiply_fusion), channel_id=1, source_target_pairs={{0,1},{1,0},{2,3},{3,2},{4,5},{5,4},{6,7},{7,6},{8,9},{9,8},{10,11... | collective-permute-start | bytes 196616 | tf_op jit(solution)/shard_map/ppermute | solution.py:297
  69.9 5.6 %collective-permute-start.21 = (f32[128,128]{1,0:T(8,128)S(1)}, f32[128,128]{1,0:T(8,128)S(1)}, u32[]{:S(2)}, u32[]{:S(2)}) collective-permute-start(f32[128,128]{1,0:T(8,128)S(1)} %add.83), channel_id=1, source_target_pairs={{0,6},{1,7},{2,4},{3,5},{4,2},{5,3},{6,0},{7,1},{8,14},{9,15},{10,... | collective-permute-start | bytes 196616 | tf_op jit(solution)/shard_map/ppermute | solution.py:297
  71.2 5.2 %collective-permute-start.20 = (f32[128,128]{1,0:T(8,128)S(1)}, f32[128,128]{1,0:T(8,128)S(1)}, u32[]{:S(2)}, u32[]{:S(2)}) collective-permute-start(f32[128,128]{1,0:T(8,128)S(1)} %add.83), channel_id=1, source_target_pairs={{0,4},{1,5},{2,6},{3,7},{4,0},{5,1},{6,2},{7,3},{8,12},{9,13},{10,... | collective-permute-start | bytes 196616 | tf_op jit(solution)/shard_map/ppermute | solution.py:297
  72.7 4.3 %collective-permute-start.19 = (f32[128,128]{1,0:T(8,128)S(1)}, f32[128,128]{1,0:T(8,128)S(1)}, u32[]{:S(2)}, u32[]{:S(2)}) collective-permute-start(f32[128,128]{1,0:T(8,128)S(1)} %add.83), channel_id=1, source_target_pairs={{0,2},{1,3},{2,0},{3,1},{4,6},{5,7},{6,4},{7,5},{8,10},{9,11},{10,... | collective-permute-start | bytes 196616 | tf_op jit(solution)/shard_map/ppermute | solution.py:297
  77.0 5.4 %collective-permute-start.22 = (f32[128,128]{1,0:T(8,128)S(1)}, f32[128,128]{1,0:T(8,128)S(1)}, u32[]{:S(2)}, u32[]{:S(2)}) collective-permute-start(f32[128,128]{1,0:T(8,128)S(1)} %add_add_fusion), channel_id=1, source_target_pairs={{0,16},{8,24},{16,0},{24,8},{1,17},{9,25},{17,1},{25,9},{2,18},{10... | collective-permute-start | bytes 196616 | tf_op jit(solution)/shard_map/ppermute | solution.py:298
  82.4 4.3 %collective-permute-start.23 = (f32[128,128]{1,0:T(8,128)S(1)}, f32[128,128]{1,0:T(8,128)S(1)}, u32[]{:S(2)}, u32[]{:S(2)}) collective-permute-start(f32[128,128]{1,0:T(8,128)S(1)} %add.87.gram_ref), channel_id=1, source_target_pairs={{0,8},{8,0},{16,24},{24,16},{1,9},{9,1},{17,25},{25,17},{2,10},{10... | collective-permute-start | bytes 196616 | tf_op jit(solution)/shard_map/ppermute | solution.py:298
  (4 other events, 6.8 us)
